TPU v7x, 32 devices: a whole 2x2x4 slice. The times are simulated.
32 devices in a mesh: state: 4 (over x, core), row: 8 (over z, y).
Axes of the slice: x: 2, y: 2, z: 4, core: 2. Of those that a mesh axis runs over, the one named last changes fastest.
Arguments:
- vectors: bfloat16 [32768, 512], P('row', 'state'), as said below
- active: int32 [8], replicated, may hold values 0 or 1
Outputs:
- orthonormal: bfloat16 [32768, 512], P('row', 'state')
Inputs may be any that keep to these rules, and one draw needn't show every extreme that they name: Each row and each column of vectors has its own scale.
All inputs are finite; a program needn't handle non-finite values.
Results may differ from a plain program's by a relative error of at most 0.00096.
Values may be sent and summed in bfloat16 or wider, within the bound.
No kernel may reach another device: no remote copies, remote signals or barrier semaphores. Data moves between devices by JAX's collectives and lax.ppermute only.
A program may use at most 64 MiB of HBM per device.

v0:
```python
import jax
import jax.numpy as jnp
from jax import lax
from jax.sharding import PartitionSpec as P

VECS = 64
ITERS = 5


def newton_schulz(gram_matrix, total_rows):
    identity = jnp.eye(gram_matrix.shape[0], dtype=jnp.float32)
    frob_norm = jnp.sqrt(jnp.sum(gram_matrix * gram_matrix))
    current = gram_matrix / frob_norm
    inverse = identity
    for repeat in range(ITERS):
        newton_step = 0.5 * (
            3.0 * identity - jnp.dot(inverse, current, precision=lax.Precision.HIGHEST)
        )
        current = jnp.dot(current, newton_step, precision=lax.Precision.HIGHEST)
        inverse = jnp.dot(newton_step, inverse, precision=lax.Precision.HIGHEST)
    return (inverse * jnp.sqrt(total_rows / frob_norm)).astype(jnp.bfloat16)


def cross_product(left_block, right_block):
    return lax.dot_general(
        left_block, right_block, (((0,), (0,)), ((), ())), preferred_element_type=jnp.float32
    )


def shards(vectors, active):
    block_width = vectors.shape[1]
    total_rows = vectors.shape[0] * lax.axis_size("row")
    start_col = lax.axis_index("state") * block_width
    flag_all = jnp.repeat(active.astype(jnp.float32), VECS)
    flag_cols = lax.dynamic_slice_in_dim(flag_all, start_col, block_width, 0)
    masked = vectors * flag_cols.astype(jnp.bfloat16)
    gathered = lax.all_gather(masked, "state", axis=1, tiled=True)
    gram_matrix = cross_product(gathered, gathered)
    gram_matrix = lax.psum(gram_matrix, "row")
    gram_matrix = gram_matrix + jnp.diag((1.0 - flag_all) * total_rows)
    factor = newton_schulz(gram_matrix, total_rows)
    my_factor = lax.dynamic_slice_in_dim(factor, start_col, block_width, 1)
    result = jnp.dot(gathered, my_factor, preferred_element_type=jnp.float32)
    result = result + (1.0 - flag_cols) * vectors.astype(jnp.float32)
    return result.astype(jnp.bfloat16)


def solution(mesh):
    in_specs = (P("row", "state"), P())
    out_specs = P("row", "state")
    return jax.shard_map(shards, mesh=mesh, in_specs=in_specs, out_specs=out_specs, check_vma=False)
```

profile of v0, /device:TPU:0, one launch (start us, length us, event | category | flops | bytes accessed | tf_op | source)
XLA Modules:
  0.0 170.7 jit_solution(12552356755403342421)
XLA Ops:
  6.5 0.0 all-gather.2.cloned.1.call-start
  6.5 0.7 convert_element_type.16
  7.2 0.1 broadcast_in_dim.21
  7.3 0.1 reshape.11
  7.3 0.1 dynamic_slice.15
  7.4 2.3 %broadcast_multiply_fusion = bf16[4096,128]{1,0:T(8,128)(2,1)} fusion(bf16[4096,128]{1,0:T(8,128)(2,1)} %param.2, bf16[128]{0:T(256)(128)(2,1)S(1)} %dynamic_slice.15), kind=kLoop, calls=%fused_computation.17 | loop fusion | flops 524288 | bytes 2097408 | tf_op jit(solution)/shard_map/mul | solution.py:36
  9.7 0.0 all-gather.2.cloned.1.call-update
  9.7 0.0 all-reduce.2.cloned.1.call-start
  9.8 37.8 %all-gather.2.cloned.1.call-done = bf16[4096,512]{1,0:T(8,128)(2,1)} async-done(((bf16[4096,128]{1,0:T(8,128)(2,1)}), bf16[4096,512]{1,0:T(8,128)(2,1)}) %all-gather.2.cloned.1.call-update) | async-done | bytes 4194320 | tf_op jit(solution)/shard_map/all_gather | solution.py:37
  47.6 6.8 %fusion.15 = f32[512,512]{1,0:T(8,128)} fusion(bf16[4096,512]{1,0:T(8,128)(2,1)} %all-gather.2.cloned.1.call-done), kind=kOutput, calls=%fused_computation.26 | convolution fusion | flops 2147483648 | bytes 5242880 | tf_op jit(solution)/shard_map/dot_general | solution.py:25
  54.4 0.0 all-reduce.2.cloned.1.call-update
  54.4 0.1 broadcast_subtract_fusion
  54.5 78.2 %all-reduce.2.cloned.1.call-done = f32[512,512]{1,0:T(8,128)} async-done(((f32[512,512]{1,0:T(8,128)}), f32[512,512]{1,0:T(8,128)}) %all-reduce.2.cloned.1.call-update) | async-done | bytes 1048592 | tf_op jit(solution)/shard_map/psum | solution.py:39
  132.7 2.2 %multiply_reduce_fusion = f32[]{:T(128)} fusion(f32[512,512]{1,0:T(8,128)} %all-reduce.2.cloned.1.call-done, f32[512]{0:T(512)S(1)} %subtract_multiply_fusion), kind=kLoop, calls=%fused_computation.12 | loop fusion | flops 1310719 | bytes 1050628 | tf_op jit(solution)/shard_map/reduce_sum | solution.py:12
  135.6 0.0 copy-start.2
  135.6 2.4 %fusion.5 = f32[512,512]{1,0:T(8,128)S(1)} fusion(f32[512,512]{1,0:T(8,128)} %all-reduce.2.cloned.1.call-done, f32[]{:T(128)S(6)} %sqrt.6, f32[512]{0:T(512)S(1)} %subtract_multiply_fusion), kind=kOutput, calls=%fused_computation.11 | convolution fusion | flops 1612972032 | bytes 2099204 | tf_op jit(solution)/shard_map/dot_general | solution.py:17
  138.0 1.0 fusion.6
  139.0 0.0 copy-done.2
  139.0 1.9 %fusion.12 = f32[512,512]{1,0:T(8,128)S(1)} fusion(f32[512,512]{1,0:T(8,128)S(1)} %fusion.5, f32[512,512]{1,0:T(8,128)S(1)} %copy-done.2, f32[]{:T(128)S(6)} %sqrt.6, f32[512]{0:T(512)S(1)} %subtract_multiply_fusion), kind=kOutput, calls=%fused_computation.25 | convolution fusion | flops 1611661312 | bytes 3147780 | tf_op jit(solution)/shard_map/dot_general | solution.py:19
  140.9 1.9 %fusion.1 = f32[512,512]{1,0:T(8,128)S(1)} fusion(f32[512,512]{1,0:T(8,128)S(1)} %fusion.6, f32[512,512]{1,0:T(8,128)S(1)} %fusion.12), kind=kOutput, calls=%fused_computation.7 | convolution fusion | flops 1611661312 | bytes 3145728 | tf_op jit(solution)/shard_map/dot_general | solution.py:17
  142.8 1.8 %fusion.17 = f32[512,512]{1,0:T(8,128)S(1)} fusion(f32[512,512]{1,0:T(8,128)S(1)} %fusion.12, f32[512,512]{1,0:T(8,128)S(1)} %fusion.1), kind=kOutput, calls=%fused_computation.28 | convolution fusion | flops 1610612736 | bytes 3145728 | tf_op jit(solution)/shard_map/dot_general | solution.py:19
  144.6 1.8 %fusion.16 = f32[512,512]{1,0:T(8,128)S(1)} fusion(f32[512,512]{1,0:T(8,128)S(1)} %fusion.1, f32[512,512]{1,0:T(8,128)S(1)} %fusion.6), kind=kOutput, calls=%fused_computation.27 | convolution fusion | flops 1610612736 | bytes 3145728 | tf_op jit(solution)/shard_map/dot_general | solution.py:20
  146.5 2.0 %fusion.2 = f32[512,512]{1,0:T(8,128)S(1)} fusion(f32[512,512]{1,0:T(8,128)S(1)} %fusion.16, f32[512,512]{1,0:T(8,128)S(1)} %fusion.17), kind=kOutput, calls=%fused_computation.8 | convolution fusion | flops 1611661312 | bytes 3145728 | tf_op jit(solution)/shard_map/dot_general | solution.py:17
  148.5 1.8 %fusion.19 = f32[512,512]{1,0:T(8,128)S(1)} fusion(f32[512,512]{1,0:T(8,128)S(1)} %fusion.17, f32[512,512]{1,0:T(8,128)S(1)} %fusion.2), kind=kOutput, calls=%fused_computation.30 | convolution fusion | flops 1610612736 | bytes 3145728 | tf_op jit(solution)/shard_map/dot_general | solution.py:19
  150.4 1.8 %fusion.18 = f32[512,512]{1,0:T(8,128)S(1)} fusion(f32[512,512]{1,0:T(8,128)S(1)} %fusion.2, f32[512,512]{1,0:T(8,128)S(1)} %fusion.16), kind=kOutput, calls=%fused_computation.29 | convolution fusion | flops 1610612736 | bytes 3145728 | tf_op jit(solution)/shard_map/dot_general | solution.py:20
  152.2 1.9 %fusion.3 = f32[512,512]{1,0:T(8,128)S(1)} fusion(f32[512,512]{1,0:T(8,128)S(1)} %fusion.18, f32[512,512]{1,0:T(8,128)S(1)} %fusion.19), kind=kOutput, calls=%fused_computation.9 | convolution fusion | flops 1611661312 | bytes 3145728 | tf_op jit(solution)/shard_map/dot_general | solution.py:17
  154.1 1.8 %fusion.20 = f32[512,512]{1,0:T(8,128)S(1)} fusion(f32[512,512]{1,0:T(8,128)S(1)} %fusion.3, f32[512,512]{1,0:T(8,128)S(1)} %fusion.18), kind=kOutput, calls=%fused_computation.31 | convolution fusion | flops 1610612736 | bytes 3145728 | tf_op jit(solution)/shard_map/dot_general | solution.py:20
  156.0 0.0 copy-start.1
  156.0 1.8 %fusion.21 = f32[512,512]{1,0:T(8,128)S(1)} fusion(f32[512,512]{1,0:T(8,128)S(1)} %fusion.19, f32[512,512]{1,0:T(8,128)S(1)} %fusion.3), kind=kOutput, calls=%fused_computation.32 | convolution fusion | flops 1610612736 | bytes 3145728 | tf_op jit(solution)/shard_map/dot_general | solution.py:19
  157.9 0.0 copy-start
  157.9 1.9 %fusion.4 = f32[512,512]{1,0:T(8,128)S(1)} fusion(f32[512,512]{1,0:T(8,128)S(1)} %fusion.20, f32[512,512]{1,0:T(8,128)S(1)} %fusion.21), kind=kOutput, calls=%fused_computation.10 | convolution fusion | flops 1611661312 | bytes 3145728 | tf_op jit(solution)/shard_map/dot_general | solution.py:17
  159.8 1.9 %fusion.22 = f32[512,512]{1,0:T(8,128)S(1)} fusion(f32[512,512]{1,0:T(8,128)S(1)} %fusion.4, f32[512,512]{1,0:T(8,128)S(1)} %fusion.20), kind=kOutput, calls=%fused_computation.33 | convolution fusion | flops 1610612736 | bytes 3145728 | tf_op jit(solution)/shard_map/dot_general | solution.py:20
  161.6 0.0 copy-done.1
  161.6 0.0 copy-done
  161.7 2.2 %fusion = bf16[4096,128]{1,0:T(8,128)(2,1)} fusion(bf16[4096,512]{1,0:T(8,128)(2,1)S(1)} %copy-done, bf16[4096,128]{1,0:T(8,128)(2,1)S(1)} %copy-done.1, f32[128]{0:T(128)S(1)} %broadcast_subtract_fusion, f32[512,512]{1,0:T(8,128)S(1)} %fusion.22, s32[]{:T(128)S(6)} %select_n.9, f32[]{:T(128)S(6)} %sqrt.7), kind=kOutput, calls=%fused_computation.1 | convolution fusion | flops 539099136 | bytes 6554120 | tf_op jit(solution)/shard_map/dot_general | solution.py:43
  (1 shorter events, 0.0 us)
Async XLA Ops:
  6.5 41.1 %all-gather.2.cloned.1.call-start = ((), (), s32[]{:S(2)}) async-start(), calls=%async_computation | async-start | bytes 5242880 | tf_op jit(solution)/shard_map/all_gather | solution.py:37
  9.7 123.0 %all-reduce.2.cloned.1.call-start = ((), (), s32[]{:S(2)}) async-start(), calls=%async_computation.1 | async-start | bytes 2097152 | tf_op jit(solution)/shard_map/psum | solution.py:39
  135.6 3.4 %copy-start.2 = (f32[512,512]{1,0:T(8,128)S(1)}, f32[512,512]{1,0:T(8,128)}, u32[]{:S(2)}) copy-start(f32[512,512]{1,0:T(8,128)} %all-reduce.2.cloned.1.call-done) | copy-start | bytes 3145732
  156.0 5.7 %copy-start.1 = (bf16[4096,128]{1,0:T(8,128)(2,1)S(1)}, bf16[4096,128]{1,0:T(8,128)(2,1)}, u32[]{:S(2)}) copy-start(bf16[4096,128]{1,0:T(8,128)(2,1)} %param.2) | copy-start | bytes 3145732
  157.9 3.7 %copy-start = (bf16[4096,512]{1,0:T(8,128)(2,1)S(1)}, bf16[4096,512]{1,0:T(8,128)(2,1)}, u32[]{:S(2)}) copy-start(bf16[4096,512]{1,0:T(8,128)(2,1)} %all-gather.2.cloned.1.call-done) | copy-start | bytes 12582916
Sparse Core Ops, SparseCore 0:
  9.8 37.7 all-gather.1
  54.5 78.1 all-reduce.1
where the time goes:
time: 171 us
  waiting for transfers between devices  116 us (68%)
  matrix products  34.9 us (20%)
  between operations  14.3 us (8%)
  other arithmetic  5.17 us (3%)
    psum x1, waiting for transfers between devices, shards(): gram_matrix = lax.psum(gram_matrix, 'row')  78.2 us
    all_gather x1, waiting for transfers between devices, shards(): gathered = lax.all_gather(masked, 'state', axis=1, tiled=True)  37.8 us
    dot_general x5, matrix products, newton_schulz(): jnp.dot(inverse, current, precision=lax.Precision.HIGHEST)  10 us
    dot_general x5, matrix products, newton_schulz(): inverse = jnp.dot(newton_step, inverse, precision=lax.Precision.HIGHEST)  8.37 us
    dot_general x4, matrix products, newton_schulz(): current = jnp.dot(current, newton_step, precision=lax.Precision.HIGHEST)  7.45 us
    dot_general x1, matrix products, cross_product(): lax.dot_general(left_block, right_block, (((0,), (0,)), ((), ())), prefer...  6.79 us
  transfers between devices with their start and end apart: 2, of which 2 were waited for; matrix products, arithmetic and copies ran while one was open for 0% of the time, Pallas kernels for 0%

commit v1 on v0

v1 whole, which is shorter than its diff:
```python
import functools

import jax
import jax.numpy as jnp
from jax import lax
from jax.experimental import pallas as pl
from jax.experimental.pallas import tpu as pltpu
from jax.sharding import PartitionSpec as P

ITERS = 5
VMEM_BYTES = 40 * 1024 * 1024
F32 = jnp.float32
BF16 = jnp.bfloat16


def dot(left, right):
    return jnp.dot(left, right, preferred_element_type=F32)


def cross(left, right):
    return lax.dot_general(left, right, (((0,), (0,)), ((), ())), preferred_element_type=F32)


def call(kernel, out_shape, n_smem, n_args, flops, name, scratch=(), in_specs=None, out_specs=None):
    smem = pl.BlockSpec(memory_space=pltpu.SMEM)
    vmem = pl.BlockSpec(memory_space=pltpu.VMEM)
    return pl.pallas_call(
        kernel,
        out_shape=out_shape,
        in_specs=in_specs or [smem] * n_smem + [vmem] * n_args,
        out_specs=out_specs or jax.tree.map(lambda _: vmem, out_shape),
        scratch_shapes=list(scratch),
        compiler_params=pltpu.CompilerParams(vmem_limit_bytes=VMEM_BYTES),
        cost_estimate=pl.CostEstimate(flops=flops, bytes_accessed=4 * 2**20, transcendentals=0),
        name=name,
    )


def chip_gram_kernel(place, own, mate, slab):
    core = place[1]
    width = own.shape[1]
    slab[pl.ds(pl.multiple_of(core * width, width), width), :] = cross(own[...], own[...])
    slab[pl.ds(pl.multiple_of((1 - core) * width, width), width), :] = cross(own[...], mate[...])


def pair_gram_kernel(place, own, mate, across, slab, later):
    chip = place[0]
    half, width = across.shape
    rows = pl.ds(pl.multiple_of(chip * half, half), half)
    left = own[rows, :]
    later[...] = left
    same = cross(across[...], left)
    other = cross(across[...], mate[rows, :])
    slab[0:width, :] = jnp.where(chip == 0, same.T, same)
    slab[width : 2 * width, :] = jnp.where(chip == 0, other.T, other)


def sum_kernel(chip_parts, pair_parts, total):
    count = total.shape[0] // 2
    total[0:count, :] = jnp.sum(chip_parts[...], axis=0)
    total[count : 2 * count, :] = jnp.sum(pair_parts[...], axis=0)


def spread_kernel(place, mine, theirs, spread):
    chip = place[0]
    count = mine.shape[0] // 2
    chip_mine, chip_theirs = mine[0:count, :], theirs[0:count, :]
    first = jnp.where(chip == 0, chip_mine, chip_theirs)
    second = jnp.where(chip == 0, chip_theirs, chip_mine)
    pair = mine[count : 2 * count, :] + theirs[count : 2 * count, :]
    for row in range(spread.shape[0]):
        spread[row, 0] = first
        spread[row, 1] = second
        spread[row, 2] = pair


def split(value):
    high = value.astype(BF16)
    return high, (value - high.astype(F32)).astype(BF16)


def product(left, right):
    return dot(left[0], right[0]) + (dot(left[0], right[1]) + dot(left[1], right[0]))


def finish_kernel(
    total_rows, place, active, gram_mine, gram_mate, own, mate, across1, mate1, across2, mate2,
    out, gram, highs, lows, factor, left, sems,
):
    chip, core = place[0], place[1]
    half, width = across1.shape
    cols = gram.shape[0]
    near, far = pl.multiple_of(chip * half, half), pl.multiple_of((1 - chip) * half, half)
    copies = [
        pltpu.make_async_copy(own, left.at[:, 0:width], sems.at[0]),
        pltpu.make_async_copy(mate, left.at[:, width : 2 * width], sems.at[1]),
        pltpu.make_async_copy(across1, left.at[pl.ds(near, half), 2 * width : 3 * width], sems.at[2]),
        pltpu.make_async_copy(mate1, left.at[pl.ds(near, half), 3 * width : 4 * width], sems.at[3]),
        pltpu.make_async_copy(across2, left.at[pl.ds(far, half), 2 * width : 3 * width], sems.at[4]),
        pltpu.make_async_copy(mate2, left.at[pl.ds(far, half), 3 * width : 4 * width], sems.at[5]),
    ]
    for copy in copies:
        copy.start()

    def parts(index):
        mine = gram_mine[:, index].reshape(2 * width, width)
        theirs = gram_mate[:, index].reshape(2 * width, width)
        core0 = jnp.where(core == 0, mine, theirs)
        core1 = jnp.where(core == 0, theirs, mine)
        return core0[:width], core0[width:], core1[:width], core1[width:]

    def put(row, col, value):
        gram[row * width : (row + 1) * width, col * width : (col + 1) * width] = value

    for side in range(2):
        top0, low0, top1, low1 = parts(side)
        put(2 * side, 2 * side, top0)
        put(2 * side + 1, 2 * side, top1)
        put(2 * side, 2 * side + 1, jnp.where(chip == side, low0, low1))
        put(2 * side + 1, 2 * side + 1, jnp.where(chip == side, low1, low0))
    top0, low0, top1, low1 = parts(2)
    off10 = jnp.where(chip == 0, low0, low1)
    off01 = jnp.where(chip == 0, low1, low0)
    put(0, 2, top0)
    put(1, 3, top1)
    put(0, 3, off01)
    put(1, 2, off10)
    put(2, 0, top0.T)
    put(3, 1, top1.T)
    put(3, 0, off01.T)
    put(2, 1, off10.T)

    states = active.shape[0]
    vecs = cols // states
    col_state = lax.broadcasted_iota(jnp.int32, (1, cols), 1) // vecs
    flags = jnp.zeros((1, cols), F32)
    for state in range(states):
        flags = jnp.where(col_state == state, active[state].astype(F32), flags)
    square = jnp.zeros((vecs, cols), F32)
    for state in range(states):
        rows = slice(state * vecs, (state + 1) * vecs)
        kept = jnp.where(jnp.logical_and(flags != 0, active[state] != 0), gram[rows, :], 0.0)
        diagonal = lax.broadcasted_iota(jnp.int32, (vecs, cols), 0) + state * vecs == lax.broadcasted_iota(
            jnp.int32, (vecs, cols), 1
        )
        kept = kept + jnp.where(diagonal, (1.0 - flags) * total_rows, 0.0)
        gram[rows, :] = kept
        square = square + kept * kept
    frob_square = jnp.sum(jnp.sum(square, axis=0, keepdims=True), axis=1, keepdims=True)
    frob_norm = jnp.sqrt(frob_square)
    inverse_norm = 1.0 / frob_norm

    current = gram[...] * inverse_norm
    mine = pl.ds(pl.multiple_of((2 * chip + core) * width, width), width)
    for step in range(ITERS - 1):
        high, low = split(current)
        highs[step], lows[step] = high, low
        if step == ITERS - 2:
            gram[...] = current
            break
        square = product((high, low), (high, low))
        cube = product((high, low), split(square))
        current = 2.25 * current - 1.5 * square + 0.25 * cube

    def times(step, slab):
        return product((highs[step], lows[step]), split(slab))

    def newton(step, slab):
        return 1.5 * slab - 0.5 * times(step, slab)

    row_id = lax.broadcasted_iota(jnp.int32, (cols, width), 0)
    col_id = lax.broadcasted_iota(jnp.int32, (cols, width), 1) + (2 * chip + core) * width
    unit = jnp.where(row_id == col_id, 1.0, 0.0)
    last = ITERS - 2
    slab = 1.5 * unit - 0.5 * gram[:, mine]
    slab = 1.5 * unit - 0.5 * times(last, newton(last, slab))
    for step in range(last, -1, -1):
        slab = newton(step, slab)
    slab = slab * jnp.sqrt(total_rows / frob_norm)

    for state in range(states):
        rows = slice(state * vecs, (state + 1) * vecs)
        factor[rows, :] = jnp.where(active[state] != 0, slab[rows, :], unit[rows, :]).astype(BF16)

    def block(index):
        return factor[pl.ds(pl.multiple_of(index * width, width), width), :]

    weights = jnp.concatenate(
        [
            block(2 * chip + core),
            block(2 * chip + 1 - core),
            block(2 * (1 - chip) + core),
            block(2 * (1 - chip) + 1 - core),
        ],
        axis=0,
    )
    for copy in copies:
        copy.wait()
    out[...] = dot(left[...], weights).astype(BF16)


def shards(vectors, active):
    rows, width = vectors.shape
    half = rows // 2
    row_devices = lax.axis_size("row")
    total_rows = rows * row_devices
    cols = width * lax.axis_size("state")
    state = lax.axis_index("state")
    chip, core = state // 2, state % 2
    place = jnp.stack([chip, core]).astype(jnp.int32)
    count = 2 * width // row_devices
    shape = jax.ShapeDtypeStruct

    def swap(value, bit):
        return lax.ppermute(value, "state", [(index, index ^ bit) for index in range(4)])

    def exchange(value):
        return lax.all_to_all(value, "row", 0, 0, tiled=True)

    across1 = swap(lax.dynamic_slice_in_dim(vectors, (1 - chip) * half, half, 0), 2)
    mate = swap(vectors, 1)

    slab = shape((2 * width, width), F32)
    chip_slab = call(chip_gram_kernel, slab, 1, 2, 4 * rows * width * width, "chip_gram")(place, vectors, mate)
    chip_parts = exchange(chip_slab)

    pair_slab, later = call(
        pair_gram_kernel, (slab, shape((half, width), BF16)), 1, 3, 4 * half * width * width, "pair_gram"
    )(place, vectors, mate, across1)
    across2 = swap(later, 2)
    pair_parts = exchange(pair_slab)

    summed = call(sum_kernel, shape((2 * count, width), F32), 0, 2, 0, "sum_parts")(
        chip_parts.reshape(row_devices, count, width), pair_parts.reshape(row_devices, count, width)
    )
    route = [
        (place_from * row_devices + row, (place_from ^ (2 if row < row_devices // 2 else 3)) * row_devices + row)
        for place_from in range(4)
        for row in range(row_devices)
    ]
    theirs = lax.ppermute(summed, ("state", "row"), route)
    spread = call(spread_kernel, shape((row_devices, 3, count, width), F32), 1, 2, 0, "spread_parts")(
        place, summed, theirs
    )
    gram_mine = exchange(spread.reshape(row_devices * 3 * count, width))
    gram_mate = swap(gram_mine, 1)
    mate1 = swap(across1, 1)
    mate2 = swap(across2, 1)

    smem = pl.BlockSpec(memory_space=pltpu.SMEM)
    vmem = pl.BlockSpec(memory_space=pltpu.VMEM)
    hbm = pl.BlockSpec(memory_space=pl.ANY)
    packed = (row_devices, 3, count, width)
    return call(
        functools.partial(finish_kernel, float(total_rows)),
        shape((rows, width), BF16),
        0,
        0,
        12 * cols**3 * 3 + 2 * rows * cols * width,
        "finish",
        scratch=[
            pltpu.VMEM((cols, cols), F32),
            pltpu.VMEM((ITERS - 1, cols, cols), BF16),
            pltpu.VMEM((ITERS - 1, cols, cols), BF16),
            pltpu.VMEM((cols, width), BF16),
            pltpu.VMEM((rows, cols), BF16),
            pltpu.SemaphoreType.DMA((6,)),
        ],
        in_specs=[smem, smem, vmem, vmem] + [hbm] * 6,
    )(
        place, active, gram_mine.reshape(packed), gram_mate.reshape(packed),
        vectors, mate, across1, mate1, across2, mate2,
    )


def solution(mesh):
    in_specs = (P("row", "state"), P())
    out_specs = P("row", "state")
    return jax.shard_map(shards, mesh=mesh, in_specs=in_specs, out_specs=out_specs, check_vma=False)
```

time: 171 us -> 70.5 us (0.41)
  waiting for transfers between devices: 116 us -> 21.7 us
  matrix products: 34.9 us -> 0 us
  Pallas kernels: 0 us -> 19 us
  starting transfers between devices: 0.04 us -> 16.1 us
  between operations: 14.3 us -> 0.04 us
  blocking collectives: 0 us -> 11.6 us
  other arithmetic: 5.17 us -> 0.07 us
    psum x1 -> x0, waiting for transfers between devices: 78.2 us -> none  [shards(): gram_matrix = lax.psum(gram_matrix, 'row')]
    all_gather x1 -> x0, waiting for transfers between devices: 37.8 us -> none  [shards(): gathered = lax.all_gather(masked, 'state', axis=1, tiled=True)]
    dot_general x16 -> x0, matrix products: 34.9 us -> none  [the longest x5 10 us: newton_schulz(): jnp.dot(inverse, current, precision=lax.Precision.HIGHEST)]
    ppermute x0 -> x7, waiting for transfers between devices: none -> 20 us  [the longest x6 17.6 us: swap(): lax.ppermute(value, 'state', [(index, index ^ bit) for index in range(4)])]
    pallas_call x0 -> x5, Pallas kernels: none -> 19 us  [the longest x1 14.6 us: shards(): call(functools.partial(finish_kernel, float(total_rows)), shape((rows, wi...]
    all_to_all x0 -> x1, blocking collectives: none -> 11.6 us  [exchange(): return lax.all_to_all(value, 'row', 0, 0, tiled=True)]
    all_to_all x0 -> x2, starting transfers between devices: none -> 9.35 us  [exchange(): return lax.all_to_all(value, 'row', 0, 0, tiled=True)]
    ppermute x0 -> x7, starting transfers between devices: none -> 6.72 us  [the longest x6 5.17 us: swap(): lax.ppermute(value, 'state', [(index, index ^ bit) for index in range(4)])]
  transfers between devices with their start and end apart: 2 -> 9, of which waited for: 2 -> 5; matrix products, arithmetic and copies ran while one was open for 0% -> 2% of each run, Pallas kernels for 0% -> 4%
where the time goes in v1:
time: 70.5 us; the launch traced here: 70.2 us
  waiting for transfers between devices  21.7 us (31%)
  Pallas kernels  19 us (27%)
  starting transfers between devices  16.1 us (23%)
  blocking collectives  11.6 us (16%)
  local copies, waits for them, and re-layouts  1.74 us (2%)
    ppermute x6, waiting for transfers between devices, swap(): lax.ppermute(value, 'state', [(index, index ^ bit) for index in range(4)])  17.6 us
    pallas_call x1, Pallas kernels, shards(): call(functools.partial(finish_kernel, float(total_rows)), shape((rows, wi...  14.6 us
    all_to_all x1, blocking collectives, exchange(): return lax.all_to_all(value, 'row', 0, 0, tiled=True)  11.6 us
    all_to_all x2, starting transfers between devices, exchange(): return lax.all_to_all(value, 'row', 0, 0, tiled=True)  9.35 us
    ppermute x6, starting transfers between devices, swap(): lax.ppermute(value, 'state', [(index, index ^ bit) for index in range(4)])  5.17 us
    ppermute x1, waiting for transfers between devices, shards(): theirs = lax.ppermute(summed, ('state', 'row'), route)  2.42 us
    pallas_call x1, Pallas kernels, shards(): call(chip_gram_kernel, slab, 1, 2, 4 * rows * width * width, 'chip_gram')  1.95 us
    all_to_all x2, waiting for transfers between devices, exchange(): return lax.all_to_all(value, 'row', 0, 0, tiled=True)  1.67 us
  transfers between devices with their start and end apart: 9, of which 5 were waited for; matrix products, arithmetic and copies ran while one was open for 2% of the time, Pallas kernels for 4%

profile of v1, /device:TPU:0, one launch (start us, length us, event | category | flops | bytes accessed | tf_op | source)
XLA Modules:
  0.0 70.2 jit_solution(2914689119997715972)
XLA Ops:
  0.0 0.0 copy-start
  0.0 0.5 collective-permute-start
  0.5 1.1 %constant_dynamic-slice_fusion = bf16[2048,128]{1,0:T(8,128)(2,1)S(1)} fusion(bf16[4096,128]{1,0:T(8,128)(2,1)} %own.5, s32[]{:T(128)S(6)} %select_n.16), kind=kLoop, calls=%fused_computation.1 | loop fusion | bytes 1048580 | tf_op jit(solution)/shard_map/dynamic_slice | solution.py:220
  1.5 2.6 %collective-permute-start.1 = (bf16[2048,128]{1,0:T(8,128)(2,1)S(1)}, bf16[2048,128]{1,0:T(8,128)(2,1)S(1)}, u32[]{:S(2)}, u32[]{:S(2)}) collective-permute-start(bf16[2048,128]{1,0:T(8,128)(2,1)S(1)} %constant_dynamic-slice_fusion), channel_id=1, source_target_pairs={{0,16},{8,24},{16,0},{24,8},{1,17},{9,25},{17,1},{25,9},{2,18},{10... | collective-permute-start | bytes 1572872 | tf_op jit(solution)/shard_map/ppermute | solution.py:215
  4.2 0.1 pad_add_fusion.place
  4.3 0.0 collective-permute-done.mate
  4.3 0.0 copy-done
  4.3 1.9 %chip_gram.1 = f32[256,128]{1,0:T(8,128)} custom-call(s32[2]{0:T(128)S(1)} %pad_add_fusion.place, bf16[4096,128]{1,0:T(8,128)(2,1)S(1)} %copy-done, bf16[4096,128]{1,0:T(8,128)(2,1)S(1)} %collective-permute-done.mate), custom_call_target="tpu_custom_call" | custom-call | flops 268435456 | bytes 4194304 | tf_op jit(solution)/shard_map/chip_gram/pallas_call | solution.py:224
  6.2 5.9 %all-to-all-start = ((f32[8,32,128]{2,1,0:T(8,128)}), f32[8,32,128]{2,1,0:T(8,128)S(1)}, u32[]{:S(2)}, u32[]{:S(2)}) async-start(f32[8,32,128]{2,1,0:T(8,128)} %bitcast.2), calls=%async_computation | async-start | bytes 262144 | tf_op jit(solution)/shard_map/all_to_all | solution.py:218
  12.1 4.6 %collective-permute-done.1.across.across1 = bf16[2048,128]{1,0:T(8,128)(2,1)S(1)} collective-permute-done((bf16[2048,128]{1,0:T(8,128)(2,1)S(1)}, bf16[2048,128]{1,0:T(8,128)(2,1)S(1)}, u32[]{:S(2)}, u32[]{:S(2)}) %collective-permute-start.1) | collective-permute-done | bytes 524320 | tf_op jit(solution)/shard_map/ppermute | solution.py:215
  16.7 1.1 %pair_gram.1 = (f32[256,128]{1,0:T(8,128)S(1)}, bf16[2048,128]{1,0:T(8,128)(2,1)S(1)}) custom-call(s32[2]{0:T(128)S(1)} %pad_add_fusion.place, bf16[4096,128]{1,0:T(8,128)(2,1)S(1)} %copy-done, bf16[4096,128]{1,0:T(8,128)(2,1)S(1)} %collective-permute-done.mate, bf16[2048,128]{1,0:T(8,128)(2,1)S(1)} %collective-permute-done.1.across.across1), custom_call_target="tpu_custom_call" | custom-call | flops 134217728 | bytes 4194304 | tf_op jit(solution)/shard_map/pair_gram/pallas_call | solution.py:227
  17.8 1.7 %all-to-all-done.chip_parts = f32[8,32,128]{2,1,0:T(8,128)S(1)} async-done(((f32[8,32,128]{2,1,0:T(8,128)}), f32[8,32,128]{2,1,0:T(8,128)S(1)}, u32[]{:S(2)}, u32[]{:S(2)}) %all-to-all-start) | async-done | bytes 131104 | tf_op jit(solution)/shard_map/all_to_all | solution.py:218
  19.5 11.6 %all_to_all.30.pair_parts = f32[8,32,128]{2,1,0:T(8,128)S(1)} all-to-all(f32[8,32,128]{2,1,0:T(8,128)S(1)} %bitcast.10), channel_id=1, replica_groups=mesh['state'=4,'row'=8] {'row'}, dimensions={0} | all-to-all | bytes 262144 | tf_op jit(solution)/shard_map/all_to_all | solution.py:218
  31.1 1.6 %collective-permute-start.2 = (f32[64,128]{1,0:T(8,128)S(1)}, f32[64,128]{1,0:T(8,128)S(1)}, u32[]{:S(2)}, u32[]{:S(2)}) collective-permute-start(f32[64,128]{1,0:T(8,128)S(1)} %sum_parts.1.mine), channel_id=1, source_target_pairs={{0,16},{1,17},{2,18},{3,19},{4,28},{5,29},{6,30},{7,31},{8,24},{9,... | collective-permute-start | bytes 98312 | tf_op jit(solution)/shard_map/ppermute | solution.py:241
  32.6 2.4 %collective-permute-done.2.theirs = f32[64,128]{1,0:T(8,128)S(1)} collective-permute-done((f32[64,128]{1,0:T(8,128)S(1)}, f32[64,128]{1,0:T(8,128)S(1)}, u32[]{:S(2)}, u32[]{:S(2)}) %collective-permute-start.2) | collective-permute-done | bytes 32800 | tf_op jit(solution)/shard_map/ppermute | solution.py:241
  35.0 1.3 %spread_parts.1 = f32[8,3,32,128]{3,2,1,0:T(8,128)} custom-call(s32[2]{0:T(128)S(1)} %pad_add_fusion.place, f32[64,128]{1,0:T(8,128)S(1)} %sum_parts.1.mine, f32[64,128]{1,0:T(8,128)S(1)} %collective-permute-done.2.theirs), custom_call_target="tpu_custom_call" | custom-call | bytes 4194304 | tf_op jit(solution)/shard_map/spread_parts/pallas_call | solution.py:242
  36.3 3.5 %all-to-all-start.2 = ((f32[8,96,128]{2,1,0:T(8,128)}), f32[8,96,128]{2,1,0:T(8,128)S(1)}, u32[]{:S(2)}, u32[]{:S(2)}) async-start(f32[8,96,128]{2,1,0:T(8,128)} %bitcast.4), calls=%async_computation.2 | async-start | bytes 786432 | tf_op jit(solution)/shard_map/all_to_all | solution.py:218
  39.8 1.6 %collective-permute-start.5 = (bf16[2048,128]{1,0:T(8,128)(2,1)S(1)}, bf16[2048,128]{1,0:T(8,128)(2,1)}, u32[]{:S(2)}, u32[]{:S(2)}) collective-permute-start(bf16[2048,128]{1,0:T(8,128)(2,1)S(1)} %get-tuple-element.8), channel_id=1, source_target_pairs={{0,16},{8,24},{16,0},{24,8},{1,17},{9,25},{17,1},{25,9},{2,18},{10... | collective-permute-start | bytes 1572872 | tf_op jit(solution)/shard_map/ppermute | solution.py:215
  41.4 0.0 collective-permute-start.4
  41.4 10.8 %collective-permute-done.5.across2 = bf16[2048,128]{1,0:T(8,128)(2,1)} collective-permute-done((bf16[2048,128]{1,0:T(8,128)(2,1)S(1)}, bf16[2048,128]{1,0:T(8,128)(2,1)}, u32[]{:S(2)}, u32[]{:S(2)}) %collective-permute-start.5) | collective-permute-done | bytes 524320 | tf_op jit(solution)/shard_map/ppermute | solution.py:215
  52.2 0.0 collective-permute-start.6
  52.2 0.0 all-to-all-done.2
  52.2 0.5 collective-permute-start.3
  52.7 0.0 collective-permute-done.4.mate1
  52.7 2.2 %collective-permute-done.6.mate2 = bf16[2048,128]{1,0:T(8,128)(2,1)S(1)} collective-permute-done((bf16[2048,128]{1,0:T(8,128)(2,1)}, bf16[2048,128]{1,0:T(8,128)(2,1)S(1)}, u32[]{:S(2)}, u32[]{:S(2)}) %collective-permute-start.6) | collective-permute-done | bytes 524320 | tf_op jit(solution)/shard_map/ppermute | solution.py:215
  54.9 0.0 collective-permute-done.3
  54.9 0.0 copy-start.1
  54.9 0.7 copy-done.1
  55.6 14.6 %finish.1 = bf16[4096,128]{1,0:T(8,128)(2,1)} custom-call(s32[2]{0:T(128)S(1)} %pad_add_fusion.place, s32[8]{0:T(128)S(1)} %copy-done.1, f32[8,3,32,128]{3,2,1,0:T(8,128)S(1)} %bitcast.9, f32[8,3,32,128]{3,2,1,0:T(8,128)S(1)} %bitcast.11, bf16[4096,128]{1,0:T(8,128)(2,1)S(1)} %copy-done, bf16[4096,128]{1,0:T(8,128)(2,1)S(1)} %collective-permute-done.mate, ...), custom_call_target="tpu_custom_call" | custom-call | flops 5368709120 | bytes 4194304 | tf_op jit(solution)/shard_map/finish/pallas_call | solution.py:254
  (1 shorter events, 0.0 us)
Async XLA Ops:
  0.0 4.3 %copy-start = (bf16[4096,128]{1,0:T(8,128)(2,1)S(1)}, bf16[4096,128]{1,0:T(8,128)(2,1)}, u32[]{:S(2)}) copy-start(bf16[4096,128]{1,0:T(8,128)(2,1)} %own.5) | copy-start | bytes 3145732
  0.0 4.3 %collective-permute-start = (bf16[4096,128]{1,0:T(8,128)(2,1)}, bf16[4096,128]{1,0:T(8,128)(2,1)S(1)}, u32[]{:S(2)}, u32[]{:S(2)}) collective-permute-start(bf16[4096,128]{1,0:T(8,128)(2,1)} %own.5), channel_id=1, source_target_pairs={{0,8},{8,0},{16,24},{24,16},{1,9},{9,1},{17,25},{25,17},{2,10},{10... | collective-permute-start | bytes 3145736 | tf_op jit(solution)/shard_map/ppermute | solution.py:215
  1.5 15.2 %collective-permute-start.1 = (bf16[2048,128]{1,0:T(8,128)(2,1)S(1)}, bf16[2048,128]{1,0:T(8,128)(2,1)S(1)}, u32[]{:S(2)}, u32[]{:S(2)}) collective-permute-start(bf16[2048,128]{1,0:T(8,128)(2,1)S(1)} %constant_dynamic-slice_fusion), channel_id=1, source_target_pairs={{0,16},{8,24},{16,0},{24,8},{1,17},{9,25},{17,1},{25,9},{2,18},{10... | collective-permute-start | bytes 1572872 | tf_op jit(solution)/shard_map/ppermute | solution.py:215
  6.2 13.2 %all-to-all-start = ((f32[8,32,128]{2,1,0:T(8,128)}), f32[8,32,128]{2,1,0:T(8,128)S(1)}, u32[]{:S(2)}, u32[]{:S(2)}) async-start(f32[8,32,128]{2,1,0:T(8,128)} %bitcast.2), calls=%async_computation | async-start | bytes 262144 | tf_op jit(solution)/shard_map/all_to_all | solution.py:218
  31.1 4.0 %collective-permute-start.2 = (f32[64,128]{1,0:T(8,128)S(1)}, f32[64,128]{1,0:T(8,128)S(1)}, u32[]{:S(2)}, u32[]{:S(2)}) collective-permute-start(f32[64,128]{1,0:T(8,128)S(1)} %sum_parts.1.mine), channel_id=1, source_target_pairs={{0,16},{1,17},{2,18},{3,19},{4,28},{5,29},{6,30},{7,31},{8,24},{9,... | collective-permute-start | bytes 98312 | tf_op jit(solution)/shard_map/ppermute | solution.py:241
  36.3 15.9 %all-to-all-start.2 = ((f32[8,96,128]{2,1,0:T(8,128)}), f32[8,96,128]{2,1,0:T(8,128)S(1)}, u32[]{:S(2)}, u32[]{:S(2)}) async-start(f32[8,96,128]{2,1,0:T(8,128)} %bitcast.4), calls=%async_computation.2 | async-start | bytes 786432 | tf_op jit(solution)/shard_map/all_to_all | solution.py:218
  39.8 12.4 %collective-permute-start.5 = (bf16[2048,128]{1,0:T(8,128)(2,1)S(1)}, bf16[2048,128]{1,0:T(8,128)(2,1)}, u32[]{:S(2)}, u32[]{:S(2)}) collective-permute-start(bf16[2048,128]{1,0:T(8,128)(2,1)S(1)} %get-tuple-element.8), channel_id=1, source_target_pairs={{0,16},{8,24},{16,0},{24,8},{1,17},{9,25},{17,1},{25,9},{2,18},{10... | collective-permute-start | bytes 1572872 | tf_op jit(solution)/shard_map/ppermute | solution.py:215
  41.4 11.4 %collective-permute-start.4 = (bf16[2048,128]{1,0:T(8,128)(2,1)S(1)}, bf16[2048,128]{1,0:T(8,128)(2,1)}, u32[]{:S(2)}, u32[]{:S(2)}) collective-permute-start(bf16[2048,128]{1,0:T(8,128)(2,1)S(1)} %collective-permute-done.1.across.across1), channel_id=1, source_target_pairs={{0,8},{8,0},{16,24},{24,16},{1,9},{9,1},{17,25},{25,17},{2,10},{10... | collective-permute-start | bytes 1572872 | tf_op jit(solution)/shard_map/ppermute | solution.py:215
  52.2 2.7 %collective-permute-start.6 = (bf16[2048,128]{1,0:T(8,128)(2,1)}, bf16[2048,128]{1,0:T(8,128)(2,1)S(1)}, u32[]{:S(2)}, u32[]{:S(2)}) collective-permute-start(bf16[2048,128]{1,0:T(8,128)(2,1)} %collective-permute-done.5.across2), channel_id=1, source_target_pairs={{0,8},{8,0},{16,24},{24,16},{1,9},{9,1},{17,25},{25,17},{2,10},{10... | collective-permute-start | bytes 1572872 | tf_op jit(solution)/shard_map/ppermute | solution.py:215
  52.2 2.7 %collective-permute-start.3 = (f32[768,128]{1,0:T(8,128)S(1)}, f32[768,128]{1,0:T(8,128)S(1)}, u32[]{:S(2)}, u32[]{:S(2)}) collective-permute-start(f32[768,128]{1,0:T(8,128)S(1)} %bitcast.8), channel_id=1, source_target_pairs={{0,8},{8,0},{16,24},{24,16},{1,9},{9,1},{17,25},{25,17},{2,10},{10... | collective-permute-start | bytes 1179656 | tf_op jit(solution)/shard_map/ppermute | solution.py:215
  54.9 0.7 copy-start.1

commit v2 on v1

v2 whole, which is shorter than its diff:
```python
import functools

import jax
import jax.numpy as jnp
from jax import lax
from jax.experimental import pallas as pl
from jax.experimental.pallas import tpu as pltpu
from jax.sharding import PartitionSpec as P

ITERS = 5
VMEM_BYTES = 40 * 1024 * 1024
F32 = jnp.float32
BF16 = jnp.bfloat16


def dot(left, right):
    return jnp.dot(left, right, preferred_element_type=F32)


def cross(left, right):
    return lax.dot_general(left, right, (((0,), (0,)), ((), ())), preferred_element_type=F32)


def call(kernel, out_shape, n_smem, n_args, flops, name, scratch=(), in_specs=None, out_specs=None):
    smem = pl.BlockSpec(memory_space=pltpu.SMEM)
    vmem = pl.BlockSpec(memory_space=pltpu.VMEM)
    return pl.pallas_call(
        kernel,
        out_shape=out_shape,
        in_specs=in_specs or [smem] * n_smem + [vmem] * n_args,
        out_specs=out_specs or jax.tree.map(lambda _: vmem, out_shape),
        scratch_shapes=list(scratch),
        compiler_params=pltpu.CompilerParams(vmem_limit_bytes=VMEM_BYTES),
        cost_estimate=pl.CostEstimate(flops=flops, bytes_accessed=4 * 2**20, transcendentals=0),
        name=name,
    )


def chip_gram_kernel(place, own, mate, slab, later):
    chip, core = place[0], place[1]
    width = own.shape[1]
    half = later.shape[0]
    later[...] = own[pl.ds(pl.multiple_of(chip * half, half), half), :]
    slab[pl.ds(pl.multiple_of(core * width, width), width), :] = cross(own[...], own[...])
    slab[pl.ds(pl.multiple_of((1 - core) * width, width), width), :] = cross(own[...], mate[...])


def pair_gram_kernel(place, own, mate, across, chip_parts, packed):
    chip = place[0]
    half, width = across.shape
    devices, _, count, _ = packed.shape
    rows = pl.ds(pl.multiple_of(chip * half, half), half)
    same = cross(across[...], own[rows, :])
    other = cross(across[...], mate[rows, :])
    slab = jnp.concatenate([jnp.where(chip == 0, same.T, same), jnp.where(chip == 0, other.T, other)], axis=0)
    chip_sum = jnp.sum(chip_parts[...], axis=0)
    for row in range(devices):
        packed[row, 0] = chip_sum
        packed[row, 1] = slab[row * count : (row + 1) * count]


def sum_kernel(parts, total):
    total[...] = jnp.sum(parts[:, 1], axis=0)


def spread_kernel(parts, mine, theirs, across2, mate1, spread, chip_slab):
    del across2, mate1
    total = mine[...] + theirs[...]
    count = total.shape[0]
    for row in range(parts.shape[0]):
        spread[row] = total
        chip_slab[row * count : (row + 1) * count, :] = parts[row, 0]


def split(value):
    high = value.astype(BF16)
    return high, (value - high.astype(F32)).astype(BF16)


def product(left, right):
    return dot(left[0], right[0]) + (dot(left[0], right[1]) + dot(left[1], right[0]))


def row_product(left, right):
    count = left[0].shape[0]
    both = dot(jnp.concatenate(left, axis=0), right[0])
    return both[:count] + (both[count:] + dot(left[0], right[1]))


def symmetric(first, mixed, last):
    return jnp.concatenate(
        [jnp.concatenate([first, mixed], axis=1), jnp.concatenate([mixed.T, last], axis=1)], axis=0
    )


def symmetric_square(high, low):
    half = high.shape[0] // 2
    cross_part = dot(high, low)
    upper = dot(high[:half], high)
    last = dot(high[half:], high[:, half:])
    return symmetric(
        upper[:, :half] + (cross_part[:half, :half] + cross_part[:half, :half].T),
        upper[:, half:] + (cross_part[:half, half:] + cross_part[half:, :half].T),
        last + (cross_part[half:, half:] + cross_part[half:, half:].T),
    )


def symmetric_product(left, right):
    half = left[0].shape[0] // 2
    upper = product((left[0][:half], left[1][:half]), right)
    last = product((left[0][half:], left[1][half:]), (right[0][:, half:], right[1][:, half:]))
    return symmetric(upper[:, :half], upper[:, half:], last)


def finish_kernel(
    total_rows, place, chip_mine, chip_mate, other_mine, other_mate, pair_mine, pair_mate,
    own, mate, across1, mate1, across2, mate2,
    out, gram, highs, lows, factor, left, result, sems, out_sems,
):
    chip, core = place[0], place[1]
    half, width = across1.shape
    cols = gram.shape[0]
    near, far = pl.multiple_of(chip * half, half), pl.multiple_of((1 - chip) * half, half)
    copies = [
        pltpu.make_async_copy(own, left.at[:, 0:width], sems.at[0]),
        pltpu.make_async_copy(mate, left.at[:, width : 2 * width], sems.at[1]),
        pltpu.make_async_copy(across1, left.at[pl.ds(near, half), 2 * width : 3 * width], sems.at[2]),
        pltpu.make_async_copy(mate1, left.at[pl.ds(near, half), 3 * width : 4 * width], sems.at[3]),
        pltpu.make_async_copy(across2, left.at[pl.ds(far, half), 2 * width : 3 * width], sems.at[4]),
        pltpu.make_async_copy(mate2, left.at[pl.ds(far, half), 3 * width : 4 * width], sems.at[5]),
    ]
    for copy in copies:
        copy.start()

    def parts(mine, theirs):
        core0 = jnp.where(core == 0, mine, theirs)
        core1 = jnp.where(core == 0, theirs, mine)
        return core0[:width], core0[width:], core1[:width], core1[width:]

    def put(row, col, value):
        gram[row * width : (row + 1) * width, col * width : (col + 1) * width] = value

    for side in range(2):
        top0, low0, top1, low1 = parts(
            jnp.where(chip == side, chip_mine[...], other_mine[...]),
            jnp.where(chip == side, chip_mate[...], other_mate[...]),
        )
        put(2 * side, 2 * side, top0)
        put(2 * side, 2 * side + 1, low0)
        put(2 * side + 1, 2 * side, top1)
        put(2 * side + 1, 2 * side + 1, low1)
    top0, low0, top1, low1 = parts(pair_mine[...], pair_mate[...])
    off10 = jnp.where(chip == 0, low0, low1)
    off01 = jnp.where(chip == 0, low1, low0)
    put(0, 2, top0)
    put(1, 3, top1)
    put(0, 3, off01)
    put(1, 2, off10)
    put(2, 0, top0.T)
    put(3, 1, top1.T)
    put(3, 0, off01.T)
    put(2, 1, off10.T)

    states = place.shape[0] - 2
    vecs = cols // states
    col_state = lax.broadcasted_iota(jnp.int32, (1, cols), 1) // vecs
    flags = jnp.zeros((1, cols), F32)
    for state in range(states):
        flags = jnp.where(col_state == state, place[2 + state].astype(F32), flags)
    square = jnp.zeros((vecs, cols), F32)
    for state in range(states):
        rows = slice(state * vecs, (state + 1) * vecs)
        kept = jnp.where(jnp.logical_and(flags != 0, place[2 + state] != 0), gram[rows, :], 0.0)
        diagonal = lax.broadcasted_iota(jnp.int32, (vecs, cols), 0) + state * vecs == lax.broadcasted_iota(
            jnp.int32, (vecs, cols), 1
        )
        kept = kept + jnp.where(diagonal, (1.0 - flags) * total_rows, 0.0)
        gram[rows, :] = kept
        square = square + kept * kept
    frob_square = jnp.sum(jnp.sum(square, axis=0, keepdims=True), axis=1, keepdims=True)
    frob_norm = jnp.sqrt(frob_square)
    inverse_norm = 1.0 / frob_norm

    current = gram[...] * inverse_norm
    start = (2 * chip + core) * width
    last = ITERS - 2
    for step in range(last):
        high, low = split(current)
        highs[step], lows[step] = high, low
        square = symmetric_square(high, low)
        cube = symmetric_product((high, low), split(square))
        current = 2.25 * current - 1.5 * square + 0.25 * cube
    highs[last], lows[last] = split(current)
    gram[...] = current

    def times(step, slab):
        return row_product(split(slab), (highs[step], lows[step]))

    def newton(step, slab):
        return 1.5 * slab - 0.5 * times(step, slab)

    row_id = lax.broadcasted_iota(jnp.int32, (width, cols), 0) + start
    col_id = lax.broadcasted_iota(jnp.int32, (width, cols), 1)
    unit = jnp.where(row_id == col_id, 1.0, 0.0)
    slab = 1.5 * unit - 0.5 * gram[pl.ds(pl.multiple_of(start, width), width), :]
    slab = 1.5 * unit - 0.5 * times(last, newton(last, slab))
    for step in range(last, -1, -1):
        slab = newton(step, slab)
    slab = slab * jnp.sqrt(total_rows / frob_norm)

    factor[...] = jnp.where(flags != 0, slab, unit).T.astype(BF16)

    def block(index):
        return factor[pl.ds(pl.multiple_of(index * width, width), width), :]

    weights = jnp.concatenate(
        [
            block(2 * chip + core),
            block(2 * chip + 1 - core),
            block(2 * (1 - chip) + core),
            block(2 * (1 - chip) + 1 - core),
        ],
        axis=0,
    )
    for copy in copies:
        copy.wait()
    pieces = out_sems.shape[0]
    size = out.shape[0] // pieces
    stores = []
    for piece in range(pieces):
        rows = slice(piece * size, (piece + 1) * size)
        result[rows, :] = dot(left[rows, :], weights).astype(BF16)
        stores.append(pltpu.make_async_copy(result.at[rows, :], out.at[rows, :], out_sems.at[piece]))
        stores[-1].start()
    for store in stores:
        store.wait()


def shards(vectors, active):
    rows, width = vectors.shape
    half = rows // 2
    row_devices = lax.axis_size("row")
    total_rows = rows * row_devices
    cols = width * lax.axis_size("state")
    state = lax.axis_index("state")
    chip, core = state // 2, state % 2
    place = jnp.concatenate([jnp.stack([chip, core]).astype(jnp.int32), active])
    count = 2 * width // row_devices
    shape = jax.ShapeDtypeStruct
    smem = pl.BlockSpec(memory_space=pltpu.SMEM)
    vmem = pl.BlockSpec(memory_space=pltpu.VMEM)
    hbm = pl.BlockSpec(memory_space=pl.ANY)

    def swap(value, bit):
        return lax.ppermute(value, "state", [(index, index ^ bit) for index in range(4)])

    def exchange(value):
        return lax.all_to_all(value, "row", 0, 0, tiled=True)

    across1 = swap(lax.dynamic_slice_in_dim(vectors, (1 - chip) * half, half, 0), 2)
    mate = swap(vectors, 1)

    slab = shape((2 * width, width), F32)
    chip_slab, later = call(
        chip_gram_kernel, (slab, shape((half, width), BF16)), 1, 2, 4 * rows * width * width, "chip_gram"
    )(place, vectors, mate)
    chip_parts = exchange(chip_slab)
    across2 = swap(later, 2)

    packed = call(
        pair_gram_kernel, shape((row_devices, 2, count, width), F32), 1, 4, 4 * half * width * width, "pair_gram"
    )(place, vectors, mate, across1, chip_parts.reshape(row_devices, count, width))
    parts = exchange(packed.reshape(row_devices * 2 * count, width)).reshape(packed.shape)

    summed = call(sum_kernel, shape((count, width), F32), 0, 1, 0, "sum_parts")(parts)
    route = [
        (place_from * row_devices + row, (place_from ^ (2 if row < row_devices // 2 else 3)) * row_devices + row)
        for place_from in range(4)
        for row in range(row_devices)
    ]
    theirs = lax.ppermute(summed, ("state", "row"), route)
    mate1 = swap(across1, 1)
    spread, chip_mine = call(
        spread_kernel, (shape((row_devices, count, width), F32), slab), 0, 3, 0, "spread_parts",
        in_specs=[vmem, vmem, vmem, hbm, hbm],
    )(parts, summed, theirs, across2, mate1)
    pair_mine = exchange(spread.reshape(2 * width, width))
    chip_mate = swap(chip_mine, 1)
    other_mine = swap(chip_mine, 2)
    other_mate = swap(other_mine, 1)
    pair_mate = swap(pair_mine, 1)
    mate2 = swap(across2, 1)

    return call(
        functools.partial(finish_kernel, float(total_rows)),
        shape((rows, width), BF16),
        0,
        0,
        12 * cols**3 * 3 + 2 * rows * cols * width,
        "finish",
        scratch=[
            pltpu.VMEM((cols, cols), F32),
            pltpu.VMEM((ITERS - 1, cols, cols), BF16),
            pltpu.VMEM((ITERS - 1, cols, cols), BF16),
            pltpu.VMEM((cols, width), BF16),
            pltpu.VMEM((rows, cols), BF16),
            pltpu.VMEM((rows, width), BF16),
            pltpu.SemaphoreType.DMA((6,)),
            pltpu.SemaphoreType.DMA((4,)),
        ],
        in_specs=[smem] + [vmem] * 6 + [hbm] * 6,
        out_specs=hbm,
    )(
        place, chip_mine, chip_mate, other_mine, other_mate, pair_mine, pair_mate,
        vectors, mate, across1, mate1, across2, mate2,
    )


def solution(mesh):
    in_specs = (P("row", "state"), P())
    out_specs = P("row", "state")
    return jax.shard_map(shards, mesh=mesh, in_specs=in_specs, out_specs=out_specs, check_vma=False)
```

time: 70.5 us -> 63.4 us (0.90)
  blocking collectives: 11.6 us -> 0 us
  Pallas kernels: 19 us -> 15.3 us
  starting transfers between devices: 16.1 us -> 19.3 us
  waiting for transfers between devices: 21.7 us -> 24.9 us
  local copies, waits for them, and re-layouts: 1.74 us -> 3.32 us
    all_to_all x1 -> x0, blocking collectives: 11.6 us -> none  [exchange(): return lax.all_to_all(value, 'row', 0, 0, tiled=True)]
    all_to_all x2 -> x3, waiting for transfers between devices: 1.67 us -> 12.6 us  [exchange(): return lax.all_to_all(value, 'row', 0, 0, tiled=True)]
    ppermute x6 -> x9, waiting for transfers between devices: 17.6 us -> 10 us  [swap(): lax.ppermute(value, 'state', [(index, index ^ bit) for index in range(4)])]
    pallas_call x1, Pallas kernels: 14.6 us -> 10.9 us  [shards(): call(functools.partial(finish_kernel, float(total_rows)), shape((rows, wi...]
    all_to_all x2 -> x3, starting transfers between devices: 9.35 us -> 12.6 us  [exchange(): return lax.all_to_all(value, 'row', 0, 0, tiled=True)]
    unnamed x4 -> x6, local copies, waits for them, and re-layouts: 0.66 us -> 1.45 us
    dynamic_slice x1, local copies, waits for them, and re-layouts: 1.08 us -> 1.87 us  [shards(): lax.dynamic_slice_in_dim(vectors, (1 - chip) * half, half, 0)]
    ppermute x6 -> x9, starting transfers between devices: 5.17 us -> 5.14 us  [swap(): lax.ppermute(value, 'state', [(index, index ^ bit) for index in range(4)])]
  transfers between devices with their start and end apart: 9 -> 13, of which waited for: 5 -> 8; matrix products, arithmetic and copies ran while one was open for 2% -> 3% of each run, Pallas kernels for 4% -> 7%
where the time goes in v2:
time: 63.4 us; the launch traced here: 63 us
  waiting for transfers between devices  24.9 us (39%)
  starting transfers between devices  19.3 us (30%)
  Pallas kernels  15.3 us (24%)
  local copies, waits for them, and re-layouts  3.32 us (5%)
    all_to_all x3, waiting for transfers between devices, exchange(): return lax.all_to_all(value, 'row', 0, 0, tiled=True)  12.6 us
    all_to_all x3, starting transfers between devices, exchange(): return lax.all_to_all(value, 'row', 0, 0, tiled=True)  12.6 us
    pallas_call x1, Pallas kernels, shards(): call(functools.partial(finish_kernel, float(total_rows)), shape((rows, wi...  10.9 us
    ppermute x9, waiting for transfers between devices, swap(): lax.ppermute(value, 'state', [(index, index ^ bit) for index in range(4)])  10 us
    ppermute x9, starting transfers between devices, swap(): lax.ppermute(value, 'state', [(index, index ^ bit) for index in range(4)])  5.14 us
    ppermute x1, waiting for transfers between devices, shards(): theirs = lax.ppermute(summed, ('state', 'row'), route)  2.24 us
    pallas_call x1, Pallas kernels, shards(): call(chip_gram_kernel, (slab, shape((half, width), BF16)), 1, 2, 4 * rows...  1.95 us
    dynamic_slice x1, local copies, waits for them, and re-layouts, shards(): lax.dynamic_slice_in_dim(vectors, (1 - chip) * half, half, 0)  1.87 us
  transfers between devices with their start and end apart: 13, of which 8 were waited for; matrix products, arithmetic and copies ran while one was open for 3% of the time, Pallas kernels for 7%

profile of v2, /device:TPU:0, one launch (start us, length us, event | category | flops | bytes accessed | tf_op | source)
XLA Modules:
  0.0 63.0 jit_solution(13299522162020854636)
XLA Ops:
  0.0 0.0 copy-start
  0.0 0.5 collective-permute-start
  0.5 1.9 %constant_dynamic-slice_fusion = bf16[2048,128]{1,0:T(8,128)(2,1)} fusion(bf16[4096,128]{1,0:T(8,128)(2,1)} %own.5, s32[]{:T(128)S(6)} %select_n.16), kind=kLoop, calls=%fused_computation.1 | loop fusion | bytes 1048580 | tf_op jit(solution)/shard_map/dynamic_slice | solution.py:260
  2.3 2.6 %collective-permute-start.1 = (bf16[2048,128]{1,0:T(8,128)(2,1)}, bf16[2048,128]{1,0:T(8,128)(2,1)S(1)}, u32[]{:S(2)}, u32[]{:S(2)}) collective-permute-start(bf16[2048,128]{1,0:T(8,128)(2,1)} %constant_dynamic-slice_fusion), channel_id=1, source_target_pairs={{0,16},{8,24},{16,0},{24,8},{1,17},{9,25},{17,1},{25,9},{2,18},{10... | collective-permute-start | bytes 1572872 | tf_op jit(solution)/shard_map/ppermute | solution.py:255
  4.9 0.0 copy-start.2
  4.9 0.7 %copy-done.2 = s32[8]{0:T(128)S(1)} copy-done((s32[8]{0:T(128)S(1)}, s32[8]{0:T(128)}, u32[]{:S(2)}) %copy-start.2) | copy-done | bytes 56
  5.6 0.1 pad_add_fusion.place
  5.6 0.0 collective-permute-done.mate
  5.6 0.0 copy-done
  5.6 1.9 %chip_gram.1 = (f32[256,128]{1,0:T(8,128)}, bf16[2048,128]{1,0:T(8,128)(2,1)S(1)}) custom-call(s32[10]{0:T(128)S(1)} %pad_add_fusion.place, bf16[4096,128]{1,0:T(8,128)(2,1)S(1)} %copy-done, bf16[4096,128]{1,0:T(8,128)(2,1)S(1)} %collective-permute-done.mate), custom_call_target="tpu_custom_call" | custom-call | flops 268435456 | bytes 4194304 | tf_op jit(solution)/shard_map/chip_gram/pallas_call | solution.py:264
  7.6 0.0 copy-start.1
  7.6 0.8 %copy-done.1 = bf16[2048,128]{1,0:T(8,128)(2,1)} copy-done((bf16[2048,128]{1,0:T(8,128)(2,1)}, bf16[2048,128]{1,0:T(8,128)(2,1)S(1)}, u32[]{:S(2)}) %copy-start.1) | copy-done | bytes 524312
  8.4 5.8 %all-to-all-start = ((f32[8,32,128]{2,1,0:T(8,128)}), f32[8,32,128]{2,1,0:T(8,128)S(1)}, u32[]{:S(2)}, u32[]{:S(2)}) async-start(f32[8,32,128]{2,1,0:T(8,128)} %bitcast.2), calls=%async_computation | async-start | bytes 262144 | tf_op jit(solution)/shard_map/all_to_all | solution.py:258
  14.2 0.5 collective-permute-start.3
  14.8 3.1 %collective-permute-done.1.across.across1 = bf16[2048,128]{1,0:T(8,128)(2,1)S(1)} collective-permute-done((bf16[2048,128]{1,0:T(8,128)(2,1)}, bf16[2048,128]{1,0:T(8,128)(2,1)S(1)}, u32[]{:S(2)}, u32[]{:S(2)}) %collective-permute-start.1) | collective-permute-done | bytes 524320 | tf_op jit(solution)/shard_map/ppermute | solution.py:255
  17.9 0.0 collective-permute-start.4
  17.9 3.7 %all-to-all-done.chip_parts = f32[8,32,128]{2,1,0:T(8,128)S(1)} async-done(((f32[8,32,128]{2,1,0:T(8,128)}), f32[8,32,128]{2,1,0:T(8,128)S(1)}, u32[]{:S(2)}, u32[]{:S(2)}) %all-to-all-start) | async-done | bytes 131104 | tf_op jit(solution)/shard_map/all_to_all | solution.py:258
  21.6 1.8 %pair_gram.1 = f32[8,2,32,128]{3,2,1,0:T(8,128)} custom-call(s32[10]{0:T(128)S(1)} %pad_add_fusion.place, bf16[4096,128]{1,0:T(8,128)(2,1)S(1)} %copy-done, bf16[4096,128]{1,0:T(8,128)(2,1)S(1)} %collective-permute-done.mate, bf16[2048,128]{1,0:T(8,128)(2,1)S(1)} %collective-permute-done.1.across.across1, f32[8,32,128]{2,1,0:T(8,128)S(1)} %all-to-all-done.chip_parts), custom_call_target="tpu_custom_call" | custom-call | flops 134217728 | bytes 4194304 | tf_op jit(solution)/shard_map/pair_gram/pallas_call | solution.py:270
  23.3 3.4 %all-to-all-start.1 = ((f32[8,64,128]{2,1,0:T(8,128)}), f32[8,64,128]{2,1,0:T(8,128)S(1)}, u32[]{:S(2)}, u32[]{:S(2)}) async-start(f32[8,64,128]{2,1,0:T(8,128)} %bitcast.3), calls=%async_computation.1 | async-start | bytes 524288 | tf_op jit(solution)/shard_map/all_to_all | solution.py:258
  26.8 2.1 %collective-permute-done.3.across2 = bf16[2048,128]{1,0:T(8,128)(2,1)S(1)} collective-permute-done((bf16[2048,128]{1,0:T(8,128)(2,1)}, bf16[2048,128]{1,0:T(8,128)(2,1)S(1)}, u32[]{:S(2)}, u32[]{:S(2)}) %collective-permute-start.3) | collective-permute-done | bytes 524320 | tf_op jit(solution)/shard_map/ppermute | solution.py:255
  28.9 0.0 collective-permute-start.9
  28.9 6.7 %all-to-all-done.1 = f32[8,64,128]{2,1,0:T(8,128)S(1)} async-done(((f32[8,64,128]{2,1,0:T(8,128)}), f32[8,64,128]{2,1,0:T(8,128)S(1)}, u32[]{:S(2)}, u32[]{:S(2)}) %all-to-all-start.1) | async-done | bytes 262176 | tf_op jit(solution)/shard_map/all_to_all | solution.py:258
  35.6 1.6 %collective-permute-start.2 = (f32[32,128]{1,0:T(8,128)S(1)}, f32[32,128]{1,0:T(8,128)S(1)}, u32[]{:S(2)}, u32[]{:S(2)}) collective-permute-start(f32[32,128]{1,0:T(8,128)S(1)} %sum_parts.1.mine), channel_id=1, source_target_pairs={{0,16},{1,17},{2,18},{3,19},{4,28},{5,29},{6,30},{7,31},{8,24},{9,... | collective-permute-start | bytes 49160 | tf_op jit(solution)/shard_map/ppermute | solution.py:281
  37.1 0.0 collective-permute-done.4.mate1
  37.1 2.2 %collective-permute-done.2.theirs = f32[32,128]{1,0:T(8,128)S(1)} collective-permute-done((f32[32,128]{1,0:T(8,128)S(1)}, f32[32,128]{1,0:T(8,128)S(1)}, u32[]{:S(2)}, u32[]{:S(2)}) %collective-permute-start.2) | collective-permute-done | bytes 16416 | tf_op jit(solution)/shard_map/ppermute | solution.py:281
  39.4 0.7 %spread_parts.1 = (f32[8,32,128]{2,1,0:T(8,128)}, f32[256,128]{1,0:T(8,128)S(1)}) custom-call(f32[8,2,32,128]{3,2,1,0:T(8,128)S(1)} %bitcast.7, f32[32,128]{1,0:T(8,128)S(1)} %sum_parts.1.mine, f32[32,128]{1,0:T(8,128)S(1)} %collective-permute-done.2.theirs, bf16[2048,128]{1,0:T(8,128)(2,1)S(1)} %collective-permute-done.3.across2, ...), custom_call_target="tpu_custom_call" | custom-call | bytes 4194304 | tf_op jit(solution)/shard_map/spread_parts/pallas_call | solution.py:283
  40.1 3.4 %all-to-all-start.2 = ((f32[8,32,128]{2,1,0:T(8,128)}), f32[8,32,128]{2,1,0:T(8,128)S(1)}, u32[]{:S(2)}, u32[]{:S(2)}) async-start(f32[8,32,128]{2,1,0:T(8,128)} %get-tuple-element.12), calls=%async_computation.2 | async-start | bytes 262144 | tf_op jit(solution)/shard_map/all_to_all | solution.py:258
  43.4 1.6 %collective-permute-start.6 = (f32[256,128]{1,0:T(8,128)S(1)}, f32[256,128]{1,0:T(8,128)S(1)}, u32[]{:S(2)}, u32[]{:S(2)}) collective-permute-start(f32[256,128]{1,0:T(8,128)S(1)} %get-tuple-element.11.chip_mine), channel_id=1, source_target_pairs={{0,16},{8,24},{16,0},{24,8},{1,17},{9,25},{17,1},{25,9},{2,18},{10... | collective-permute-start | bytes 393224 | tf_op jit(solution)/shard_map/ppermute | solution.py:255
  45.0 0.0 collective-permute-start.5
  45.0 3.5 %collective-permute-done.6.other_mine = f32[256,128]{1,0:T(8,128)S(1)} collective-permute-done((f32[256,128]{1,0:T(8,128)S(1)}, f32[256,128]{1,0:T(8,128)S(1)}, u32[]{:S(2)}, u32[]{:S(2)}) %collective-permute-start.6) | collective-permute-done | bytes 131104 | tf_op jit(solution)/shard_map/ppermute | solution.py:255
  48.5 0.0 collective-permute-start.7
  48.5 2.2 %all-to-all-done.2 = f32[8,32,128]{2,1,0:T(8,128)S(1)} async-done(((f32[8,32,128]{2,1,0:T(8,128)}), f32[8,32,128]{2,1,0:T(8,128)S(1)}, u32[]{:S(2)}, u32[]{:S(2)}) %all-to-all-start.2) | async-done | bytes 131104 | tf_op jit(solution)/shard_map/all_to_all | solution.py:258
  50.7 0.0 collective-permute-start.8
  50.7 0.0 collective-permute-done.5.chip_mate
  50.7 0.0 collective-permute-done.7.other_mate
  50.7 0.0 collective-permute-done.9.mate2
  50.7 1.3 %collective-permute-done.8.pair_mate = f32[256,128]{1,0:T(8,128)S(1)} collective-permute-done((f32[256,128]{1,0:T(8,128)S(1)}, f32[256,128]{1,0:T(8,128)S(1)}, u32[]{:S(2)}, u32[]{:S(2)}) %collective-permute-start.8) | collective-permute-done | bytes 131104 | tf_op jit(solution)/shard_map/ppermute | solution.py:255
  52.1 10.9 %finish.1 = bf16[4096,128]{1,0:T(8,128)(2,1)} custom-call(s32[10]{0:T(128)S(1)} %pad_add_fusion.place, f32[256,128]{1,0:T(8,128)S(1)} %get-tuple-element.11.chip_mine, f32[256,128]{1,0:T(8,128)} %collective-permute-done.5.chip_mate, f32[256,128]{1,0:T(8,128)S(1)} %collective-permute-done.6.other_mine, f32[256,128]{1,0:T(8,128)} %collective-permute-done.7.other_mate, ...), custom_call_target="tpu_custom_call" | custom-call | flops 5368709120 | bytes 4194304 | tf_op jit(solution)/shard_map/finish/pallas_call | solution.py:294
  (1 shorter events, 0.0 us)
Async XLA Ops:
  0.0 5.6 %copy-start = (bf16[4096,128]{1,0:T(8,128)(2,1)S(1)}, bf16[4096,128]{1,0:T(8,128)(2,1)}, u32[]{:S(2)}) copy-start(bf16[4096,128]{1,0:T(8,128)(2,1)} %own.5) | copy-start | bytes 3145732
  0.0 5.6 %collective-permute-start = (bf16[4096,128]{1,0:T(8,128)(2,1)}, bf16[4096,128]{1,0:T(8,128)(2,1)S(1)}, u32[]{:S(2)}, u32[]{:S(2)}) collective-permute-start(bf16[4096,128]{1,0:T(8,128)(2,1)} %own.5), channel_id=1, source_target_pairs={{0,8},{8,0},{16,24},{24,16},{1,9},{9,1},{17,25},{25,17},{2,10},{10... | collective-permute-start | bytes 3145736 | tf_op jit(solution)/shard_map/ppermute | solution.py:255
  2.3 15.6 %collective-permute-start.1 = (bf16[2048,128]{1,0:T(8,128)(2,1)}, bf16[2048,128]{1,0:T(8,128)(2,1)S(1)}, u32[]{:S(2)}, u32[]{:S(2)}) collective-permute-start(bf16[2048,128]{1,0:T(8,128)(2,1)} %constant_dynamic-slice_fusion), channel_id=1, source_target_pairs={{0,16},{8,24},{16,0},{24,8},{1,17},{9,25},{17,1},{25,9},{2,18},{10... | collective-permute-start | bytes 1572872 | tf_op jit(solution)/shard_map/ppermute | solution.py:255
  4.9 0.7 %copy-start.2 = (s32[8]{0:T(128)S(1)}, s32[8]{0:T(128)}, u32[]{:S(2)}) copy-start(s32[8]{0:T(128)} %param.3) | copy-start | bytes 100
  7.6 0.8 %copy-start.1 = (bf16[2048,128]{1,0:T(8,128)(2,1)}, bf16[2048,128]{1,0:T(8,128)(2,1)S(1)}, u32[]{:S(2)}) copy-start(bf16[2048,128]{1,0:T(8,128)(2,1)S(1)} %get-tuple-element.10) | copy-start | bytes 1572868
  8.4 13.2 %all-to-all-start = ((f32[8,32,128]{2,1,0:T(8,128)}), f32[8,32,128]{2,1,0:T(8,128)S(1)}, u32[]{:S(2)}, u32[]{:S(2)}) async-start(f32[8,32,128]{2,1,0:T(8,128)} %bitcast.2), calls=%async_computation | async-start | bytes 262144 | tf_op jit(solution)/shard_map/all_to_all | solution.py:258
  14.2 14.6 %collective-permute-start.3 = (bf16[2048,128]{1,0:T(8,128)(2,1)}, bf16[2048,128]{1,0:T(8,128)(2,1)S(1)}, u32[]{:S(2)}, u32[]{:S(2)}) collective-permute-start(bf16[2048,128]{1,0:T(8,128)(2,1)} %copy-done.1), channel_id=1, source_target_pairs={{0,16},{8,24},{16,0},{24,8},{1,17},{9,25},{17,1},{25,9},{2,18},{10... | collective-permute-start | bytes 1572872 | tf_op jit(solution)/shard_map/ppermute | solution.py:255
  17.9 19.3 %collective-permute-start.4 = (bf16[2048,128]{1,0:T(8,128)(2,1)S(1)}, bf16[2048,128]{1,0:T(8,128)(2,1)}, u32[]{:S(2)}, u32[]{:S(2)}) collective-permute-start(bf16[2048,128]{1,0:T(8,128)(2,1)S(1)} %collective-permute-done.1.across.across1), channel_id=1, source_target_pairs={{0,8},{8,0},{16,24},{24,16},{1,9},{9,1},{17,25},{25,17},{2,10},{10... | collective-permute-start | bytes 1572872 | tf_op jit(solution)/shard_map/ppermute | solution.py:255
  23.3 12.2 %all-to-all-start.1 = ((f32[8,64,128]{2,1,0:T(8,128)}), f32[8,64,128]{2,1,0:T(8,128)S(1)}, u32[]{:S(2)}, u32[]{:S(2)}) async-start(f32[8,64,128]{2,1,0:T(8,128)} %bitcast.3), calls=%async_computation.1 | async-start | bytes 524288 | tf_op jit(solution)/shard_map/all_to_all | solution.py:258
  28.9 21.9 %collective-permute-start.9 = (bf16[2048,128]{1,0:T(8,128)(2,1)S(1)}, bf16[2048,128]{1,0:T(8,128)(2,1)}, u32[]{:S(2)}, u32[]{:S(2)}) collective-permute-start(bf16[2048,128]{1,0:T(8,128)(2,1)S(1)} %collective-permute-done.3.across2), channel_id=1, source_target_pairs={{0,8},{8,0},{16,24},{24,16},{1,9},{9,1},{17,25},{25,17},{2,10},{10... | collective-permute-start | bytes 1572872 | tf_op jit(solution)/shard_map/ppermute | solution.py:255
  35.6 3.8 %collective-permute-start.2 = (f32[32,128]{1,0:T(8,128)S(1)}, f32[32,128]{1,0:T(8,128)S(1)}, u32[]{:S(2)}, u32[]{:S(2)}) collective-permute-start(f32[32,128]{1,0:T(8,128)S(1)} %sum_parts.1.mine), channel_id=1, source_target_pairs={{0,16},{1,17},{2,18},{3,19},{4,28},{5,29},{6,30},{7,31},{8,24},{9,... | collective-permute-start | bytes 49160 | tf_op jit(solution)/shard_map/ppermute | solution.py:281
  40.1 10.7 %all-to-all-start.2 = ((f32[8,32,128]{2,1,0:T(8,128)}), f32[8,32,128]{2,1,0:T(8,128)S(1)}, u32[]{:S(2)}, u32[]{:S(2)}) async-start(f32[8,32,128]{2,1,0:T(8,128)} %get-tuple-element.12), calls=%async_computation.2 | async-start | bytes 262144 | tf_op jit(solution)/shard_map/all_to_all | solution.py:258
  43.4 5.0 %collective-permute-start.6 = (f32[256,128]{1,0:T(8,128)S(1)}, f32[256,128]{1,0:T(8,128)S(1)}, u32[]{:S(2)}, u32[]{:S(2)}) collective-permute-start(f32[256,128]{1,0:T(8,128)S(1)} %get-tuple-element.11.chip_mine), channel_id=1, source_target_pairs={{0,16},{8,24},{16,0},{24,8},{1,17},{9,25},{17,1},{25,9},{2,18},{10... | collective-permute-start | bytes 393224 | tf_op jit(solution)/shard_map/ppermute | solution.py:255
  45.0 5.7 %collective-permute-start.5 = (f32[256,128]{1,0:T(8,128)S(1)}, f32[256,128]{1,0:T(8,128)}, u32[]{:S(2)}, u32[]{:S(2)}) collective-permute-start(f32[256,128]{1,0:T(8,128)S(1)} %get-tuple-element.11.chip_mine), channel_id=1, source_target_pairs={{0,8},{8,0},{16,24},{24,16},{1,9},{9,1},{17,25},{25,17},{2,10},{10... | collective-permute-start | bytes 393224 | tf_op jit(solution)/shard_map/ppermute | solution.py:255
  48.5 2.3 %collective-permute-start.7 = (f32[256,128]{1,0:T(8,128)S(1)}, f32[256,128]{1,0:T(8,128)}, u32[]{:S(2)}, u32[]{:S(2)}) collective-permute-start(f32[256,128]{1,0:T(8,128)S(1)} %collective-permute-done.6.other_mine), channel_id=1, source_target_pairs={{0,8},{8,0},{16,24},{24,16},{1,9},{9,1},{17,25},{25,17},{2,10},{10... | collective-permute-start | bytes 393224 | tf_op jit(solution)/shard_map/ppermute | solution.py:255
  50.7 1.3 %collective-permute-start.8 = (f32[256,128]{1,0:T(8,128)S(1)}, f32[256,128]{1,0:T(8,128)S(1)}, u32[]{:S(2)}, u32[]{:S(2)}) collective-permute-start(f32[256,128]{1,0:T(8,128)S(1)} %bitcast.8), channel_id=1, source_target_pairs={{0,8},{8,0},{16,24},{24,16},{1,9},{9,1},{17,25},{25,17},{2,10},{10... | collective-permute-start | bytes 393224 | tf_op jit(solution)/shard_map/ppermute | solution.py:255

commit v3 on v2

v3 whole, which is shorter than its diff:
```python
import functools

import jax
import jax.numpy as jnp
from jax import lax
from jax.experimental import pallas as pl
from jax.experimental.pallas import tpu as pltpu
from jax.sharding import PartitionSpec as P

ITERS = 5
F32 = jnp.float32
BF16 = jnp.bfloat16
SMEM = pl.BlockSpec(memory_space=pltpu.SMEM)
VMEM = pl.BlockSpec(memory_space=pltpu.VMEM)
ANY = pl.BlockSpec(memory_space=pl.ANY)


def dot(left, right):
    return jnp.dot(left, right, preferred_element_type=F32)


def cross(left, right):
    return lax.dot_general(left, right, (((0,), (0,)), ((), ())), preferred_element_type=F32)


def call(kernel, out_shape, n_smem, n_args, flops, name, scratch=(), in_specs=None, out_specs=None, mib=12, aliases=None):
    return pl.pallas_call(
        kernel,
        out_shape=out_shape,
        in_specs=in_specs or [SMEM] * n_smem + [VMEM] * n_args,
        out_specs=out_specs or jax.tree.map(lambda _: VMEM, out_shape),
        scratch_shapes=list(scratch),
        input_output_aliases=aliases or {},
        compiler_params=pltpu.CompilerParams(vmem_limit_bytes=mib * 2**20),
        cost_estimate=pl.CostEstimate(flops=flops, bytes_accessed=2**20, transcendentals=0),
        name=name,
    )


def piece(place, step, size):
    return pl.ds(pl.multiple_of(lax.bitwise_xor(place[2], jnp.int32(step)) * size, size), size)


def tree_sum(values):
    while len(values) > 1:
        values = [left + right for left, right in zip(values[::2], values[1::2])]
    return values[0]


def later_kernel(place, own, after, part, sem):
    del after
    size = part.shape[0]
    copy = pltpu.make_async_copy(own.at[pl.ds(pl.multiple_of(place[0] * size, size), size), :], part, sem)
    copy.start()
    copy.wait()


def chip_gram_kernel(place, own, mate, keep, send1, send2, send3, slab):
    core = place[1]
    width = own.shape[1]
    size = keep.shape[0]
    slab[pl.ds(pl.multiple_of(core * width, width), width), :] = cross(own[...], own[...])
    slab[pl.ds(pl.multiple_of((1 - core) * width, width), width), :] = cross(own[...], mate[...])
    for step, out in enumerate((keep, send1, send2, send3)):
        out[...] = slab[piece(place, step, size), :]


def chip_sum_kernel(keep, part1, part2, part3, later, total):
    del later
    total[...] = tree_sum([keep[...], part1[...], part2[...], part3[...]])


def pair_gram_kernel(place, own, mate, across, *rest):
    chip_parts, (chip_piece, keep, send1, send2, send3, slab) = rest[:-6], rest[-6:]
    chip = place[0]
    half, width = across.shape
    size = keep.shape[0]
    rows = pl.ds(pl.multiple_of(chip * half, half), half)
    same = cross(across[...], own[rows, :])
    other = cross(across[...], mate[rows, :])
    slab[0:width, :] = jnp.where(chip == 0, same.T, same)
    slab[width : 2 * width, :] = jnp.where(chip == 0, other.T, other)
    chip_sum = tree_sum([part[...] for part in chip_parts])
    chip_piece[...] = chip_sum
    keep[...] = slab[piece(place, 0, size), :]
    for step, out in enumerate((send1, send2, send3)):
        out[0:size, :] = slab[piece(place, step + 1, size), :]
        out[size : 2 * size, :] = chip_sum


def pass_kernel(value, after, same):
    del value, after, same


def group_sum_kernel(place, keep, chip_piece, part1, part2, part3, mate1, total, payload, chip_slab):
    del mate1
    size = keep.shape[0]
    parts = (part1, part2, part3)
    group_sum = tree_sum([keep[...]] + [part[0:size, :] for part in parts])
    total[...] = group_sum
    payload[0:size, :] = group_sum
    payload[size : 2 * size, :] = chip_piece[...]
    chip_slab[piece(place, 0, size), :] = chip_piece[...]
    for step, part in enumerate(parts):
        chip_slab[piece(place, step + 1, size), :] = part[size : 2 * size, :]


def pair_sum_kernel(total, across, *rest):
    parts, payload = rest[:-2], rest[-1]
    size = total.shape[0]
    payload[0:size, :] = tree_sum([total[...], across[0:size, :]] + [part[...] for part in parts])
    payload[size : 2 * size, :] = across[size : 2 * size, :]


def join_kernel(place, own, part1, part2, part3, chip_mine, joined):
    size = own.shape[0] // 2
    for step, part in enumerate((own, part1, part2, part3)):
        joined[piece(place, step, size), :] = part[0:size, :]
        start = pl.multiple_of(8 * size + lax.bitwise_xor(place[2], jnp.int32(step)) * size, size)
        joined[pl.ds(start, size), :] = part[size : 2 * size, :]
    joined[4 * size : 8 * size, :] = chip_mine[...]


def split(value):
    high = value.astype(BF16)
    return high, (value - high.astype(F32)).astype(BF16)


def product(left, right):
    return dot(left[0], right[0]) + (dot(left[0], right[1]) + dot(left[1], right[0]))


def row_product(left, right):
    count = left[0].shape[0]
    both = dot(jnp.concatenate(left, axis=0), right[0])
    return both[:count] + (both[count:] + dot(left[0], right[1]))


def symmetric(first, mixed, last):
    return jnp.concatenate(
        [jnp.concatenate([first, mixed], axis=1), jnp.concatenate([mixed.T, last], axis=1)], axis=0
    )


def symmetric_square(high, low):
    half = high.shape[0] // 2
    cross_part = dot(high, low)
    upper = dot(high[:half], high)
    last = dot(high[half:], high[:, half:])
    return symmetric(
        upper[:, :half] + (cross_part[:half, :half] + cross_part[:half, :half].T),
        upper[:, half:] + (cross_part[:half, half:] + cross_part[half:, :half].T),
        last + (cross_part[half:, half:] + cross_part[half:, half:].T),
    )


def symmetric_product(left, right):
    half = left[0].shape[0] // 2
    upper = product((left[0][:half], left[1][:half]), right)
    last = product((left[0][half:], left[1][half:]), (right[0][:, half:], right[1][:, half:]))
    return symmetric(upper[:, :half], upper[:, half:], last)


def finish_kernel(
    total_rows, place, active, joined_mine, joined_mate, own, mate, across1, mate1, across2, mate2,
    out, gram, highs, lows, factor, left, result, state_flags, sems, out_sems,
):
    chip, core = place[0], place[1]
    half, width = across1.shape
    cols = gram.shape[0]
    near, far = pl.multiple_of(chip * half, half), pl.multiple_of((1 - chip) * half, half)
    fetch = pltpu.make_async_copy(active, state_flags, sems.at[6])
    fetch.start()
    every = pl.ds(0, 2 * half)
    copies = [
        pltpu.make_async_copy(source, left.at[where, index * width : (index + 1) * width], sems.at[number])
        for number, (source, where, index) in enumerate(
            [
                (own, every, 0),
                (mate, every, 1),
                (across1, pl.ds(near, half), 2),
                (mate1, pl.ds(near, half), 3),
                (across2, pl.ds(far, half), 2),
                (mate2, pl.ds(far, half), 3),
            ]
        )
    ]
    for copy in copies:
        copy.start()

    def parts(part):
        rows = slice(2 * width * part, 2 * width * (part + 1))
        mine, theirs = joined_mine[rows, :], joined_mate[rows, :]
        core0 = jnp.where(core == 0, mine, theirs)
        core1 = jnp.where(core == 0, theirs, mine)
        return core0[:width], core0[width:], core1[:width], core1[width:]

    def put(row, col, value):
        gram[row * width : (row + 1) * width, col * width : (col + 1) * width] = value

    here, there = parts(1), parts(2)
    there = there[0], there[3], there[2], there[1]
    for side in range(2):
        top0, low0, top1, low1 = [jnp.where(chip == side, near_part, far_part) for near_part, far_part in zip(here, there)]
        put(2 * side, 2 * side, top0)
        put(2 * side, 2 * side + 1, low0)
        put(2 * side + 1, 2 * side, top1)
        put(2 * side + 1, 2 * side + 1, low1)
    top0, low0, top1, low1 = parts(0)
    off10 = jnp.where(chip == 0, low0, low1)
    off01 = jnp.where(chip == 0, low1, low0)
    put(0, 2, top0)
    put(1, 3, top1)
    put(0, 3, off01)
    put(1, 2, off10)
    put(2, 0, top0.T)
    put(3, 1, top1.T)
    put(3, 0, off01.T)
    put(2, 1, off10.T)

    fetch.wait()
    states = active.shape[0]
    vecs = cols // states
    col_state = lax.broadcasted_iota(jnp.int32, (1, cols), 1) // vecs
    flags = jnp.zeros((1, cols), F32)
    for state in range(states):
        flags = jnp.where(col_state == state, state_flags[state].astype(F32), flags)
    square = jnp.zeros((vecs, cols), F32)
    for state in range(states):
        rows = slice(state * vecs, (state + 1) * vecs)
        kept = jnp.where(jnp.logical_and(flags != 0, state_flags[state] != 0), gram[rows, :], 0.0)
        diagonal = lax.broadcasted_iota(jnp.int32, (vecs, cols), 0) + state * vecs == lax.broadcasted_iota(
            jnp.int32, (vecs, cols), 1
        )
        kept = kept + jnp.where(diagonal, (1.0 - flags) * total_rows, 0.0)
        gram[rows, :] = kept
        square = square + kept * kept
    frob_square = jnp.sum(jnp.sum(square, axis=0, keepdims=True), axis=1, keepdims=True)
    frob_norm = jnp.sqrt(frob_square)
    inverse_norm = 1.0 / frob_norm

    current = gram[...] * inverse_norm
    start = (2 * chip + core) * width
    last = ITERS - 2
    for step in range(last):
        high, low = split(current)
        highs[step], lows[step] = high, low
        square = symmetric_square(high, low)
        cube = symmetric_product((high, low), split(square))
        current = 2.25 * current - 1.5 * square + 0.25 * cube
    highs[last], lows[last] = split(current)
    gram[...] = current

    def times(step, slab):
        return row_product(split(slab), (highs[step], lows[step]))

    def newton(step, slab):
        return 1.5 * slab - 0.5 * times(step, slab)

    row_id = lax.broadcasted_iota(jnp.int32, (width, cols), 0) + start
    col_id = lax.broadcasted_iota(jnp.int32, (width, cols), 1)
    unit = jnp.where(row_id == col_id, 1.0, 0.0)
    slab = 1.5 * unit - 0.5 * gram[pl.ds(pl.multiple_of(start, width), width), :]
    slab = 1.5 * unit - 0.5 * times(last, newton(last, slab))
    for step in range(last, -1, -1):
        slab = newton(step, slab)
    slab = slab * jnp.sqrt(total_rows / frob_norm)

    factor[...] = jnp.where(flags != 0, slab, unit).T.astype(BF16)

    def block(index):
        return factor[pl.ds(pl.multiple_of(index * width, width), width), :]

    weights = jnp.concatenate(
        [
            block(2 * chip + core),
            block(2 * chip + 1 - core),
            block(2 * (1 - chip) + core),
            block(2 * (1 - chip) + 1 - core),
        ],
        axis=0,
    )
    for copy in copies:
        copy.wait()
    pieces = out_sems.shape[0]
    size = out.shape[0] // pieces
    stores = []
    for piece in range(pieces):
        rows = slice(piece * size, (piece + 1) * size)
        result[rows, :] = dot(left[rows, :], weights).astype(BF16)
        stores.append(pltpu.make_async_copy(result.at[rows, :], out.at[rows, :], out_sems.at[piece]))
        stores[-1].start()
    for store in stores:
        store.wait()


def shards(vectors, active):
    rows, width = vectors.shape
    half = rows // 2
    row_devices = lax.axis_size("row")
    total_rows = rows * row_devices
    cols = width * lax.axis_size("state")
    state, row = lax.axis_index("state"), lax.axis_index("row")
    chip, core = state // 2, state % 2
    place = jnp.stack([chip, core, row % 4]).astype(jnp.int32)
    size = width // 2
    shape = jax.ShapeDtypeStruct
    small, slab = shape((size, width), F32), shape((2 * width, width), F32)

    def swap(value, bit):
        return lax.ppermute(value, "state", [(index, index ^ bit) for index in range(4)])

    def move(value, bits, chips=0):
        pairs = []
        for state_from in range(4):
            for row_from in range(row_devices):
                state_to = state_from ^ ((2 if row_from % 4 < 2 else 3) if chips else 0)
                pairs.append((state_from * row_devices + row_from, state_to * row_devices + (row_from ^ bits)))
        return lax.ppermute(value, ("state", "row"), pairs)

    def after(value, other):
        return call(
            pass_kernel, shape(value.shape, value.dtype), 0, 0, 0, "after", in_specs=[ANY, ANY], out_specs=ANY,
            aliases={0: 0},
        )(value, other)

    across1 = swap(lax.dynamic_slice_in_dim(vectors, (1 - chip) * half, half, 0), 2)
    mate = swap(vectors, 1)
    keep, *sends = call(
        chip_gram_kernel, (small,) * 4, 1, 2, 4 * rows * width * width, "chip_gram", scratch=[pltpu.VMEM(slab.shape, F32)]
    )(place, vectors, mate)
    later = call(
        later_kernel, shape((half, width), BF16), 1, 0, 0, "later", scratch=[pltpu.SemaphoreType.DMA],
        in_specs=[SMEM, ANY, ANY], out_specs=ANY,
    )(place, vectors, keep)
    across2 = swap(later, 2)

    groups = [4 * index for index in range(row_devices // 4)]
    parts = [move(send, step + 1) for step, send in enumerate(sends)]
    chip_sum = call(chip_sum_kernel, small, 0, 4, 0, "chip_sum", in_specs=[VMEM] * 4 + [ANY])(keep, *parts, later)
    chip_parts = [chip_sum] + [move(chip_sum, bits) for bits in groups[1:]]
    double = shape((2 * size, width), F32)
    chip_piece, keep, *sends = call(
        pair_gram_kernel, (small, small, double, double, double), 1, 3 + len(chip_parts), 4 * half * width * width,
        "pair_gram", scratch=[pltpu.VMEM(slab.shape, F32)],
    )(place, vectors, mate, across1, *chip_parts)
    parts = [move(send, step + 1) for step, send in enumerate(sends)]
    mate1 = swap(after(across1, chip_piece), 1)
    pair_sum, payload, chip_mine = call(
        group_sum_kernel, (small, double, slab), 0, 0, 0, "group_sum", in_specs=[SMEM] + [VMEM] * 5 + [ANY]
    )(place, keep, chip_piece, *parts, mate1)
    pair_parts = [move(payload, 0, 1)] + [move(pair_sum, bits, chips) for bits in groups[1:] for chips in range(2)]
    payload = call(
        pair_sum_kernel, double, 0, 0, 0, "pair_sum", in_specs=[VMEM] * (1 + len(pair_parts)) + [ANY]
    )(pair_sum, *pair_parts, across2)
    parts = [move(payload, step) for step in (1, 2, 3)]
    mate2 = swap(after(across2, payload), 1)
    joined_mine = call(join_kernel, shape((6 * width, width), F32), 1, 5, 0, "join")(place, payload, *parts, chip_mine)
    joined_mate = swap(joined_mine, 1)

    return call(
        functools.partial(finish_kernel, float(total_rows)),
        shape((rows, width), BF16),
        0,
        0,
        12 * cols**3 * 3 + 2 * rows * cols * width,
        "finish",
        scratch=[
            pltpu.VMEM((cols, cols), F32),
            pltpu.VMEM((ITERS - 1, cols, cols), BF16),
            pltpu.VMEM((ITERS - 1, cols, cols), BF16),
            pltpu.VMEM((cols, width), BF16),
            pltpu.VMEM((rows, cols), BF16),
            pltpu.VMEM((rows, width), BF16),
            pltpu.SMEM(active.shape, jnp.int32),
            pltpu.SemaphoreType.DMA((7,)),
            pltpu.SemaphoreType.DMA((4,)),
        ],
        in_specs=[SMEM, ANY, VMEM, VMEM] + [ANY] * 6,
        out_specs=ANY,
        mib=24,
    )(
        place, active, joined_mine, joined_mate, vectors, mate, across1, mate1, across2, mate2
    )


def solution(mesh):
    in_specs = (P("row", "state"), P())
    out_specs = P("row", "state")
    return jax.shard_map(shards, mesh=mesh, in_specs=in_specs, out_specs=out_specs, check_vma=False)
```

time: 63.4 us -> 58.1 us (0.916)
  waiting for transfers between devices: 24.9 us -> 19.1 us
  starting transfers between devices: 19.3 us -> 22.6 us
  local copies, waits for them, and re-layouts: 3.32 us -> 1.15 us
    ppermute x1 -> x13, starting transfers between devices: 1.56 us -> 17.7 us  [move(): return lax.ppermute(value, ('state', 'row'), pairs)]
    ppermute x1 -> x13, waiting for transfers between devices: 2.24 us -> 15.2 us  [move(): return lax.ppermute(value, ('state', 'row'), pairs)]
    all_to_all x3 -> x0, waiting for transfers between devices: 12.6 us -> none  [exchange(): return lax.all_to_all(value, 'row', 0, 0, tiled=True)]
    all_to_all x3 -> x0, starting transfers between devices: 12.6 us -> none  [exchange(): return lax.all_to_all(value, 'row', 0, 0, tiled=True)]
    ppermute x9 -> x6, waiting for transfers between devices: 10 us -> 3.97 us  [swap(): lax.ppermute(value, 'state', [(index, index ^ bit) for index in range(4)])]
    unnamed x6, local copies, waits for them, and re-layouts: 1.45 us -> 0.08 us
    dynamic_slice x1, local copies, waits for them, and re-layouts: 1.87 us -> 1.08 us  [shards(): lax.dynamic_slice_in_dim(vectors, (1 - chip) * half, half, 0)]
    pallas_call x4 -> x9, Pallas kernels: 4.42 us -> 4.14 us  [the longest x1 1.3 us: shards(): call(chip_gram_kernel, (small,) * 4, 1, 2, 4 * rows * width * width, 'chi...]
  transfers between devices with their start and end apart: 13 -> 19, of which waited for: 8 -> 13; matrix products, arithmetic and copies ran while one was open for 3% -> 2% of each run, Pallas kernels for 7% -> 5%
where the time goes in v3:
time: 58.1 us; the launch traced here: 58 us
  starting transfers between devices  22.6 us (39%)
  waiting for transfers between devices  19.1 us (33%)
  Pallas kernels  14.9 us (26%)
  local copies, waits for them, and re-layouts  1.15 us (2%)
    ppermute x13, starting transfers between devices, move(): return lax.ppermute(value, ('state', 'row'), pairs)  17.7 us
    ppermute x13, waiting for transfers between devices, move(): return lax.ppermute(value, ('state', 'row'), pairs)  15.2 us
    pallas_call x1, Pallas kernels, shards(): call(functools.partial(finish_kernel, float(total_rows)), shape((rows, wi...  10.8 us
    ppermute x6, starting transfers between devices, swap(): lax.ppermute(value, 'state', [(index, index ^ bit) for index in range(4)])  4.87 us
    ppermute x6, waiting for transfers between devices, swap(): lax.ppermute(value, 'state', [(index, index ^ bit) for index in range(4)])  3.97 us
    pallas_call x1, Pallas kernels, shards(): call(chip_gram_kernel, (small,) * 4, 1, 2, 4 * rows * width * width, 'chi...  1.3 us
  transfers between devices with their start and end apart: 19, of which 13 were waited for; matrix products, arithmetic and copies ran while one was open for 2% of the time, Pallas kernels for 5%

profile of v3, /device:TPU:0, one launch (start us, length us, event | category | flops | bytes accessed | tf_op | source)
XLA Modules:
  0.0 58.0 jit_solution(3069592160989387198)
XLA Ops:
  0.0 0.0 copy-start
  0.0 0.5 collective-permute-start
  0.5 1.1 %constant_dynamic-slice_fusion = bf16[2048,128]{1,0:T(8,128)(2,1)S(1)} fusion(bf16[4096,128]{1,0:T(8,128)(2,1)} %own.7, s32[]{:T(128)S(6)} %select_n.21), kind=kLoop, calls=%fused_computation.1 | loop fusion | bytes 1048580 | tf_op jit(solution)/shard_map/dynamic_slice | solution.py:327
  1.5 2.6 %collective-permute-start.1 = (bf16[2048,128]{1,0:T(8,128)(2,1)S(1)}, bf16[2048,128]{1,0:T(8,128)(2,1)S(1)}, u32[]{:S(2)}, u32[]{:S(2)}) collective-permute-start(bf16[2048,128]{1,0:T(8,128)(2,1)S(1)} %constant_dynamic-slice_fusion), channel_id=1, source_target_pairs={{0,16},{8,24},{16,0},{24,8},{1,17},{9,25},{17,1},{25,9},{2,18},{10... | collective-permute-start | bytes 1572872 | tf_op jit(solution)/shard_map/ppermute | solution.py:311
  4.2 0.1 pad_add_fusion.place
  4.3 0.0 collective-permute-done.mate
  4.3 0.0 copy-done
  4.3 1.3 %chip_gram.1 = (f32[64,128]{1,0:T(8,128)S(1)}, f32[64,128]{1,0:T(8,128)S(1)}, f32[64,128]{1,0:T(8,128)S(1)}, f32[64,128]{1,0:T(8,128)S(1)}) custom-call(s32[3]{0:T(128)S(1)} %pad_add_fusion.place, bf16[4096,128]{1,0:T(8,128)(2,1)S(1)} %copy-done, bf16[4096,128]{1,0:T(8,128)(2,1)S(1)} %collective-permute-done.mate), custom_call_target="tpu_custom_call" | custom-call | flops 268435456 | bytes 1048576 | tf_op jit(solution)/shard_map/chip_gram/pallas_call | solution.py:329
  5.6 1.6 %collective-permute-start.2 = (f32[64,128]{1,0:T(8,128)S(1)}, f32[64,128]{1,0:T(8,128)S(1)}, u32[]{:S(2)}, u32[]{:S(2)}) collective-permute-start(f32[64,128]{1,0:T(8,128)S(1)} %get-tuple-element.18), channel_id=1, source_target_pairs={{0,1},{1,0},{2,3},{3,2},{4,5},{5,4},{6,7},{7,6},{8,9},{9,8},{10,11... | collective-permute-start | bytes 98312 | tf_op jit(solution)/shard_map/ppermute | solution.py:319
  7.2 1.6 %collective-permute-start.3 = (f32[64,128]{1,0:T(8,128)S(1)}, f32[64,128]{1,0:T(8,128)S(1)}, u32[]{:S(2)}, u32[]{:S(2)}) collective-permute-start(f32[64,128]{1,0:T(8,128)S(1)} %get-tuple-element.19), channel_id=1, source_target_pairs={{0,2},{1,3},{2,0},{3,1},{4,6},{5,7},{6,4},{7,5},{8,10},{9,11},{10,... | collective-permute-start | bytes 98312 | tf_op jit(solution)/shard_map/ppermute | solution.py:319
  8.8 0.3 collective-permute-start.4
  9.1 0.6 %later.1 = bf16[2048,128]{1,0:T(8,128)(2,1)S(1)} custom-call(s32[3]{0:T(128)S(1)} %pad_add_fusion.place, bf16[4096,128]{1,0:T(8,128)(2,1)S(1)} %copy-done, f32[64,128]{1,0:T(8,128)S(1)} %get-tuple-element.17.after.keep), custom_call_target="tpu_custom_call" | custom-call | bytes 1048576 | tf_op jit(solution)/shard_map/later/pallas_call | solution.py:332
  9.7 0.0 collective-permute-done.2.part1
  9.7 1.6 %collective-permute-done.3.part2 = f32[64,128]{1,0:T(8,128)S(1)} collective-permute-done((f32[64,128]{1,0:T(8,128)S(1)}, f32[64,128]{1,0:T(8,128)S(1)}, u32[]{:S(2)}, u32[]{:S(2)}) %collective-permute-start.3) | collective-permute-done | bytes 32800 | tf_op jit(solution)/shard_map/ppermute | solution.py:319
  11.3 2.3 %collective-permute-done.4.part3 = f32[64,128]{1,0:T(8,128)S(1)} collective-permute-done((f32[64,128]{1,0:T(8,128)S(1)}, f32[64,128]{1,0:T(8,128)S(1)}, u32[]{:S(2)}, u32[]{:S(2)}) %collective-permute-start.4) | collective-permute-done | bytes 32800 | tf_op jit(solution)/shard_map/ppermute | solution.py:319
  13.6 2.7 %collective-permute-start.5 = (f32[64,128]{1,0:T(8,128)S(1)}, f32[64,128]{1,0:T(8,128)S(1)}, u32[]{:S(2)}, u32[]{:S(2)}) collective-permute-start(f32[64,128]{1,0:T(8,128)S(1)} %chip_sum.1.rest_0_), channel_id=1, source_target_pairs={{0,4},{1,5},{2,6},{3,7},{4,0},{5,1},{6,2},{7,3},{8,12},{9,13},{10,... | collective-permute-start | bytes 98312 | tf_op jit(solution)/shard_map/ppermute | solution.py:319
  16.3 0.4 collective-permute-done.1.across.across1
  16.7 2.0 %collective-permute-done.5.rest_1_ = f32[64,128]{1,0:T(8,128)S(1)} collective-permute-done((f32[64,128]{1,0:T(8,128)S(1)}, f32[64,128]{1,0:T(8,128)S(1)}, u32[]{:S(2)}, u32[]{:S(2)}) %collective-permute-start.5) | collective-permute-done | bytes 32800 | tf_op jit(solution)/shard_map/ppermute | solution.py:319
  18.7 1.1 %pair_gram.1 = (f32[64,128]{1,0:T(8,128)S(1)}, f32[64,128]{1,0:T(8,128)S(1)}, f32[128,128]{1,0:T(8,128)S(1)}, f32[128,128]{1,0:T(8,128)S(1)}, f32[128,128]{1,0:T(8,128)S(1)}) custom-call(s32[3]{0:T(128)S(1)} %pad_add_fusion.place, bf16[4096,128]{1,0:T(8,128)(2,1)S(1)} %copy-done, bf16[4096,128]{1,0:T(8,128)(2,1)S(1)} %collective-permute-done.mate, ...), custom_call_target="tpu_custom_call" | custom-call | flops 134217728 | bytes 1048576 | tf_op jit(solution)/shard_map/pair_gram/pallas_call | solution.py:343
  19.8 0.1 collective-permute-start.9
  19.9 1.6 %collective-permute-start.13 = (bf16[2048,128]{1,0:T(8,128)(2,1)S(1)}, bf16[2048,128]{1,0:T(8,128)(2,1)S(1)}, u32[]{:S(2)}, u32[]{:S(2)}) collective-permute-start(bf16[2048,128]{1,0:T(8,128)(2,1)S(1)} %later.1), channel_id=1, source_target_pairs={{0,16},{8,24},{16,0},{24,8},{1,17},{9,25},{17,1},{25,9},{2,18},{10... | collective-permute-start | bytes 1572872 | tf_op jit(solution)/shard_map/ppermute | solution.py:311
  21.5 0.5 collective-permute-start.6
  22.0 0.9 %collective-permute-start.7 = (f32[128,128]{1,0:T(8,128)S(1)}, f32[128,128]{1,0:T(8,128)S(1)}, u32[]{:S(2)}, u32[]{:S(2)}) collective-permute-start(f32[128,128]{1,0:T(8,128)S(1)} %get-tuple-element.24), channel_id=1, source_target_pairs={{0,2},{1,3},{2,0},{3,1},{4,6},{5,7},{6,4},{7,5},{8,10},{9,11},{10,... | collective-permute-start | bytes 196616 | tf_op jit(solution)/shard_map/ppermute | solution.py:319
  22.8 2.1 %collective-permute-start.8 = (f32[128,128]{1,0:T(8,128)S(1)}, f32[128,128]{1,0:T(8,128)S(1)}, u32[]{:S(2)}, u32[]{:S(2)}) collective-permute-start(f32[128,128]{1,0:T(8,128)S(1)} %get-tuple-element.25), channel_id=1, source_target_pairs={{0,3},{1,2},{2,1},{3,0},{4,7},{5,6},{6,5},{7,4},{8,11},{9,10},{10,... | collective-permute-start | bytes 196616 | tf_op jit(solution)/shard_map/ppermute | solution.py:319
  25.0 0.8 %collective-permute-done.6.part1 = f32[128,128]{1,0:T(8,128)S(1)} collective-permute-done((f32[128,128]{1,0:T(8,128)S(1)}, f32[128,128]{1,0:T(8,128)S(1)}, u32[]{:S(2)}, u32[]{:S(2)}) %collective-permute-start.6) | collective-permute-done | bytes 65568 | tf_op jit(solution)/shard_map/ppermute | solution.py:319
  25.7 1.1 %collective-permute-done.7.part2 = f32[128,128]{1,0:T(8,128)S(1)} collective-permute-done((f32[128,128]{1,0:T(8,128)S(1)}, f32[128,128]{1,0:T(8,128)S(1)}, u32[]{:S(2)}, u32[]{:S(2)}) %collective-permute-start.7) | collective-permute-done | bytes 65568 | tf_op jit(solution)/shard_map/ppermute | solution.py:319
  26.8 1.4 %collective-permute-done.8.part3 = f32[128,128]{1,0:T(8,128)S(1)} collective-permute-done((f32[128,128]{1,0:T(8,128)S(1)}, f32[128,128]{1,0:T(8,128)S(1)}, u32[]{:S(2)}, u32[]{:S(2)}) %collective-permute-start.8) | collective-permute-done | bytes 65568 | tf_op jit(solution)/shard_map/ppermute | solution.py:319
  28.2 0.0 collective-permute-done.9.mate1
  28.2 0.6 group_sum.1
  28.8 0.6 %collective-permute-start.10 = (f32[128,128]{1,0:T(8,128)S(1)}, f32[128,128]{1,0:T(8,128)S(1)}, u32[]{:S(2)}, u32[]{:S(2)}) collective-permute-start(f32[128,128]{1,0:T(8,128)S(1)} %get-tuple-element.27), channel_id=1, source_target_pairs={{0,16},{1,17},{2,26},{3,27},{4,20},{5,21},{6,30},{7,31},{8,24},{9,... | collective-permute-start | bytes 196616 | tf_op jit(solution)/shard_map/ppermute | solution.py:319
  29.4 3.3 %collective-permute-start.12 = (f32[64,128]{1,0:T(8,128)S(1)}, f32[64,128]{1,0:T(8,128)S(1)}, u32[]{:S(2)}, u32[]{:S(2)}) collective-permute-start(f32[64,128]{1,0:T(8,128)S(1)} %get-tuple-element.26.total), channel_id=1, source_target_pairs={{0,20},{1,21},{2,30},{3,31},{4,16},{5,17},{6,26},{7,27},{8,28},{9,... | collective-permute-start | bytes 98312 | tf_op jit(solution)/shard_map/ppermute | solution.py:319
  32.7 0.5 collective-permute-start.11
  33.3 1.8 %collective-permute-done.13.rest_2_.across2 = bf16[2048,128]{1,0:T(8,128)(2,1)S(1)} collective-permute-done((bf16[2048,128]{1,0:T(8,128)(2,1)S(1)}, bf16[2048,128]{1,0:T(8,128)(2,1)S(1)}, u32[]{:S(2)}, u32[]{:S(2)}) %collective-permute-start.13) | collective-permute-done | bytes 524320 | tf_op jit(solution)/shard_map/ppermute | solution.py:311
  35.1 0.5 collective-permute-done.12.rest_1_
  35.6 2.3 %collective-permute-done.11.rest_0_ = f32[64,128]{1,0:T(8,128)S(1)} collective-permute-done((f32[64,128]{1,0:T(8,128)S(1)}, f32[64,128]{1,0:T(8,128)S(1)}, u32[]{:S(2)}, u32[]{:S(2)}) %collective-permute-start.11) | collective-permute-done | bytes 32800 | tf_op jit(solution)/shard_map/ppermute | solution.py:319
  37.9 0.0 collective-permute-done.10.across
  37.9 0.1 collective-permute-start.18
  38.0 1.3 %collective-permute-start.16 = (f32[128,128]{1,0:T(8,128)S(1)}, f32[128,128]{1,0:T(8,128)S(1)}, u32[]{:S(2)}, u32[]{:S(2)}) collective-permute-start(f32[128,128]{1,0:T(8,128)S(1)} %pair_sum.1.own.after), channel_id=1, source_target_pairs={{0,3},{1,2},{2,1},{3,0},{4,7},{5,6},{6,5},{7,4},{8,11},{9,10},{10,... | collective-permute-start | bytes 196616 | tf_op jit(solution)/shard_map/ppermute | solution.py:319
  39.3 0.7 %collective-permute-start.15 = (f32[128,128]{1,0:T(8,128)S(1)}, f32[128,128]{1,0:T(8,128)S(1)}, u32[]{:S(2)}, u32[]{:S(2)}) collective-permute-start(f32[128,128]{1,0:T(8,128)S(1)} %pair_sum.1.own.after), channel_id=1, source_target_pairs={{0,2},{1,3},{2,0},{3,1},{4,6},{5,7},{6,4},{7,5},{8,10},{9,11},{10,... | collective-permute-start | bytes 196616 | tf_op jit(solution)/shard_map/ppermute | solution.py:319
  40.0 1.5 %collective-permute-start.14 = (f32[128,128]{1,0:T(8,128)S(1)}, f32[128,128]{1,0:T(8,128)S(1)}, u32[]{:S(2)}, u32[]{:S(2)}) collective-permute-start(f32[128,128]{1,0:T(8,128)S(1)} %pair_sum.1.own.after), channel_id=1, source_target_pairs={{0,1},{1,0},{2,3},{3,2},{4,5},{5,4},{6,7},{7,6},{8,9},{9,8},{10,11... | collective-permute-start | bytes 196616 | tf_op jit(solution)/shard_map/ppermute | solution.py:319
  41.6 2.3 %collective-permute-done.16.part3 = f32[128,128]{1,0:T(8,128)S(1)} collective-permute-done((f32[128,128]{1,0:T(8,128)S(1)}, f32[128,128]{1,0:T(8,128)S(1)}, u32[]{:S(2)}, u32[]{:S(2)}) %collective-permute-start.16) | collective-permute-done | bytes 65568 | tf_op jit(solution)/shard_map/ppermute | solution.py:319
  43.9 0.0 collective-permute-done.15.part2
  43.9 1.0 %collective-permute-done.14.part1 = f32[128,128]{1,0:T(8,128)S(1)} collective-permute-done((f32[128,128]{1,0:T(8,128)S(1)}, f32[128,128]{1,0:T(8,128)S(1)}, u32[]{:S(2)}, u32[]{:S(2)}) %collective-permute-start.14) | collective-permute-done | bytes 65568 | tf_op jit(solution)/shard_map/ppermute | solution.py:319
  44.8 0.0 copy-start.1
  44.8 0.6 join.1.joined_mine
  45.4 0.1 collective-permute-start.17
  45.5 1.7 %collective-permute-done.17.joined_mate = f32[768,128]{1,0:T(8,128)S(1)} collective-permute-done((f32[768,128]{1,0:T(8,128)S(1)}, f32[768,128]{1,0:T(8,128)S(1)}, u32[]{:S(2)}, u32[]{:S(2)}) %collective-permute-start.17) | collective-permute-done | bytes 393248 | tf_op jit(solution)/shard_map/ppermute | solution.py:311
  47.2 0.0 collective-permute-done.18.mate2
  47.2 0.0 copy-done.1
  47.2 10.8 %finish.1 = bf16[4096,128]{1,0:T(8,128)(2,1)} custom-call(s32[3]{0:T(128)S(1)} %pad_add_fusion.place, s32[8]{0:T(128)S(1)} %copy-done.1, f32[768,128]{1,0:T(8,128)S(1)} %join.1.joined_mine, f32[768,128]{1,0:T(8,128)S(1)} %collective-permute-done.17.joined_mate, bf16[4096,128]{1,0:T(8,128)(2,1)S(1)} %copy-done, ...), custom_call_target="tpu_custom_call" | custom-call | flops 5368709120 | bytes 1048576 | tf_op jit(solution)/shard_map/finish/pallas_call | solution.py:361
  (6 shorter events, 0.1 us)
Async XLA Ops:
  0.0 4.3 %copy-start = (bf16[4096,128]{1,0:T(8,128)(2,1)S(1)}, bf16[4096,128]{1,0:T(8,128)(2,1)}, u32[]{:S(2)}) copy-start(bf16[4096,128]{1,0:T(8,128)(2,1)} %own.7) | copy-start | bytes 3145732
  0.0 4.3 %collective-permute-start = (bf16[4096,128]{1,0:T(8,128)(2,1)}, bf16[4096,128]{1,0:T(8,128)(2,1)S(1)}, u32[]{:S(2)}, u32[]{:S(2)}) collective-permute-start(bf16[4096,128]{1,0:T(8,128)(2,1)} %own.7), channel_id=1, source_target_pairs={{0,8},{8,0},{16,24},{24,16},{1,9},{9,1},{17,25},{25,17},{2,10},{10... | collective-permute-start | bytes 3145736 | tf_op jit(solution)/shard_map/ppermute | solution.py:311
  1.5 15.2 %collective-permute-start.1 = (bf16[2048,128]{1,0:T(8,128)(2,1)S(1)}, bf16[2048,128]{1,0:T(8,128)(2,1)S(1)}, u32[]{:S(2)}, u32[]{:S(2)}) collective-permute-start(bf16[2048,128]{1,0:T(8,128)(2,1)S(1)} %constant_dynamic-slice_fusion), channel_id=1, source_target_pairs={{0,16},{8,24},{16,0},{24,8},{1,17},{9,25},{17,1},{25,9},{2,18},{10... | collective-permute-start | bytes 1572872 | tf_op jit(solution)/shard_map/ppermute | solution.py:311
  5.6 4.2 %collective-permute-start.2 = (f32[64,128]{1,0:T(8,128)S(1)}, f32[64,128]{1,0:T(8,128)S(1)}, u32[]{:S(2)}, u32[]{:S(2)}) collective-permute-start(f32[64,128]{1,0:T(8,128)S(1)} %get-tuple-element.18), channel_id=1, source_target_pairs={{0,1},{1,0},{2,3},{3,2},{4,5},{5,4},{6,7},{7,6},{8,9},{9,8},{10,11... | collective-permute-start | bytes 98312 | tf_op jit(solution)/shard_map/ppermute | solution.py:319
  7.2 4.1 %collective-permute-start.3 = (f32[64,128]{1,0:T(8,128)S(1)}, f32[64,128]{1,0:T(8,128)S(1)}, u32[]{:S(2)}, u32[]{:S(2)}) collective-permute-start(f32[64,128]{1,0:T(8,128)S(1)} %get-tuple-element.19), channel_id=1, source_target_pairs={{0,2},{1,3},{2,0},{3,1},{4,6},{5,7},{6,4},{7,5},{8,10},{9,11},{10,... | collective-permute-start | bytes 98312 | tf_op jit(solution)/shard_map/ppermute | solution.py:319
  8.8 4.8 %collective-permute-start.4 = (f32[64,128]{1,0:T(8,128)S(1)}, f32[64,128]{1,0:T(8,128)S(1)}, u32[]{:S(2)}, u32[]{:S(2)}) collective-permute-start(f32[64,128]{1,0:T(8,128)S(1)} %get-tuple-element.20), channel_id=1, source_target_pairs={{0,3},{1,2},{2,1},{3,0},{4,7},{5,6},{6,5},{7,4},{8,11},{9,10},{10,... | collective-permute-start | bytes 98312 | tf_op jit(solution)/shard_map/ppermute | solution.py:319
  13.6 5.1 %collective-permute-start.5 = (f32[64,128]{1,0:T(8,128)S(1)}, f32[64,128]{1,0:T(8,128)S(1)}, u32[]{:S(2)}, u32[]{:S(2)}) collective-permute-start(f32[64,128]{1,0:T(8,128)S(1)} %chip_sum.1.rest_0_), channel_id=1, source_target_pairs={{0,4},{1,5},{2,6},{3,7},{4,0},{5,1},{6,2},{7,3},{8,12},{9,13},{10,... | collective-permute-start | bytes 98312 | tf_op jit(solution)/shard_map/ppermute | solution.py:319
  19.8 8.4 %collective-permute-start.9 = (bf16[2048,128]{1,0:T(8,128)(2,1)S(1)}, bf16[2048,128]{1,0:T(8,128)(2,1)S(1)}, u32[]{:S(2)}, u32[]{:S(2)}) collective-permute-start(bf16[2048,128]{1,0:T(8,128)(2,1)S(1)} %after.2), channel_id=1, source_target_pairs={{0,8},{8,0},{16,24},{24,16},{1,9},{9,1},{17,25},{25,17},{2,10},{10... | collective-permute-start | bytes 1572872 | tf_op jit(solution)/shard_map/ppermute | solution.py:311
  19.9 15.2 %collective-permute-start.13 = (bf16[2048,128]{1,0:T(8,128)(2,1)S(1)}, bf16[2048,128]{1,0:T(8,128)(2,1)S(1)}, u32[]{:S(2)}, u32[]{:S(2)}) collective-permute-start(bf16[2048,128]{1,0:T(8,128)(2,1)S(1)} %later.1), channel_id=1, source_target_pairs={{0,16},{8,24},{16,0},{24,8},{1,17},{9,25},{17,1},{25,9},{2,18},{10... | collective-permute-start | bytes 1572872 | tf_op jit(solution)/shard_map/ppermute | solution.py:311
  21.5 4.3 %collective-permute-start.6 = (f32[128,128]{1,0:T(8,128)S(1)}, f32[128,128]{1,0:T(8,128)S(1)}, u32[]{:S(2)}, u32[]{:S(2)}) collective-permute-start(f32[128,128]{1,0:T(8,128)S(1)} %get-tuple-element.23), channel_id=1, source_target_pairs={{0,1},{1,0},{2,3},{3,2},{4,5},{5,4},{6,7},{7,6},{8,9},{9,8},{10,11... | collective-permute-start | bytes 196616 | tf_op jit(solution)/shard_map/ppermute | solution.py:319
  22.0 4.8 %collective-permute-start.7 = (f32[128,128]{1,0:T(8,128)S(1)}, f32[128,128]{1,0:T(8,128)S(1)}, u32[]{:S(2)}, u32[]{:S(2)}) collective-permute-start(f32[128,128]{1,0:T(8,128)S(1)} %get-tuple-element.24), channel_id=1, source_target_pairs={{0,2},{1,3},{2,0},{3,1},{4,6},{5,7},{6,4},{7,5},{8,10},{9,11},{10,... | collective-permute-start | bytes 196616 | tf_op jit(solution)/shard_map/ppermute | solution.py:319
  22.8 5.4 %collective-permute-start.8 = (f32[128,128]{1,0:T(8,128)S(1)}, f32[128,128]{1,0:T(8,128)S(1)}, u32[]{:S(2)}, u32[]{:S(2)}) collective-permute-start(f32[128,128]{1,0:T(8,128)S(1)} %get-tuple-element.25), channel_id=1, source_target_pairs={{0,3},{1,2},{2,1},{3,0},{4,7},{5,6},{6,5},{7,4},{8,11},{9,10},{10,... | collective-permute-start | bytes 196616 | tf_op jit(solution)/shard_map/ppermute | solution.py:319
  28.8 9.1 %collective-permute-start.10 = (f32[128,128]{1,0:T(8,128)S(1)}, f32[128,128]{1,0:T(8,128)S(1)}, u32[]{:S(2)}, u32[]{:S(2)}) collective-permute-start(f32[128,128]{1,0:T(8,128)S(1)} %get-tuple-element.27), channel_id=1, source_target_pairs={{0,16},{1,17},{2,26},{3,27},{4,20},{5,21},{6,30},{7,31},{8,24},{9,... | collective-permute-start | bytes 196616 | tf_op jit(solution)/shard_map/ppermute | solution.py:319
  29.4 6.2 %collective-permute-start.12 = (f32[64,128]{1,0:T(8,128)S(1)}, f32[64,128]{1,0:T(8,128)S(1)}, u32[]{:S(2)}, u32[]{:S(2)}) collective-permute-start(f32[64,128]{1,0:T(8,128)S(1)} %get-tuple-element.26.total), channel_id=1, source_target_pairs={{0,20},{1,21},{2,30},{3,31},{4,16},{5,17},{6,26},{7,27},{8,28},{9,... | collective-permute-start | bytes 98312 | tf_op jit(solution)/shard_map/ppermute | solution.py:319
  32.7 5.2 %collective-permute-start.11 = (f32[64,128]{1,0:T(8,128)S(1)}, f32[64,128]{1,0:T(8,128)S(1)}, u32[]{:S(2)}, u32[]{:S(2)}) collective-permute-start(f32[64,128]{1,0:T(8,128)S(1)} %get-tuple-element.26.total), channel_id=1, source_target_pairs={{0,4},{1,5},{2,6},{3,7},{4,0},{5,1},{6,2},{7,3},{8,12},{9,13},{10,... | collective-permute-start | bytes 98312 | tf_op jit(solution)/shard_map/ppermute | solution.py:319
  37.9 9.3 %collective-permute-start.18 = (bf16[2048,128]{1,0:T(8,128)(2,1)S(1)}, bf16[2048,128]{1,0:T(8,128)(2,1)S(1)}, u32[]{:S(2)}, u32[]{:S(2)}) collective-permute-start(bf16[2048,128]{1,0:T(8,128)(2,1)S(1)} %after.3), channel_id=1, source_target_pairs={{0,8},{8,0},{16,24},{24,16},{1,9},{9,1},{17,25},{25,17},{2,10},{10... | collective-permute-start | bytes 1572872 | tf_op jit(solution)/shard_map/ppermute | solution.py:311
  38.0 5.9 %collective-permute-start.16 = (f32[128,128]{1,0:T(8,128)S(1)}, f32[128,128]{1,0:T(8,128)S(1)}, u32[]{:S(2)}, u32[]{:S(2)}) collective-permute-start(f32[128,128]{1,0:T(8,128)S(1)} %pair_sum.1.own.after), channel_id=1, source_target_pairs={{0,3},{1,2},{2,1},{3,0},{4,7},{5,6},{6,5},{7,4},{8,11},{9,10},{10,... | collective-permute-start | bytes 196616 | tf_op jit(solution)/shard_map/ppermute | solution.py:319
  39.3 4.6 %collective-permute-start.15 = (f32[128,128]{1,0:T(8,128)S(1)}, f32[128,128]{1,0:T(8,128)S(1)}, u32[]{:S(2)}, u32[]{:S(2)}) collective-permute-start(f32[128,128]{1,0:T(8,128)S(1)} %pair_sum.1.own.after), channel_id=1, source_target_pairs={{0,2},{1,3},{2,0},{3,1},{4,6},{5,7},{6,4},{7,5},{8,10},{9,11},{10,... | collective-permute-start | bytes 196616 | tf_op jit(solution)/shard_map/ppermute | solution.py:319
  40.0 4.8 %collective-permute-start.14 = (f32[128,128]{1,0:T(8,128)S(1)}, f32[128,128]{1,0:T(8,128)S(1)}, u32[]{:S(2)}, u32[]{:S(2)}) collective-permute-start(f32[128,128]{1,0:T(8,128)S(1)} %pair_sum.1.own.after), channel_id=1, source_target_pairs={{0,1},{1,0},{2,3},{3,2},{4,5},{5,4},{6,7},{7,6},{8,9},{9,8},{10,11... | collective-permute-start | bytes 196616 | tf_op jit(solution)/shard_map/ppermute | solution.py:319
  44.8 2.4 %copy-start.1 = (s32[8]{0:T(128)S(1)}, s32[8]{0:T(128)}, u32[]{:S(2)}) copy-start(s32[8]{0:T(128)} %active.1) | copy-start | bytes 100
  45.4 1.8 %collective-permute-start.17 = (f32[768,128]{1,0:T(8,128)S(1)}, f32[768,128]{1,0:T(8,128)S(1)}, u32[]{:S(2)}, u32[]{:S(2)}) collective-permute-start(f32[768,128]{1,0:T(8,128)S(1)} %join.1.joined_mine), channel_id=1, source_target_pairs={{0,8},{8,0},{16,24},{24,16},{1,9},{9,1},{17,25},{25,17},{2,10},{10... | collective-permute-start | bytes 1179656 | tf_op jit(solution)/shard_map/ppermute | solution.py:311

commit v4 on v3

--- a/solution.py
+++ b/solution.py
@@ -10,7 +10,6 @@
 ITERS = 5
 F32 = jnp.float32
 BF16 = jnp.bfloat16
-SMEM = pl.BlockSpec(memory_space=pltpu.SMEM)
 VMEM = pl.BlockSpec(memory_space=pltpu.VMEM)
 ANY = pl.BlockSpec(memory_space=pl.ANY)
 
@@ -23,22 +22,31 @@
     return lax.dot_general(left, right, (((0,), (0,)), ((), ())), preferred_element_type=F32)
 
 
-def call(kernel, out_shape, n_smem, n_args, flops, name, scratch=(), in_specs=None, out_specs=None, mib=12, aliases=None):
+def call(kernel, out_shape, n_args, flops, name, scratch=(), in_specs=None, out_specs=None, mib=12, aliases=None):
     return pl.pallas_call(
         kernel,
         out_shape=out_shape,
-        in_specs=in_specs or [SMEM] * n_smem + [VMEM] * n_args,
+        in_specs=in_specs or [VMEM] * n_args,
         out_specs=out_specs or jax.tree.map(lambda _: VMEM, out_shape),
         scratch_shapes=list(scratch),
         input_output_aliases=aliases or {},
         compiler_params=pltpu.CompilerParams(vmem_limit_bytes=mib * 2**20),
-        cost_estimate=pl.CostEstimate(flops=flops, bytes_accessed=2**20, transcendentals=0),
+        cost_estimate=pl.CostEstimate(flops=0, bytes_accessed=0, transcendentals=0),
         name=name,
     )
 
 
-def piece(place, step, size):
-    return pl.ds(pl.multiple_of(lax.bitwise_xor(place[2], jnp.int32(step)) * size, size), size)
+def chip_index():
+    return lax.axis_index("state") // 2
+
+
+def core_index():
+    return lax.axis_index("state") % 2
+
+
+def piece(step, size, base=0):
+    member = lax.bitwise_xor(lax.axis_index("row") % 4, jnp.int32(step))
+    return pl.ds(pl.multiple_of(base + member * size, size), size)
 
 
 def tree_sum(values):
@@ -47,22 +55,22 @@
     return values[0]
 
 
-def later_kernel(place, own, after, part, sem):
+def later_kernel(own, after, part, sem):
     del after
     size = part.shape[0]
-    copy = pltpu.make_async_copy(own.at[pl.ds(pl.multiple_of(place[0] * size, size), size), :], part, sem)
+    copy = pltpu.make_async_copy(own.at[pl.ds(pl.multiple_of(chip_index() * size, size), size), :], part, sem)
     copy.start()
     copy.wait()
 
 
-def chip_gram_kernel(place, own, mate, keep, send1, send2, send3, slab):
-    core = place[1]
+def chip_gram_kernel(own, mate, keep, send1, send2, send3, slab):
+    core = core_index()
     width = own.shape[1]
     size = keep.shape[0]
     slab[pl.ds(pl.multiple_of(core * width, width), width), :] = cross(own[...], own[...])
     slab[pl.ds(pl.multiple_of((1 - core) * width, width), width), :] = cross(own[...], mate[...])
     for step, out in enumerate((keep, send1, send2, send3)):
-        out[...] = slab[piece(place, step, size), :]
+        out[...] = slab[piece(step, size), :]
 
 
 def chip_sum_kernel(keep, part1, part2, part3, later, total):
@@ -70,9 +78,9 @@
     total[...] = tree_sum([keep[...], part1[...], part2[...], part3[...]])
 
 
-def pair_gram_kernel(place, own, mate, across, *rest):
+def pair_gram_kernel(own, mate, across, *rest):
     chip_parts, (chip_piece, keep, send1, send2, send3, slab) = rest[:-6], rest[-6:]
-    chip = place[0]
+    chip = chip_index()
     half, width = across.shape
     size = keep.shape[0]
     rows = pl.ds(pl.multiple_of(chip * half, half), half)
@@ -82,9 +90,9 @@
     slab[width : 2 * width, :] = jnp.where(chip == 0, other.T, other)
     chip_sum = tree_sum([part[...] for part in chip_parts])
     chip_piece[...] = chip_sum
-    keep[...] = slab[piece(place, 0, size), :]
+    keep[...] = slab[piece(0, size), :]
     for step, out in enumerate((send1, send2, send3)):
-        out[0:size, :] = slab[piece(place, step + 1, size), :]
+        out[0:size, :] = slab[piece(step + 1, size), :]
         out[size : 2 * size, :] = chip_sum
 
 
@@ -92,7 +100,7 @@
     del value, after, same
 
 
-def group_sum_kernel(place, keep, chip_piece, part1, part2, part3, mate1, total, payload, chip_slab):
+def group_sum_kernel(keep, chip_piece, part1, part2, part3, mate1, total, payload, chip_slab):
     del mate1
     size = keep.shape[0]
     parts = (part1, part2, part3)
@@ -100,9 +108,9 @@
     total[...] = group_sum
     payload[0:size, :] = group_sum
     payload[size : 2 * size, :] = chip_piece[...]
-    chip_slab[piece(place, 0, size), :] = chip_piece[...]
+    chip_slab[piece(0, size), :] = chip_piece[...]
     for step, part in enumerate(parts):
-        chip_slab[piece(place, step + 1, size), :] = part[size : 2 * size, :]
+        chip_slab[piece(step + 1, size), :] = part[size : 2 * size, :]
 
 
 def pair_sum_kernel(total, across, *rest):
@@ -112,12 +120,11 @@
     payload[size : 2 * size, :] = across[size : 2 * size, :]
 
 
-def join_kernel(place, own, part1, part2, part3, chip_mine, joined):
+def join_kernel(own, part1, part2, part3, chip_mine, joined):
     size = own.shape[0] // 2
     for step, part in enumerate((own, part1, part2, part3)):
-        joined[piece(place, step, size), :] = part[0:size, :]
-        start = pl.multiple_of(8 * size + lax.bitwise_xor(place[2], jnp.int32(step)) * size, size)
-        joined[pl.ds(start, size), :] = part[size : 2 * size, :]
+        joined[piece(step, size), :] = part[0:size, :]
+        joined[piece(step, size, 8 * size), :] = part[size : 2 * size, :]
     joined[4 * size : 8 * size, :] = chip_mine[...]
 
 
@@ -162,10 +169,10 @@
 
 
 def finish_kernel(
-    total_rows, place, active, joined_mine, joined_mate, own, mate, across1, mate1, across2, mate2,
+    total_rows, active, joined_mine, joined_mate, own, mate, across1, mate1, across2, mate2,
     out, gram, highs, lows, factor, left, result, state_flags, sems, out_sems,
 ):
-    chip, core = place[0], place[1]
+    chip, core = chip_index(), core_index()
     half, width = across1.shape
     cols = gram.shape[0]
     near, far = pl.multiple_of(chip * half, half), pl.multiple_of((1 - chip) * half, half)
@@ -300,9 +307,7 @@
     row_devices = lax.axis_size("row")
     total_rows = rows * row_devices
     cols = width * lax.axis_size("state")
-    state, row = lax.axis_index("state"), lax.axis_index("row")
-    chip, core = state // 2, state % 2
-    place = jnp.stack([chip, core, row % 4]).astype(jnp.int32)
+    chip = chip_index()
     size = width // 2
     shape = jax.ShapeDtypeStruct
     small, slab = shape((size, width), F32), shape((2 * width, width), F32)
@@ -320,48 +325,47 @@
 
     def after(value, other):
         return call(
-            pass_kernel, shape(value.shape, value.dtype), 0, 0, 0, "after", in_specs=[ANY, ANY], out_specs=ANY,
+            pass_kernel, shape(value.shape, value.dtype), 0, 0, "after", in_specs=[ANY, ANY], out_specs=ANY,
             aliases={0: 0},
         )(value, other)
 
     across1 = swap(lax.dynamic_slice_in_dim(vectors, (1 - chip) * half, half, 0), 2)
     mate = swap(vectors, 1)
     keep, *sends = call(
-        chip_gram_kernel, (small,) * 4, 1, 2, 4 * rows * width * width, "chip_gram", scratch=[pltpu.VMEM(slab.shape, F32)]
-    )(place, vectors, mate)
+        chip_gram_kernel, (small,) * 4, 2, 4 * rows * width * width, "chip_gram", scratch=[pltpu.VMEM(slab.shape, F32)]
+    )(vectors, mate)
     later = call(
-        later_kernel, shape((half, width), BF16), 1, 0, 0, "later", scratch=[pltpu.SemaphoreType.DMA],
-        in_specs=[SMEM, ANY, ANY], out_specs=ANY,
-    )(place, vectors, keep)
+        later_kernel, shape((half, width), BF16), 0, 0, "later", scratch=[pltpu.SemaphoreType.DMA],
+        in_specs=[ANY, ANY], out_specs=ANY,
+    )(vectors, keep)
     across2 = swap(later, 2)
 
     groups = [4 * index for index in range(row_devices // 4)]
     parts = [move(send, step + 1) for step, send in enumerate(sends)]
-    chip_sum = call(chip_sum_kernel, small, 0, 4, 0, "chip_sum", in_specs=[VMEM] * 4 + [ANY])(keep, *parts, later)
+    chip_sum = call(chip_sum_kernel, small, 4, 0, "chip_sum", in_specs=[VMEM] * 4 + [ANY])(keep, *parts, later)
     chip_parts = [chip_sum] + [move(chip_sum, bits) for bits in groups[1:]]
     double = shape((2 * size, width), F32)
     chip_piece, keep, *sends = call(
-        pair_gram_kernel, (small, small, double, double, double), 1, 3 + len(chip_parts), 4 * half * width * width,
+        pair_gram_kernel, (small, small, double, double, double), 3 + len(chip_parts), 4 * half * width * width,
         "pair_gram", scratch=[pltpu.VMEM(slab.shape, F32)],
-    )(place, vectors, mate, across1, *chip_parts)
+    )(vectors, mate, across1, *chip_parts)
     parts = [move(send, step + 1) for step, send in enumerate(sends)]
     mate1 = swap(after(across1, chip_piece), 1)
     pair_sum, payload, chip_mine = call(
-        group_sum_kernel, (small, double, slab), 0, 0, 0, "group_sum", in_specs=[SMEM] + [VMEM] * 5 + [ANY]
-    )(place, keep, chip_piece, *parts, mate1)
+        group_sum_kernel, (small, double, slab), 0, 0, "group_sum", in_specs=[VMEM] * 5 + [ANY]
+    )(keep, chip_piece, *parts, mate1)
     pair_parts = [move(payload, 0, 1)] + [move(pair_sum, bits, chips) for bits in groups[1:] for chips in range(2)]
     payload = call(
-        pair_sum_kernel, double, 0, 0, 0, "pair_sum", in_specs=[VMEM] * (1 + len(pair_parts)) + [ANY]
+        pair_sum_kernel, double, 0, 0, "pair_sum", in_specs=[VMEM] * (1 + len(pair_parts)) + [ANY]
     )(pair_sum, *pair_parts, across2)
     parts = [move(payload, step) for step in (1, 2, 3)]
     mate2 = swap(after(across2, payload), 1)
-    joined_mine = call(join_kernel, shape((6 * width, width), F32), 1, 5, 0, "join")(place, payload, *parts, chip_mine)
+    joined_mine = call(join_kernel, shape((6 * width, width), F32), 5, 0, "join")(payload, *parts, chip_mine)
     joined_mate = swap(joined_mine, 1)
 
     return call(
         functools.partial(finish_kernel, float(total_rows)),
         shape((rows, width), BF16),
-        0,
         0,
         12 * cols**3 * 3 + 2 * rows * cols * width,
         "finish",
@@ -376,11 +380,11 @@
             pltpu.SemaphoreType.DMA((7,)),
             pltpu.SemaphoreType.DMA((4,)),
         ],
-        in_specs=[SMEM, ANY, VMEM, VMEM] + [ANY] * 6,
+        in_specs=[ANY, VMEM, VMEM] + [ANY] * 6,
         out_specs=ANY,
         mib=24,
     )(
-        place, active, joined_mine, joined_mate, vectors, mate, across1, mate1, across2, mate2
+        active, joined_mine, joined_mate, vectors, mate, across1, mate1, across2, mate2
     )
 
 

time: 58.1 us -> 55.6 us (0.957)
  Pallas kernels: 14.9 us -> 11.7 us
  waiting for transfers between devices: 19.1 us -> 19.9 us
    pallas_call x9, Pallas kernels: 4.14 us -> 1.45 us  [the longest x1 0.76 us: shards(): call(chip_gram_kernel, (small,) * 4, 2, 4 * rows * width * width, 'chip_g...]
    ppermute x6, waiting for transfers between devices: 3.97 us -> 5.01 us  [swap(): lax.ppermute(value, 'state', [(index, index ^ bit) for index in range(4)])]
  transfers between devices with their start and end apart: 19 -> 19, of which waited for: 13 -> 13; matrix products, arithmetic and copies ran while one was open for 2% -> 2% of each run, Pallas kernels for 5% -> 2%
where the time goes in v4:
time: 55.6 us; the launch traced here: 55.5 us
  starting transfers between devices  22.6 us (41%)
  waiting for transfers between devices  19.9 us (36%)
  Pallas kernels  11.7 us (21%)
  local copies, waits for them, and re-layouts  1.15 us (2%)
    ppermute x13, starting transfers between devices, move(): return lax.ppermute(value, ('state', 'row'), pairs)  17.7 us
    ppermute x13, waiting for transfers between devices, move(): return lax.ppermute(value, ('state', 'row'), pairs)  14.9 us
    pallas_call x1, Pallas kernels, shards(): call(functools.partial(finish_kernel, float(total_rows)), shape((rows, wi...  10.3 us
    ppermute x6, waiting for transfers between devices, swap(): lax.ppermute(value, 'state', [(index, index ^ bit) for index in range(4)])  5.01 us
    ppermute x6, starting transfers between devices, swap(): lax.ppermute(value, 'state', [(index, index ^ bit) for index in range(4)])  4.87 us
  transfers between devices with their start and end apart: 19, of which 13 were waited for; matrix products, arithmetic and copies ran while one was open for 2% of the time, Pallas kernels for 2%

profile of v4, /device:TPU:0, one launch (start us, length us, event | category | flops | bytes accessed | tf_op | source)
XLA Modules:
  0.0 55.5 jit_solution(8230228677561330944)
XLA Ops:
  0.0 0.0 copy-start
  0.0 0.5 collective-permute-start
  0.5 1.1 %constant_dynamic-slice_fusion = bf16[2048,128]{1,0:T(8,128)(2,1)S(1)} fusion(bf16[4096,128]{1,0:T(8,128)(2,1)} %own.7, s32[]{:T(128)S(6)} %select_n.9), kind=kLoop, calls=%fused_computation | loop fusion | bytes 1048580 | tf_op jit(solution)/shard_map/dynamic_slice | solution.py:332
  1.5 2.6 %collective-permute-start.1 = (bf16[2048,128]{1,0:T(8,128)(2,1)S(1)}, bf16[2048,128]{1,0:T(8,128)(2,1)S(1)}, u32[]{:S(2)}, u32[]{:S(2)}) collective-permute-start(bf16[2048,128]{1,0:T(8,128)(2,1)S(1)} %constant_dynamic-slice_fusion), channel_id=1, source_target_pairs={{0,16},{8,24},{16,0},{24,8},{1,17},{9,25},{17,1},{25,9},{2,18},{10... | collective-permute-start | bytes 1572872 | tf_op jit(solution)/shard_map/ppermute | solution.py:316
  4.2 0.0 collective-permute-done.mate
  4.2 0.0 copy-done
  4.2 0.8 %chip_gram.1 = (f32[64,128]{1,0:T(8,128)S(1)}, f32[64,128]{1,0:T(8,128)S(1)}, f32[64,128]{1,0:T(8,128)S(1)}, f32[64,128]{1,0:T(8,128)S(1)}) custom-call(bf16[4096,128]{1,0:T(8,128)(2,1)S(1)} %copy-done, bf16[4096,128]{1,0:T(8,128)(2,1)S(1)} %collective-permute-done.mate), custom_call_target="tpu_custom_call" | custom-call | tf_op jit(solution)/shard_map/chip_gram/pallas_call | solution.py:334
  4.9 1.7 %collective-permute-start.2 = (f32[64,128]{1,0:T(8,128)S(1)}, f32[64,128]{1,0:T(8,128)S(1)}, u32[]{:S(2)}, u32[]{:S(2)}) collective-permute-start(f32[64,128]{1,0:T(8,128)S(1)} %get-tuple-element.18), channel_id=1, source_target_pairs={{0,1},{1,0},{2,3},{3,2},{4,5},{5,4},{6,7},{7,6},{8,9},{9,8},{10,11... | collective-permute-start | bytes 98312 | tf_op jit(solution)/shard_map/ppermute | solution.py:324
  6.7 1.6 %collective-permute-start.3 = (f32[64,128]{1,0:T(8,128)S(1)}, f32[64,128]{1,0:T(8,128)S(1)}, u32[]{:S(2)}, u32[]{:S(2)}) collective-permute-start(f32[64,128]{1,0:T(8,128)S(1)} %get-tuple-element.19), channel_id=1, source_target_pairs={{0,2},{1,3},{2,0},{3,1},{4,6},{5,7},{6,4},{7,5},{8,10},{9,11},{10,... | collective-permute-start | bytes 98312 | tf_op jit(solution)/shard_map/ppermute | solution.py:324
  8.3 0.3 collective-permute-start.4
  8.6 0.4 collective-permute-done.2.part1
  8.9 1.9 %collective-permute-done.3.part2 = f32[64,128]{1,0:T(8,128)S(1)} collective-permute-done((f32[64,128]{1,0:T(8,128)S(1)}, f32[64,128]{1,0:T(8,128)S(1)}, u32[]{:S(2)}, u32[]{:S(2)}) %collective-permute-start.3) | collective-permute-done | bytes 32800 | tf_op jit(solution)/shard_map/ppermute | solution.py:324
  10.8 2.3 %collective-permute-done.4.part3 = f32[64,128]{1,0:T(8,128)S(1)} collective-permute-done((f32[64,128]{1,0:T(8,128)S(1)}, f32[64,128]{1,0:T(8,128)S(1)}, u32[]{:S(2)}, u32[]{:S(2)}) %collective-permute-start.4) | collective-permute-done | bytes 32800 | tf_op jit(solution)/shard_map/ppermute | solution.py:324
  13.1 2.7 %collective-permute-start.5 = (f32[64,128]{1,0:T(8,128)S(1)}, f32[64,128]{1,0:T(8,128)S(1)}, u32[]{:S(2)}, u32[]{:S(2)}) collective-permute-start(f32[64,128]{1,0:T(8,128)S(1)} %chip_sum.1.rest_0_), channel_id=1, source_target_pairs={{0,4},{1,5},{2,6},{3,7},{4,0},{5,1},{6,2},{7,3},{8,12},{9,13},{10,... | collective-permute-start | bytes 98312 | tf_op jit(solution)/shard_map/ppermute | solution.py:324
  15.7 1.0 %collective-permute-done.1.across.across1 = bf16[2048,128]{1,0:T(8,128)(2,1)S(1)} collective-permute-done((bf16[2048,128]{1,0:T(8,128)(2,1)S(1)}, bf16[2048,128]{1,0:T(8,128)(2,1)S(1)}, u32[]{:S(2)}, u32[]{:S(2)}) %collective-permute-start.1) | collective-permute-done | bytes 524320 | tf_op jit(solution)/shard_map/ppermute | solution.py:316
  16.7 1.5 %collective-permute-done.5.rest_1_ = f32[64,128]{1,0:T(8,128)S(1)} collective-permute-done((f32[64,128]{1,0:T(8,128)S(1)}, f32[64,128]{1,0:T(8,128)S(1)}, u32[]{:S(2)}, u32[]{:S(2)}) %collective-permute-start.5) | collective-permute-done | bytes 32800 | tf_op jit(solution)/shard_map/ppermute | solution.py:324
  18.2 0.6 %pair_gram.1 = (f32[64,128]{1,0:T(8,128)S(1)}, f32[64,128]{1,0:T(8,128)S(1)}, f32[128,128]{1,0:T(8,128)S(1)}, f32[128,128]{1,0:T(8,128)S(1)}, f32[128,128]{1,0:T(8,128)S(1)}) custom-call(bf16[4096,128]{1,0:T(8,128)(2,1)S(1)} %copy-done, bf16[4096,128]{1,0:T(8,128)(2,1)S(1)} %collective-permute-done.mate, ...), custom_call_target="tpu_custom_call" | custom-call | tf_op jit(solution)/shard_map/pair_gram/pallas_call | solution.py:348
  18.8 0.1 collective-permute-start.9
  18.8 1.6 %collective-permute-start.13 = (bf16[2048,128]{1,0:T(8,128)(2,1)S(1)}, bf16[2048,128]{1,0:T(8,128)(2,1)S(1)}, u32[]{:S(2)}, u32[]{:S(2)}) collective-permute-start(bf16[2048,128]{1,0:T(8,128)(2,1)S(1)} %later.1), channel_id=1, source_target_pairs={{0,16},{8,24},{16,0},{24,8},{1,17},{9,25},{17,1},{25,9},{2,18},{10... | collective-permute-start | bytes 1572872 | tf_op jit(solution)/shard_map/ppermute | solution.py:316
  20.4 0.5 collective-permute-start.6
  20.9 1.4 %collective-permute-start.7 = (f32[128,128]{1,0:T(8,128)S(1)}, f32[128,128]{1,0:T(8,128)S(1)}, u32[]{:S(2)}, u32[]{:S(2)}) collective-permute-start(f32[128,128]{1,0:T(8,128)S(1)} %get-tuple-element.24), channel_id=1, source_target_pairs={{0,2},{1,3},{2,0},{3,1},{4,6},{5,7},{6,4},{7,5},{8,10},{9,11},{10,... | collective-permute-start | bytes 196616 | tf_op jit(solution)/shard_map/ppermute | solution.py:324
  22.3 1.6 %collective-permute-start.8 = (f32[128,128]{1,0:T(8,128)S(1)}, f32[128,128]{1,0:T(8,128)S(1)}, u32[]{:S(2)}, u32[]{:S(2)}) collective-permute-start(f32[128,128]{1,0:T(8,128)S(1)} %get-tuple-element.25), channel_id=1, source_target_pairs={{0,3},{1,2},{2,1},{3,0},{4,7},{5,6},{6,5},{7,4},{8,11},{9,10},{10,... | collective-permute-start | bytes 196616 | tf_op jit(solution)/shard_map/ppermute | solution.py:324
  23.9 0.8 %collective-permute-done.6.part1 = f32[128,128]{1,0:T(8,128)S(1)} collective-permute-done((f32[128,128]{1,0:T(8,128)S(1)}, f32[128,128]{1,0:T(8,128)S(1)}, u32[]{:S(2)}, u32[]{:S(2)}) %collective-permute-start.6) | collective-permute-done | bytes 65568 | tf_op jit(solution)/shard_map/ppermute | solution.py:324
  24.7 1.2 %collective-permute-done.7.part2 = f32[128,128]{1,0:T(8,128)S(1)} collective-permute-done((f32[128,128]{1,0:T(8,128)S(1)}, f32[128,128]{1,0:T(8,128)S(1)}, u32[]{:S(2)}, u32[]{:S(2)}) %collective-permute-start.7) | collective-permute-done | bytes 65568 | tf_op jit(solution)/shard_map/ppermute | solution.py:324
  25.8 1.7 %collective-permute-done.8.part3 = f32[128,128]{1,0:T(8,128)S(1)} collective-permute-done((f32[128,128]{1,0:T(8,128)S(1)}, f32[128,128]{1,0:T(8,128)S(1)}, u32[]{:S(2)}, u32[]{:S(2)}) %collective-permute-start.8) | collective-permute-done | bytes 65568 | tf_op jit(solution)/shard_map/ppermute | solution.py:324
  27.5 0.0 collective-permute-done.9.mate1
  27.5 0.6 %collective-permute-start.10 = (f32[128,128]{1,0:T(8,128)S(1)}, f32[128,128]{1,0:T(8,128)S(1)}, u32[]{:S(2)}, u32[]{:S(2)}) collective-permute-start(f32[128,128]{1,0:T(8,128)S(1)} %get-tuple-element.27), channel_id=1, source_target_pairs={{0,16},{1,17},{2,26},{3,27},{4,20},{5,21},{6,30},{7,31},{8,24},{9,... | collective-permute-start | bytes 196616 | tf_op jit(solution)/shard_map/ppermute | solution.py:324
  28.1 3.5 %collective-permute-start.12 = (f32[64,128]{1,0:T(8,128)S(1)}, f32[64,128]{1,0:T(8,128)S(1)}, u32[]{:S(2)}, u32[]{:S(2)}) collective-permute-start(f32[64,128]{1,0:T(8,128)S(1)} %get-tuple-element.26.total), channel_id=1, source_target_pairs={{0,20},{1,21},{2,30},{3,31},{4,16},{5,17},{6,26},{7,27},{8,28},{9,... | collective-permute-start | bytes 98312 | tf_op jit(solution)/shard_map/ppermute | solution.py:324
  31.6 0.4 collective-permute-start.11
  32.0 2.3 %collective-permute-done.13.rest_2_.across2 = bf16[2048,128]{1,0:T(8,128)(2,1)S(1)} collective-permute-done((bf16[2048,128]{1,0:T(8,128)(2,1)S(1)}, bf16[2048,128]{1,0:T(8,128)(2,1)S(1)}, u32[]{:S(2)}, u32[]{:S(2)}) %collective-permute-start.13) | collective-permute-done | bytes 524320 | tf_op jit(solution)/shard_map/ppermute | solution.py:316
  34.4 0.0 collective-permute-done.12.rest_1_
  34.4 2.0 %collective-permute-done.11.rest_0_ = f32[64,128]{1,0:T(8,128)S(1)} collective-permute-done((f32[64,128]{1,0:T(8,128)S(1)}, f32[64,128]{1,0:T(8,128)S(1)}, u32[]{:S(2)}, u32[]{:S(2)}) %collective-permute-start.11) | collective-permute-done | bytes 32800 | tf_op jit(solution)/shard_map/ppermute | solution.py:324
  36.4 0.0 collective-permute-done.10.across
  36.5 0.1 collective-permute-start.18
  36.5 1.2 %collective-permute-start.16 = (f32[128,128]{1,0:T(8,128)S(1)}, f32[128,128]{1,0:T(8,128)S(1)}, u32[]{:S(2)}, u32[]{:S(2)}) collective-permute-start(f32[128,128]{1,0:T(8,128)S(1)} %pair_sum.1.own.after), channel_id=1, source_target_pairs={{0,3},{1,2},{2,1},{3,0},{4,7},{5,6},{6,5},{7,4},{8,11},{9,10},{10,... | collective-permute-start | bytes 196616 | tf_op jit(solution)/shard_map/ppermute | solution.py:324
  37.7 0.9 %collective-permute-start.15 = (f32[128,128]{1,0:T(8,128)S(1)}, f32[128,128]{1,0:T(8,128)S(1)}, u32[]{:S(2)}, u32[]{:S(2)}) collective-permute-start(f32[128,128]{1,0:T(8,128)S(1)} %pair_sum.1.own.after), channel_id=1, source_target_pairs={{0,2},{1,3},{2,0},{3,1},{4,6},{5,7},{6,4},{7,5},{8,10},{9,11},{10,... | collective-permute-start | bytes 196616 | tf_op jit(solution)/shard_map/ppermute | solution.py:324
  38.6 1.5 %collective-permute-start.14 = (f32[128,128]{1,0:T(8,128)S(1)}, f32[128,128]{1,0:T(8,128)S(1)}, u32[]{:S(2)}, u32[]{:S(2)}) collective-permute-start(f32[128,128]{1,0:T(8,128)S(1)} %pair_sum.1.own.after), channel_id=1, source_target_pairs={{0,1},{1,0},{2,3},{3,2},{4,5},{5,4},{6,7},{7,6},{8,9},{9,8},{10,11... | collective-permute-start | bytes 196616 | tf_op jit(solution)/shard_map/ppermute | solution.py:324
  40.1 2.3 %collective-permute-done.16.part3 = f32[128,128]{1,0:T(8,128)S(1)} collective-permute-done((f32[128,128]{1,0:T(8,128)S(1)}, f32[128,128]{1,0:T(8,128)S(1)}, u32[]{:S(2)}, u32[]{:S(2)}) %collective-permute-start.16) | collective-permute-done | bytes 65568 | tf_op jit(solution)/shard_map/ppermute | solution.py:324
  42.4 0.0 collective-permute-done.15.part2
  42.4 1.0 %collective-permute-done.14.part1 = f32[128,128]{1,0:T(8,128)S(1)} collective-permute-done((f32[128,128]{1,0:T(8,128)S(1)}, f32[128,128]{1,0:T(8,128)S(1)}, u32[]{:S(2)}, u32[]{:S(2)}) %collective-permute-start.14) | collective-permute-done | bytes 65568 | tf_op jit(solution)/shard_map/ppermute | solution.py:324
  43.4 0.0 copy-start.1
  43.4 0.1 collective-permute-start.17
  43.5 1.7 %collective-permute-done.17.joined_mate = f32[768,128]{1,0:T(8,128)S(1)} collective-permute-done((f32[768,128]{1,0:T(8,128)S(1)}, f32[768,128]{1,0:T(8,128)S(1)}, u32[]{:S(2)}, u32[]{:S(2)}) %collective-permute-start.17) | collective-permute-done | bytes 393248 | tf_op jit(solution)/shard_map/ppermute | solution.py:316
  45.2 0.0 collective-permute-done.18.mate2
  45.2 0.0 copy-done.1
  45.2 10.3 %finish.1 = bf16[4096,128]{1,0:T(8,128)(2,1)} custom-call(s32[8]{0:T(128)S(1)} %copy-done.1, f32[768,128]{1,0:T(8,128)S(1)} %join.1.joined_mine, f32[768,128]{1,0:T(8,128)S(1)} %collective-permute-done.17.joined_mate, bf16[4096,128]{1,0:T(8,128)(2,1)S(1)} %copy-done, bf16[4096,128]{1,0:T(8,128)(2,1)S(1)} %collective-permute-done.mate, ...), custom_call_target="tpu_custom_call" | custom-call | tf_op jit(solution)/shard_map/finish/pallas_call | solution.py:366
  (9 shorter events, 0.2 us)
Async XLA Ops:
  0.0 4.2 %copy-start = (bf16[4096,128]{1,0:T(8,128)(2,1)S(1)}, bf16[4096,128]{1,0:T(8,128)(2,1)}, u32[]{:S(2)}) copy-start(bf16[4096,128]{1,0:T(8,128)(2,1)} %own.7) | copy-start | bytes 3145732
  0.0 4.2 %collective-permute-start = (bf16[4096,128]{1,0:T(8,128)(2,1)}, bf16[4096,128]{1,0:T(8,128)(2,1)S(1)}, u32[]{:S(2)}, u32[]{:S(2)}) collective-permute-start(bf16[4096,128]{1,0:T(8,128)(2,1)} %own.7), channel_id=1, source_target_pairs={{0,8},{8,0},{16,24},{24,16},{1,9},{9,1},{17,25},{25,17},{2,10},{10... | collective-permute-start | bytes 3145736 | tf_op jit(solution)/shard_map/ppermute | solution.py:316
  1.5 15.2 %collective-permute-start.1 = (bf16[2048,128]{1,0:T(8,128)(2,1)S(1)}, bf16[2048,128]{1,0:T(8,128)(2,1)S(1)}, u32[]{:S(2)}, u32[]{:S(2)}) collective-permute-start(bf16[2048,128]{1,0:T(8,128)(2,1)S(1)} %constant_dynamic-slice_fusion), channel_id=1, source_target_pairs={{0,16},{8,24},{16,0},{24,8},{1,17},{9,25},{17,1},{25,9},{2,18},{10... | collective-permute-start | bytes 1572872 | tf_op jit(solution)/shard_map/ppermute | solution.py:316
  4.9 4.0 %collective-permute-start.2 = (f32[64,128]{1,0:T(8,128)S(1)}, f32[64,128]{1,0:T(8,128)S(1)}, u32[]{:S(2)}, u32[]{:S(2)}) collective-permute-start(f32[64,128]{1,0:T(8,128)S(1)} %get-tuple-element.18), channel_id=1, source_target_pairs={{0,1},{1,0},{2,3},{3,2},{4,5},{5,4},{6,7},{7,6},{8,9},{9,8},{10,11... | collective-permute-start | bytes 98312 | tf_op jit(solution)/shard_map/ppermute | solution.py:324
  6.7 4.1 %collective-permute-start.3 = (f32[64,128]{1,0:T(8,128)S(1)}, f32[64,128]{1,0:T(8,128)S(1)}, u32[]{:S(2)}, u32[]{:S(2)}) collective-permute-start(f32[64,128]{1,0:T(8,128)S(1)} %get-tuple-element.19), channel_id=1, source_target_pairs={{0,2},{1,3},{2,0},{3,1},{4,6},{5,7},{6,4},{7,5},{8,10},{9,11},{10,... | collective-permute-start | bytes 98312 | tf_op jit(solution)/shard_map/ppermute | solution.py:324
  8.3 4.8 %collective-permute-start.4 = (f32[64,128]{1,0:T(8,128)S(1)}, f32[64,128]{1,0:T(8,128)S(1)}, u32[]{:S(2)}, u32[]{:S(2)}) collective-permute-start(f32[64,128]{1,0:T(8,128)S(1)} %get-tuple-element.20), channel_id=1, source_target_pairs={{0,3},{1,2},{2,1},{3,0},{4,7},{5,6},{6,5},{7,4},{8,11},{9,10},{10,... | collective-permute-start | bytes 98312 | tf_op jit(solution)/shard_map/ppermute | solution.py:324
  13.1 5.1 %collective-permute-start.5 = (f32[64,128]{1,0:T(8,128)S(1)}, f32[64,128]{1,0:T(8,128)S(1)}, u32[]{:S(2)}, u32[]{:S(2)}) collective-permute-start(f32[64,128]{1,0:T(8,128)S(1)} %chip_sum.1.rest_0_), channel_id=1, source_target_pairs={{0,4},{1,5},{2,6},{3,7},{4,0},{5,1},{6,2},{7,3},{8,12},{9,13},{10,... | collective-permute-start | bytes 98312 | tf_op jit(solution)/shard_map/ppermute | solution.py:324
  18.8 8.7 %collective-permute-start.9 = (bf16[2048,128]{1,0:T(8,128)(2,1)S(1)}, bf16[2048,128]{1,0:T(8,128)(2,1)S(1)}, u32[]{:S(2)}, u32[]{:S(2)}) collective-permute-start(bf16[2048,128]{1,0:T(8,128)(2,1)S(1)} %after.2), channel_id=1, source_target_pairs={{0,8},{8,0},{16,24},{24,16},{1,9},{9,1},{17,25},{25,17},{2,10},{10... | collective-permute-start | bytes 1572872 | tf_op jit(solution)/shard_map/ppermute | solution.py:316
  18.8 15.5 %collective-permute-start.13 = (bf16[2048,128]{1,0:T(8,128)(2,1)S(1)}, bf16[2048,128]{1,0:T(8,128)(2,1)S(1)}, u32[]{:S(2)}, u32[]{:S(2)}) collective-permute-start(bf16[2048,128]{1,0:T(8,128)(2,1)S(1)} %later.1), channel_id=1, source_target_pairs={{0,16},{8,24},{16,0},{24,8},{1,17},{9,25},{17,1},{25,9},{2,18},{10... | collective-permute-start | bytes 1572872 | tf_op jit(solution)/shard_map/ppermute | solution.py:316
  20.4 4.3 %collective-permute-start.6 = (f32[128,128]{1,0:T(8,128)S(1)}, f32[128,128]{1,0:T(8,128)S(1)}, u32[]{:S(2)}, u32[]{:S(2)}) collective-permute-start(f32[128,128]{1,0:T(8,128)S(1)} %get-tuple-element.23), channel_id=1, source_target_pairs={{0,1},{1,0},{2,3},{3,2},{4,5},{5,4},{6,7},{7,6},{8,9},{9,8},{10,11... | collective-permute-start | bytes 196616 | tf_op jit(solution)/shard_map/ppermute | solution.py:324
  20.9 4.9 %collective-permute-start.7 = (f32[128,128]{1,0:T(8,128)S(1)}, f32[128,128]{1,0:T(8,128)S(1)}, u32[]{:S(2)}, u32[]{:S(2)}) collective-permute-start(f32[128,128]{1,0:T(8,128)S(1)} %get-tuple-element.24), channel_id=1, source_target_pairs={{0,2},{1,3},{2,0},{3,1},{4,6},{5,7},{6,4},{7,5},{8,10},{9,11},{10,... | collective-permute-start | bytes 196616 | tf_op jit(solution)/shard_map/ppermute | solution.py:324
  22.3 5.2 %collective-permute-start.8 = (f32[128,128]{1,0:T(8,128)S(1)}, f32[128,128]{1,0:T(8,128)S(1)}, u32[]{:S(2)}, u32[]{:S(2)}) collective-permute-start(f32[128,128]{1,0:T(8,128)S(1)} %get-tuple-element.25), channel_id=1, source_target_pairs={{0,3},{1,2},{2,1},{3,0},{4,7},{5,6},{6,5},{7,4},{8,11},{9,10},{10,... | collective-permute-start | bytes 196616 | tf_op jit(solution)/shard_map/ppermute | solution.py:324
  27.5 8.9 %collective-permute-start.10 = (f32[128,128]{1,0:T(8,128)S(1)}, f32[128,128]{1,0:T(8,128)S(1)}, u32[]{:S(2)}, u32[]{:S(2)}) collective-permute-start(f32[128,128]{1,0:T(8,128)S(1)} %get-tuple-element.27), channel_id=1, source_target_pairs={{0,16},{1,17},{2,26},{3,27},{4,20},{5,21},{6,30},{7,31},{8,24},{9,... | collective-permute-start | bytes 196616 | tf_op jit(solution)/shard_map/ppermute | solution.py:324
  28.1 6.2 %collective-permute-start.12 = (f32[64,128]{1,0:T(8,128)S(1)}, f32[64,128]{1,0:T(8,128)S(1)}, u32[]{:S(2)}, u32[]{:S(2)}) collective-permute-start(f32[64,128]{1,0:T(8,128)S(1)} %get-tuple-element.26.total), channel_id=1, source_target_pairs={{0,20},{1,21},{2,30},{3,31},{4,16},{5,17},{6,26},{7,27},{8,28},{9,... | collective-permute-start | bytes 98312 | tf_op jit(solution)/shard_map/ppermute | solution.py:324
  31.6 4.8 %collective-permute-start.11 = (f32[64,128]{1,0:T(8,128)S(1)}, f32[64,128]{1,0:T(8,128)S(1)}, u32[]{:S(2)}, u32[]{:S(2)}) collective-permute-start(f32[64,128]{1,0:T(8,128)S(1)} %get-tuple-element.26.total), channel_id=1, source_target_pairs={{0,4},{1,5},{2,6},{3,7},{4,0},{5,1},{6,2},{7,3},{8,12},{9,13},{10,... | collective-permute-start | bytes 98312 | tf_op jit(solution)/shard_map/ppermute | solution.py:324
  36.5 8.7 %collective-permute-start.18 = (bf16[2048,128]{1,0:T(8,128)(2,1)S(1)}, bf16[2048,128]{1,0:T(8,128)(2,1)S(1)}, u32[]{:S(2)}, u32[]{:S(2)}) collective-permute-start(bf16[2048,128]{1,0:T(8,128)(2,1)S(1)} %after.3), channel_id=1, source_target_pairs={{0,8},{8,0},{16,24},{24,16},{1,9},{9,1},{17,25},{25,17},{2,10},{10... | collective-permute-start | bytes 1572872 | tf_op jit(solution)/shard_map/ppermute | solution.py:316
  36.5 5.9 %collective-permute-start.16 = (f32[128,128]{1,0:T(8,128)S(1)}, f32[128,128]{1,0:T(8,128)S(1)}, u32[]{:S(2)}, u32[]{:S(2)}) collective-permute-start(f32[128,128]{1,0:T(8,128)S(1)} %pair_sum.1.own.after), channel_id=1, source_target_pairs={{0,3},{1,2},{2,1},{3,0},{4,7},{5,6},{6,5},{7,4},{8,11},{9,10},{10,... | collective-permute-start | bytes 196616 | tf_op jit(solution)/shard_map/ppermute | solution.py:324
  37.7 4.7 %collective-permute-start.15 = (f32[128,128]{1,0:T(8,128)S(1)}, f32[128,128]{1,0:T(8,128)S(1)}, u32[]{:S(2)}, u32[]{:S(2)}) collective-permute-start(f32[128,128]{1,0:T(8,128)S(1)} %pair_sum.1.own.after), channel_id=1, source_target_pairs={{0,2},{1,3},{2,0},{3,1},{4,6},{5,7},{6,4},{7,5},{8,10},{9,11},{10,... | collective-permute-start | bytes 196616 | tf_op jit(solution)/shard_map/ppermute | solution.py:324
  38.6 4.8 %collective-permute-start.14 = (f32[128,128]{1,0:T(8,128)S(1)}, f32[128,128]{1,0:T(8,128)S(1)}, u32[]{:S(2)}, u32[]{:S(2)}) collective-permute-start(f32[128,128]{1,0:T(8,128)S(1)} %pair_sum.1.own.after), channel_id=1, source_target_pairs={{0,1},{1,0},{2,3},{3,2},{4,5},{5,4},{6,7},{7,6},{8,9},{9,8},{10,11... | collective-permute-start | bytes 196616 | tf_op jit(solution)/shard_map/ppermute | solution.py:324
  43.4 1.8 %copy-start.1 = (s32[8]{0:T(128)S(1)}, s32[8]{0:T(128)}, u32[]{:S(2)}) copy-start(s32[8]{0:T(128)} %active.1) | copy-start | bytes 100
  43.4 1.8 %collective-permute-start.17 = (f32[768,128]{1,0:T(8,128)S(1)}, f32[768,128]{1,0:T(8,128)S(1)}, u32[]{:S(2)}, u32[]{:S(2)}) collective-permute-start(f32[768,128]{1,0:T(8,128)S(1)} %join.1.joined_mine), channel_id=1, source_target_pairs={{0,8},{8,0},{16,24},{24,16},{1,9},{9,1},{17,25},{25,17},{2,10},{10... | collective-permute-start | bytes 1179656 | tf_op jit(solution)/shard_map/ppermute | solution.py:316

commit v5 on v4

--- a/solution.py
+++ b/solution.py
@@ -67,8 +67,9 @@
     core = core_index()
     width = own.shape[1]
     size = keep.shape[0]
-    slab[pl.ds(pl.multiple_of(core * width, width), width), :] = cross(own[...], own[...])
-    slab[pl.ds(pl.multiple_of((1 - core) * width, width), width), :] = cross(own[...], mate[...])
+    between = cross(own[...], mate[...])
+    slab[0:width, :] = cross(own[...], own[...])
+    slab[width:, :] = jnp.where(core == 0, between[: width // 2, :], between.T[width // 2 :, :])
     for step, out in enumerate((keep, send1, send2, send3)):
         out[...] = slab[piece(step, size), :]
 
@@ -93,39 +94,40 @@
     keep[...] = slab[piece(0, size), :]
     for step, out in enumerate((send1, send2, send3)):
         out[0:size, :] = slab[piece(step + 1, size), :]
-        out[size : 2 * size, :] = chip_sum
+        out[size:, :] = chip_sum
 
 
 def pass_kernel(value, after, same):
     del value, after, same
 
 
-def group_sum_kernel(keep, chip_piece, part1, part2, part3, mate1, total, payload, chip_slab):
-    del mate1
-    size = keep.shape[0]
+def group_sum_kernel(keep, chip_piece, part1, part2, part3, total, payload, chip_slab):
+    size, count = keep.shape[0], chip_piece.shape[0]
     parts = (part1, part2, part3)
     group_sum = tree_sum([keep[...]] + [part[0:size, :] for part in parts])
     total[...] = group_sum
     payload[0:size, :] = group_sum
-    payload[size : 2 * size, :] = chip_piece[...]
-    chip_slab[piece(0, size), :] = chip_piece[...]
+    payload[size:, :] = chip_piece[...]
+    chip_slab[piece(0, count), :] = chip_piece[...]
     for step, part in enumerate(parts):
-        chip_slab[piece(step + 1, size), :] = part[size : 2 * size, :]
+        chip_slab[piece(step + 1, count), :] = part[size:, :]
 
 
 def pair_sum_kernel(total, across, *rest):
-    parts, payload = rest[:-2], rest[-1]
+    parts, pieces = rest[:-1], rest[-1]
     size = total.shape[0]
-    payload[0:size, :] = tree_sum([total[...], across[0:size, :]] + [part[...] for part in parts])
-    payload[size : 2 * size, :] = across[size : 2 * size, :]
-
-
-def join_kernel(own, part1, part2, part3, chip_mine, joined):
-    size = own.shape[0] // 2
+    pieces[0:size, :] = tree_sum([total[...], across[0:size, :]] + [part[0:size, :] for part in parts])
+    pieces[size:, :] = across[size:, :]
+
+
+def join_kernel(own, part1, part2, part3, chip_slab, mate1, joined):
+    del mate1
+    size = own.shape[1] // 2
+    count = own.shape[0] - size
     for step, part in enumerate((own, part1, part2, part3)):
         joined[piece(step, size), :] = part[0:size, :]
-        joined[piece(step, size, 8 * size), :] = part[size : 2 * size, :]
-    joined[4 * size : 8 * size, :] = chip_mine[...]
+        joined[piece(step, count, 4 * size + 4 * count), :] = part[size:, :]
+    joined[4 * size : 4 * size + 4 * count, :] = chip_slab[...]
 
 
 def split(value):
@@ -195,25 +197,29 @@
     for copy in copies:
         copy.start()
 
-    def parts(part):
-        rows = slice(2 * width * part, 2 * width * (part + 1))
-        mine, theirs = joined_mine[rows, :], joined_mate[rows, :]
-        core0 = jnp.where(core == 0, mine, theirs)
-        core1 = jnp.where(core == 0, theirs, mine)
-        return core0[:width], core0[width:], core1[:width], core1[width:]
+    def parts(start, stop):
+        mine, theirs = joined_mine[start:stop, :], joined_mate[start:stop, :]
+        return jnp.where(core == 0, mine, theirs), jnp.where(core == 0, theirs, mine)
 
     def put(row, col, value):
         gram[row * width : (row + 1) * width, col * width : (col + 1) * width] = value
 
-    here, there = parts(1), parts(2)
-    there = there[0], there[3], there[2], there[1]
+    count = 3 * width // 2
+    chip_first = 2 * width
+    other_first = chip_first + count
+    middle = other_first + count // 2
+    here = parts(chip_first, other_first)
+    upper, lower = parts(other_first, middle), parts(middle, other_first + count)
+    there = [jnp.concatenate([upper[index], lower[1 - index]], axis=0) for index in range(2)]
     for side in range(2):
-        top0, low0, top1, low1 = [jnp.where(chip == side, near_part, far_part) for near_part, far_part in zip(here, there)]
-        put(2 * side, 2 * side, top0)
-        put(2 * side, 2 * side + 1, low0)
-        put(2 * side + 1, 2 * side, top1)
-        put(2 * side + 1, 2 * side + 1, low1)
-    top0, low0, top1, low1 = parts(0)
+        core0, core1 = [jnp.where(chip == side, near_part, far_part) for near_part, far_part in zip(here, there)]
+        between = jnp.concatenate([core0[width:], core1[width:]], axis=0)
+        put(2 * side, 2 * side, core0[:width])
+        put(2 * side + 1, 2 * side + 1, core1[:width])
+        put(2 * side, 2 * side + 1, between)
+        put(2 * side + 1, 2 * side, between.T)
+    core0, core1 = parts(0, 2 * width)
+    top0, low0, top1, low1 = core0[:width], core0[width:], core1[:width], core1[width:]
     off10 = jnp.where(chip == 0, low0, low1)
     off01 = jnp.where(chip == 0, low1, low0)
     put(0, 2, top0)
@@ -310,7 +316,6 @@
     chip = chip_index()
     size = width // 2
     shape = jax.ShapeDtypeStruct
-    small, slab = shape((size, width), F32), shape((2 * width, width), F32)
 
     def swap(value, bit):
         return lax.ppermute(value, "state", [(index, index ^ bit) for index in range(4)])
@@ -331,8 +336,10 @@
 
     across1 = swap(lax.dynamic_slice_in_dim(vectors, (1 - chip) * half, half, 0), 2)
     mate = swap(vectors, 1)
+    quarter = 3 * width // 8
+    small = shape((quarter, width), F32)
     keep, *sends = call(
-        chip_gram_kernel, (small,) * 4, 2, 4 * rows * width * width, "chip_gram", scratch=[pltpu.VMEM(slab.shape, F32)]
+        chip_gram_kernel, (small,) * 4, 2, 0, "chip_gram", scratch=[pltpu.VMEM((4 * quarter, width), F32)]
     )(vectors, mate)
     later = call(
         later_kernel, shape((half, width), BF16), 0, 0, "later", scratch=[pltpu.SemaphoreType.DMA],
@@ -341,26 +348,26 @@
     across2 = swap(later, 2)
 
     groups = [4 * index for index in range(row_devices // 4)]
-    parts = [move(send, step + 1) for step, send in enumerate(sends)]
+    parts = [move(sends[step - 1], step) for step in (3, 2, 1)][::-1]
     chip_sum = call(chip_sum_kernel, small, 4, 0, "chip_sum", in_specs=[VMEM] * 4 + [ANY])(keep, *parts, later)
     chip_parts = [chip_sum] + [move(chip_sum, bits) for bits in groups[1:]]
-    double = shape((2 * size, width), F32)
+    pair, both = shape((size, width), F32), shape((size + quarter, width), F32)
     chip_piece, keep, *sends = call(
-        pair_gram_kernel, (small, small, double, double, double), 3 + len(chip_parts), 4 * half * width * width,
-        "pair_gram", scratch=[pltpu.VMEM(slab.shape, F32)],
+        pair_gram_kernel, (small, pair, both, both, both), 3 + len(chip_parts), 0, "pair_gram",
+        scratch=[pltpu.VMEM((4 * size, width), F32)],
     )(vectors, mate, across1, *chip_parts)
-    parts = [move(send, step + 1) for step, send in enumerate(sends)]
-    mate1 = swap(after(across1, chip_piece), 1)
-    pair_sum, payload, chip_mine = call(
-        group_sum_kernel, (small, double, slab), 0, 0, "group_sum", in_specs=[VMEM] * 5 + [ANY]
-    )(keep, chip_piece, *parts, mate1)
-    pair_parts = [move(payload, 0, 1)] + [move(pair_sum, bits, chips) for bits in groups[1:] for chips in range(2)]
-    payload = call(
-        pair_sum_kernel, double, 0, 0, "pair_sum", in_specs=[VMEM] * (1 + len(pair_parts)) + [ANY]
-    )(pair_sum, *pair_parts, across2)
-    parts = [move(payload, step) for step in (1, 2, 3)]
-    mate2 = swap(after(across2, payload), 1)
-    joined_mine = call(join_kernel, shape((6 * width, width), F32), 5, 0, "join")(payload, *parts, chip_mine)
+    parts = [move(sends[step - 1], step) for step in (3, 2, 1)][::-1]
+    pair_sum, payload, chip_slab = call(
+        group_sum_kernel, (pair, both, shape((4 * quarter, width), F32)), 5, 0, "group_sum"
+    )(keep, chip_piece, *parts)
+    mate1 = swap(after(across1, pair_sum), 1)
+    pair_parts = [move(payload, bits, chips) for bits in groups for chips in range(2) if bits or chips]
+    pieces = call(pair_sum_kernel, both, 1 + len(pair_parts), 0, "pair_sum")(pair_sum, *pair_parts)
+    parts = [move(pieces, step) for step in (1, 2, 3)]
+    mate2 = swap(after(across2, pieces), 1)
+    joined_mine = call(
+        join_kernel, shape((4 * (size + 2 * quarter), width), F32), 0, 0, "join", in_specs=[VMEM] * 5 + [ANY]
+    )(pieces, *parts, chip_slab, mate1)
     joined_mate = swap(joined_mine, 1)
 
     return call(

time: 55.6 us -> 54.8 us (0.986)
  waiting for transfers between devices: 19.9 us -> 18.8 us
    ppermute x6, waiting for transfers between devices: 5.01 us -> 1.63 us  [swap(): lax.ppermute(value, 'state', [(index, index ^ bit) for index in range(4)])]
    ppermute x13, waiting for transfers between devices: 14.9 us -> 17.1 us  [move(): return lax.ppermute(value, ('state', 'row'), pairs)]
  transfers between devices with their start and end apart: 19 -> 19, of which waited for: 13 -> 12; matrix products, arithmetic and copies ran while one was open for 2% -> 2% of each run, Pallas kernels for 2% -> 3%
where the time goes in v5:
time: 54.8 us; the launch traced here: 54.7 us
  starting transfers between devices  22.9 us (42%)
  waiting for transfers between devices  18.8 us (34%)
  Pallas kernels  11.7 us (21%)
  local copies, waits for them, and re-layouts  1.15 us (2%)
    ppermute x13, starting transfers between devices, move(): return lax.ppermute(value, ('state', 'row'), pairs)  17.9 us
    ppermute x13, waiting for transfers between devices, move(): return lax.ppermute(value, ('state', 'row'), pairs)  17.1 us
    pallas_call x1, Pallas kernels, shards(): call(functools.partial(finish_kernel, float(total_rows)), shape((rows, wi...  10.3 us
    ppermute x6, starting transfers between devices, swap(): lax.ppermute(value, 'state', [(index, index ^ bit) for index in range(4)])  5.01 us
    ppermute x6, waiting for transfers between devices, swap(): lax.ppermute(value, 'state', [(index, index ^ bit) for index in range(4)])  1.63 us
  transfers between devices with their start and end apart: 19, of which 12 were waited for; matrix products, arithmetic and copies ran while one was open for 2% of the time, Pallas kernels for 3%

profile of v5, /device:TPU:0, one launch (start us, length us, event | category | flops | bytes accessed | tf_op | source)
XLA Modules:
  0.0 54.7 jit_solution(8394154128579548633)
XLA Ops:
  0.0 0.0 copy-start
  0.0 0.5 collective-permute-start
  0.5 1.1 %constant_dynamic-slice_fusion = bf16[2048,128]{1,0:T(8,128)(2,1)S(1)} fusion(bf16[4096,128]{1,0:T(8,128)(2,1)} %own.7, s32[]{:T(128)S(6)} %select_n.9), kind=kLoop, calls=%fused_computation | loop fusion | bytes 1048580 | tf_op jit(solution)/shard_map/dynamic_slice | solution.py:337
  1.5 2.6 %collective-permute-start.1 = (bf16[2048,128]{1,0:T(8,128)(2,1)S(1)}, bf16[2048,128]{1,0:T(8,128)(2,1)S(1)}, u32[]{:S(2)}, u32[]{:S(2)}) collective-permute-start(bf16[2048,128]{1,0:T(8,128)(2,1)S(1)} %constant_dynamic-slice_fusion), channel_id=1, source_target_pairs={{0,16},{8,24},{16,0},{24,8},{1,17},{9,25},{17,1},{25,9},{2,18},{10... | collective-permute-start | bytes 1572872 | tf_op jit(solution)/shard_map/ppermute | solution.py:321
  4.2 0.0 collective-permute-done.mate
  4.2 0.0 copy-done
  4.2 0.8 %chip_gram.1 = (f32[48,128]{1,0:T(8,128)S(1)}, f32[48,128]{1,0:T(8,128)S(1)}, f32[48,128]{1,0:T(8,128)S(1)}, f32[48,128]{1,0:T(8,128)S(1)}) custom-call(bf16[4096,128]{1,0:T(8,128)(2,1)S(1)} %copy-done, bf16[4096,128]{1,0:T(8,128)(2,1)S(1)} %collective-permute-done.mate), custom_call_target="tpu_custom_call" | custom-call | tf_op jit(solution)/shard_map/chip_gram/pallas_call | solution.py:341
  4.9 0.1 later.1
  5.0 1.7 %collective-permute-start.17 = (bf16[2048,128]{1,0:T(8,128)(2,1)S(1)}, bf16[2048,128]{1,0:T(8,128)(2,1)S(1)}, u32[]{:S(2)}, u32[]{:S(2)}) collective-permute-start(bf16[2048,128]{1,0:T(8,128)(2,1)S(1)} %later.1), channel_id=1, source_target_pairs={{0,16},{8,24},{16,0},{24,8},{1,17},{9,25},{17,1},{25,9},{2,18},{10... | collective-permute-start | bytes 1572872 | tf_op jit(solution)/shard_map/ppermute | solution.py:321
  6.7 1.5 %collective-permute-start.2 = (f32[48,128]{1,0:T(8,128)S(1)}, f32[48,128]{1,0:T(8,128)S(1)}, u32[]{:S(2)}, u32[]{:S(2)}) collective-permute-start(f32[48,128]{1,0:T(8,128)S(1)} %get-tuple-element.18), channel_id=1, source_target_pairs={{0,1},{1,0},{2,3},{3,2},{4,5},{5,4},{6,7},{7,6},{8,9},{9,8},{10,11... | collective-permute-start | bytes 73736 | tf_op jit(solution)/shard_map/ppermute | solution.py:329
  8.2 1.6 %collective-permute-start.3 = (f32[48,128]{1,0:T(8,128)S(1)}, f32[48,128]{1,0:T(8,128)S(1)}, u32[]{:S(2)}, u32[]{:S(2)}) collective-permute-start(f32[48,128]{1,0:T(8,128)S(1)} %get-tuple-element.19), channel_id=1, source_target_pairs={{0,2},{1,3},{2,0},{3,1},{4,6},{5,7},{6,4},{7,5},{8,10},{9,11},{10,... | collective-permute-start | bytes 73736 | tf_op jit(solution)/shard_map/ppermute | solution.py:329
  9.8 0.4 collective-permute-start.4
  10.2 0.3 collective-permute-done.2.part1
  10.5 1.6 %collective-permute-done.3.part2 = f32[48,128]{1,0:T(8,128)S(1)} collective-permute-done((f32[48,128]{1,0:T(8,128)S(1)}, f32[48,128]{1,0:T(8,128)S(1)}, u32[]{:S(2)}, u32[]{:S(2)}) %collective-permute-start.3) | collective-permute-done | bytes 24608 | tf_op jit(solution)/shard_map/ppermute | solution.py:329
  12.2 2.4 %collective-permute-done.4.part3 = f32[48,128]{1,0:T(8,128)S(1)} collective-permute-done((f32[48,128]{1,0:T(8,128)S(1)}, f32[48,128]{1,0:T(8,128)S(1)}, u32[]{:S(2)}, u32[]{:S(2)}) %collective-permute-start.4) | collective-permute-done | bytes 24608 | tf_op jit(solution)/shard_map/ppermute | solution.py:329
  14.6 2.8 %collective-permute-start.5 = (f32[48,128]{1,0:T(8,128)S(1)}, f32[48,128]{1,0:T(8,128)S(1)}, u32[]{:S(2)}, u32[]{:S(2)}) collective-permute-start(f32[48,128]{1,0:T(8,128)S(1)} %chip_sum.1.rest_0_), channel_id=1, source_target_pairs={{0,4},{1,5},{2,6},{3,7},{4,0},{5,1},{6,2},{7,3},{8,12},{9,13},{10,... | collective-permute-start | bytes 73736 | tf_op jit(solution)/shard_map/ppermute | solution.py:329
  17.4 0.0 collective-permute-done.1.across.across1
  17.4 2.1 %collective-permute-done.5.rest_1_ = f32[48,128]{1,0:T(8,128)S(1)} collective-permute-done((f32[48,128]{1,0:T(8,128)S(1)}, f32[48,128]{1,0:T(8,128)S(1)}, u32[]{:S(2)}, u32[]{:S(2)}) %collective-permute-start.5) | collective-permute-done | bytes 24608 | tf_op jit(solution)/shard_map/ppermute | solution.py:329
  19.5 0.6 %pair_gram.1 = (f32[48,128]{1,0:T(8,128)S(1)}, f32[64,128]{1,0:T(8,128)S(1)}, f32[112,128]{1,0:T(8,128)S(1)}, f32[112,128]{1,0:T(8,128)S(1)}, f32[112,128]{1,0:T(8,128)S(1)}) custom-call(bf16[4096,128]{1,0:T(8,128)(2,1)S(1)} %copy-done, bf16[4096,128]{1,0:T(8,128)(2,1)S(1)} %collective-permute-done.mate, ...), custom_call_target="tpu_custom_call" | custom-call | tf_op jit(solution)/shard_map/pair_gram/pallas_call | solution.py:355
  20.1 0.6 %collective-permute-start.6 = (f32[112,128]{1,0:T(8,128)S(1)}, f32[112,128]{1,0:T(8,128)S(1)}, u32[]{:S(2)}, u32[]{:S(2)}) collective-permute-start(f32[112,128]{1,0:T(8,128)S(1)} %get-tuple-element.23), channel_id=1, source_target_pairs={{0,1},{1,0},{2,3},{3,2},{4,5},{5,4},{6,7},{7,6},{8,9},{9,8},{10,11... | collective-permute-start | bytes 172040 | tf_op jit(solution)/shard_map/ppermute | solution.py:329
  20.6 0.5 collective-permute-start.7
  21.1 2.5 %collective-permute-start.8 = (f32[112,128]{1,0:T(8,128)S(1)}, f32[112,128]{1,0:T(8,128)S(1)}, u32[]{:S(2)}, u32[]{:S(2)}) collective-permute-start(f32[112,128]{1,0:T(8,128)S(1)} %get-tuple-element.25), channel_id=1, source_target_pairs={{0,3},{1,2},{2,1},{3,0},{4,7},{5,6},{6,5},{7,4},{8,11},{9,10},{10,... | collective-permute-start | bytes 172040 | tf_op jit(solution)/shard_map/ppermute | solution.py:329
  23.6 0.8 %collective-permute-done.6.part1 = f32[112,128]{1,0:T(8,128)S(1)} collective-permute-done((f32[112,128]{1,0:T(8,128)S(1)}, f32[112,128]{1,0:T(8,128)S(1)}, u32[]{:S(2)}, u32[]{:S(2)}) %collective-permute-start.6) | collective-permute-done | bytes 57376 | tf_op jit(solution)/shard_map/ppermute | solution.py:329
  24.5 0.3 collective-permute-done.7.part2
  24.8 1.6 %collective-permute-done.8.part3 = f32[112,128]{1,0:T(8,128)S(1)} collective-permute-done((f32[112,128]{1,0:T(8,128)S(1)}, f32[112,128]{1,0:T(8,128)S(1)}, u32[]{:S(2)}, u32[]{:S(2)}) %collective-permute-start.8) | collective-permute-done | bytes 57376 | tf_op jit(solution)/shard_map/ppermute | solution.py:329
  26.4 0.1 collective-permute-start.15
  26.5 3.4 %collective-permute-start.11 = (f32[112,128]{1,0:T(8,128)S(1)}, f32[112,128]{1,0:T(8,128)S(1)}, u32[]{:S(2)}, u32[]{:S(2)}) collective-permute-start(f32[112,128]{1,0:T(8,128)S(1)} %get-tuple-element.27), channel_id=1, source_target_pairs={{0,20},{1,21},{2,30},{3,31},{4,16},{5,17},{6,26},{7,27},{8,28},{9,... | collective-permute-start | bytes 172040 | tf_op jit(solution)/shard_map/ppermute | solution.py:329
  29.9 0.3 collective-permute-start.10
  30.2 0.7 %collective-permute-start.9 = (f32[112,128]{1,0:T(8,128)S(1)}, f32[112,128]{1,0:T(8,128)S(1)}, u32[]{:S(2)}, u32[]{:S(2)}) collective-permute-start(f32[112,128]{1,0:T(8,128)S(1)} %get-tuple-element.27), channel_id=1, source_target_pairs={{0,16},{1,17},{2,26},{3,27},{4,20},{5,21},{6,30},{7,31},{8,24},{9,... | collective-permute-start | bytes 172040 | tf_op jit(solution)/shard_map/ppermute | solution.py:329
  30.9 2.9 %collective-permute-done.11.rest_1_ = f32[112,128]{1,0:T(8,128)S(1)} collective-permute-done((f32[112,128]{1,0:T(8,128)S(1)}, f32[112,128]{1,0:T(8,128)S(1)}, u32[]{:S(2)}, u32[]{:S(2)}) %collective-permute-start.11) | collective-permute-done | bytes 57376 | tf_op jit(solution)/shard_map/ppermute | solution.py:329
  33.9 2.1 %collective-permute-done.10.rest_0_ = f32[112,128]{1,0:T(8,128)S(1)} collective-permute-done((f32[112,128]{1,0:T(8,128)S(1)}, f32[112,128]{1,0:T(8,128)S(1)}, u32[]{:S(2)}, u32[]{:S(2)}) %collective-permute-start.10) | collective-permute-done | bytes 57376 | tf_op jit(solution)/shard_map/ppermute | solution.py:329
  36.0 0.0 collective-permute-done.9.across
  36.0 0.0 collective-permute-done.17.across2
  36.1 0.1 collective-permute-start.18
  36.2 0.9 %collective-permute-start.14 = (f32[112,128]{1,0:T(8,128)S(1)}, f32[112,128]{1,0:T(8,128)S(1)}, u32[]{:S(2)}, u32[]{:S(2)}) collective-permute-start(f32[112,128]{1,0:T(8,128)S(1)} %pair_sum.1.own.after), channel_id=1, source_target_pairs={{0,3},{1,2},{2,1},{3,0},{4,7},{5,6},{6,5},{7,4},{8,11},{9,10},{10,... | collective-permute-start | bytes 172040 | tf_op jit(solution)/shard_map/ppermute | solution.py:329
  37.0 1.4 %collective-permute-start.13 = (f32[112,128]{1,0:T(8,128)S(1)}, f32[112,128]{1,0:T(8,128)S(1)}, u32[]{:S(2)}, u32[]{:S(2)}) collective-permute-start(f32[112,128]{1,0:T(8,128)S(1)} %pair_sum.1.own.after), channel_id=1, source_target_pairs={{0,2},{1,3},{2,0},{3,1},{4,6},{5,7},{6,4},{7,5},{8,10},{9,11},{10,... | collective-permute-start | bytes 172040 | tf_op jit(solution)/shard_map/ppermute | solution.py:329
  38.4 1.3 %collective-permute-start.12 = (f32[112,128]{1,0:T(8,128)S(1)}, f32[112,128]{1,0:T(8,128)S(1)}, u32[]{:S(2)}, u32[]{:S(2)}) collective-permute-start(f32[112,128]{1,0:T(8,128)S(1)} %pair_sum.1.own.after), channel_id=1, source_target_pairs={{0,1},{1,0},{2,3},{3,2},{4,5},{5,4},{6,7},{7,6},{8,9},{9,8},{10,11... | collective-permute-start | bytes 172040 | tf_op jit(solution)/shard_map/ppermute | solution.py:329
  39.7 2.1 %collective-permute-done.14.part3 = f32[112,128]{1,0:T(8,128)S(1)} collective-permute-done((f32[112,128]{1,0:T(8,128)S(1)}, f32[112,128]{1,0:T(8,128)S(1)}, u32[]{:S(2)}, u32[]{:S(2)}) %collective-permute-start.14) | collective-permute-done | bytes 57376 | tf_op jit(solution)/shard_map/ppermute | solution.py:329
  41.9 0.0 collective-permute-done.13.part2
  41.9 0.8 %collective-permute-done.12.part1 = f32[112,128]{1,0:T(8,128)S(1)} collective-permute-done((f32[112,128]{1,0:T(8,128)S(1)}, f32[112,128]{1,0:T(8,128)S(1)}, u32[]{:S(2)}, u32[]{:S(2)}) %collective-permute-start.12) | collective-permute-done | bytes 57376 | tf_op jit(solution)/shard_map/ppermute | solution.py:329
  42.6 0.0 collective-permute-done.15.mate1
  42.6 0.0 copy-start.1
  42.7 0.1 collective-permute-start.16
  42.8 1.6 %collective-permute-done.16.joined_mate = f32[640,128]{1,0:T(8,128)S(1)} collective-permute-done((f32[640,128]{1,0:T(8,128)S(1)}, f32[640,128]{1,0:T(8,128)S(1)}, u32[]{:S(2)}, u32[]{:S(2)}) %collective-permute-start.16) | collective-permute-done | bytes 327712 | tf_op jit(solution)/shard_map/ppermute | solution.py:321
  44.4 0.0 collective-permute-done.18.mate2
  44.4 0.0 copy-done.1
  44.4 10.3 %finish.1 = bf16[4096,128]{1,0:T(8,128)(2,1)} custom-call(s32[8]{0:T(128)S(1)} %copy-done.1, f32[640,128]{1,0:T(8,128)S(1)} %join.1.joined_mine, f32[640,128]{1,0:T(8,128)S(1)} %collective-permute-done.16.joined_mate, bf16[4096,128]{1,0:T(8,128)(2,1)S(1)} %copy-done, bf16[4096,128]{1,0:T(8,128)(2,1)S(1)} %collective-permute-done.mate, ...), custom_call_target="tpu_custom_call" | custom-call | tf_op jit(solution)/shard_map/finish/pallas_call | solution.py:373
  (8 shorter events, 0.1 us)
Async XLA Ops:
  0.0 4.2 %copy-start = (bf16[4096,128]{1,0:T(8,128)(2,1)S(1)}, bf16[4096,128]{1,0:T(8,128)(2,1)}, u32[]{:S(2)}) copy-start(bf16[4096,128]{1,0:T(8,128)(2,1)} %own.7) | copy-start | bytes 3145732
  0.0 4.2 %collective-permute-start = (bf16[4096,128]{1,0:T(8,128)(2,1)}, bf16[4096,128]{1,0:T(8,128)(2,1)S(1)}, u32[]{:S(2)}, u32[]{:S(2)}) collective-permute-start(bf16[4096,128]{1,0:T(8,128)(2,1)} %own.7), channel_id=1, source_target_pairs={{0,8},{8,0},{16,24},{24,16},{1,9},{9,1},{17,25},{25,17},{2,10},{10... | collective-permute-start | bytes 3145736 | tf_op jit(solution)/shard_map/ppermute | solution.py:321
  1.5 15.9 %collective-permute-start.1 = (bf16[2048,128]{1,0:T(8,128)(2,1)S(1)}, bf16[2048,128]{1,0:T(8,128)(2,1)S(1)}, u32[]{:S(2)}, u32[]{:S(2)}) collective-permute-start(bf16[2048,128]{1,0:T(8,128)(2,1)S(1)} %constant_dynamic-slice_fusion), channel_id=1, source_target_pairs={{0,16},{8,24},{16,0},{24,8},{1,17},{9,25},{17,1},{25,9},{2,18},{10... | collective-permute-start | bytes 1572872 | tf_op jit(solution)/shard_map/ppermute | solution.py:321
  5.0 31.0 %collective-permute-start.17 = (bf16[2048,128]{1,0:T(8,128)(2,1)S(1)}, bf16[2048,128]{1,0:T(8,128)(2,1)S(1)}, u32[]{:S(2)}, u32[]{:S(2)}) collective-permute-start(bf16[2048,128]{1,0:T(8,128)(2,1)S(1)} %later.1), channel_id=1, source_target_pairs={{0,16},{8,24},{16,0},{24,8},{1,17},{9,25},{17,1},{25,9},{2,18},{10... | collective-permute-start | bytes 1572872 | tf_op jit(solution)/shard_map/ppermute | solution.py:321
  6.7 3.8 %collective-permute-start.2 = (f32[48,128]{1,0:T(8,128)S(1)}, f32[48,128]{1,0:T(8,128)S(1)}, u32[]{:S(2)}, u32[]{:S(2)}) collective-permute-start(f32[48,128]{1,0:T(8,128)S(1)} %get-tuple-element.18), channel_id=1, source_target_pairs={{0,1},{1,0},{2,3},{3,2},{4,5},{5,4},{6,7},{7,6},{8,9},{9,8},{10,11... | collective-permute-start | bytes 73736 | tf_op jit(solution)/shard_map/ppermute | solution.py:329
  8.2 3.9 %collective-permute-start.3 = (f32[48,128]{1,0:T(8,128)S(1)}, f32[48,128]{1,0:T(8,128)S(1)}, u32[]{:S(2)}, u32[]{:S(2)}) collective-permute-start(f32[48,128]{1,0:T(8,128)S(1)} %get-tuple-element.19), channel_id=1, source_target_pairs={{0,2},{1,3},{2,0},{3,1},{4,6},{5,7},{6,4},{7,5},{8,10},{9,11},{10,... | collective-permute-start | bytes 73736 | tf_op jit(solution)/shard_map/ppermute | solution.py:329
  9.8 4.7 %collective-permute-start.4 = (f32[48,128]{1,0:T(8,128)S(1)}, f32[48,128]{1,0:T(8,128)S(1)}, u32[]{:S(2)}, u32[]{:S(2)}) collective-permute-start(f32[48,128]{1,0:T(8,128)S(1)} %get-tuple-element.20), channel_id=1, source_target_pairs={{0,3},{1,2},{2,1},{3,0},{4,7},{5,6},{6,5},{7,4},{8,11},{9,10},{10,... | collective-permute-start | bytes 73736 | tf_op jit(solution)/shard_map/ppermute | solution.py:329
  14.6 4.9 %collective-permute-start.5 = (f32[48,128]{1,0:T(8,128)S(1)}, f32[48,128]{1,0:T(8,128)S(1)}, u32[]{:S(2)}, u32[]{:S(2)}) collective-permute-start(f32[48,128]{1,0:T(8,128)S(1)} %chip_sum.1.rest_0_), channel_id=1, source_target_pairs={{0,4},{1,5},{2,6},{3,7},{4,0},{5,1},{6,2},{7,3},{8,12},{9,13},{10,... | collective-permute-start | bytes 73736 | tf_op jit(solution)/shard_map/ppermute | solution.py:329
  20.1 4.4 %collective-permute-start.6 = (f32[112,128]{1,0:T(8,128)S(1)}, f32[112,128]{1,0:T(8,128)S(1)}, u32[]{:S(2)}, u32[]{:S(2)}) collective-permute-start(f32[112,128]{1,0:T(8,128)S(1)} %get-tuple-element.23), channel_id=1, source_target_pairs={{0,1},{1,0},{2,3},{3,2},{4,5},{5,4},{6,7},{7,6},{8,9},{9,8},{10,11... | collective-permute-start | bytes 172040 | tf_op jit(solution)/shard_map/ppermute | solution.py:329
  20.6 4.2 %collective-permute-start.7 = (f32[112,128]{1,0:T(8,128)S(1)}, f32[112,128]{1,0:T(8,128)S(1)}, u32[]{:S(2)}, u32[]{:S(2)}) collective-permute-start(f32[112,128]{1,0:T(8,128)S(1)} %get-tuple-element.24), channel_id=1, source_target_pairs={{0,2},{1,3},{2,0},{3,1},{4,6},{5,7},{6,4},{7,5},{8,10},{9,11},{10,... | collective-permute-start | bytes 172040 | tf_op jit(solution)/shard_map/ppermute | solution.py:329
  21.1 5.2 %collective-permute-start.8 = (f32[112,128]{1,0:T(8,128)S(1)}, f32[112,128]{1,0:T(8,128)S(1)}, u32[]{:S(2)}, u32[]{:S(2)}) collective-permute-start(f32[112,128]{1,0:T(8,128)S(1)} %get-tuple-element.25), channel_id=1, source_target_pairs={{0,3},{1,2},{2,1},{3,0},{4,7},{5,6},{6,5},{7,4},{8,11},{9,10},{10,... | collective-permute-start | bytes 172040 | tf_op jit(solution)/shard_map/ppermute | solution.py:329
  26.4 16.2 %collective-permute-start.15 = (bf16[2048,128]{1,0:T(8,128)(2,1)S(1)}, bf16[2048,128]{1,0:T(8,128)(2,1)S(1)}, u32[]{:S(2)}, u32[]{:S(2)}) collective-permute-start(bf16[2048,128]{1,0:T(8,128)(2,1)S(1)} %after.2), channel_id=1, source_target_pairs={{0,8},{8,0},{16,24},{24,16},{1,9},{9,1},{17,25},{25,17},{2,10},{10... | collective-permute-start | bytes 1572872 | tf_op jit(solution)/shard_map/ppermute | solution.py:321
  26.5 7.4 %collective-permute-start.11 = (f32[112,128]{1,0:T(8,128)S(1)}, f32[112,128]{1,0:T(8,128)S(1)}, u32[]{:S(2)}, u32[]{:S(2)}) collective-permute-start(f32[112,128]{1,0:T(8,128)S(1)} %get-tuple-element.27), channel_id=1, source_target_pairs={{0,20},{1,21},{2,30},{3,31},{4,16},{5,17},{6,26},{7,27},{8,28},{9,... | collective-permute-start | bytes 172040 | tf_op jit(solution)/shard_map/ppermute | solution.py:329
  29.9 6.1 %collective-permute-start.10 = (f32[112,128]{1,0:T(8,128)S(1)}, f32[112,128]{1,0:T(8,128)S(1)}, u32[]{:S(2)}, u32[]{:S(2)}) collective-permute-start(f32[112,128]{1,0:T(8,128)S(1)} %get-tuple-element.27), channel_id=1, source_target_pairs={{0,4},{1,5},{2,6},{3,7},{4,0},{5,1},{6,2},{7,3},{8,12},{9,13},{10,... | collective-permute-start | bytes 172040 | tf_op jit(solution)/shard_map/ppermute | solution.py:329
  30.2 5.8 %collective-permute-start.9 = (f32[112,128]{1,0:T(8,128)S(1)}, f32[112,128]{1,0:T(8,128)S(1)}, u32[]{:S(2)}, u32[]{:S(2)}) collective-permute-start(f32[112,128]{1,0:T(8,128)S(1)} %get-tuple-element.27), channel_id=1, source_target_pairs={{0,16},{1,17},{2,26},{3,27},{4,20},{5,21},{6,30},{7,31},{8,24},{9,... | collective-permute-start | bytes 172040 | tf_op jit(solution)/shard_map/ppermute | solution.py:329
  36.1 8.3 %collective-permute-start.18 = (bf16[2048,128]{1,0:T(8,128)(2,1)S(1)}, bf16[2048,128]{1,0:T(8,128)(2,1)S(1)}, u32[]{:S(2)}, u32[]{:S(2)}) collective-permute-start(bf16[2048,128]{1,0:T(8,128)(2,1)S(1)} %after.3), channel_id=1, source_target_pairs={{0,8},{8,0},{16,24},{24,16},{1,9},{9,1},{17,25},{25,17},{2,10},{10... | collective-permute-start | bytes 1572872 | tf_op jit(solution)/shard_map/ppermute | solution.py:321
  36.2 5.7 %collective-permute-start.14 = (f32[112,128]{1,0:T(8,128)S(1)}, f32[112,128]{1,0:T(8,128)S(1)}, u32[]{:S(2)}, u32[]{:S(2)}) collective-permute-start(f32[112,128]{1,0:T(8,128)S(1)} %pair_sum.1.own.after), channel_id=1, source_target_pairs={{0,3},{1,2},{2,1},{3,0},{4,7},{5,6},{6,5},{7,4},{8,11},{9,10},{10,... | collective-permute-start | bytes 172040 | tf_op jit(solution)/shard_map/ppermute | solution.py:329
  37.0 4.8 %collective-permute-start.13 = (f32[112,128]{1,0:T(8,128)S(1)}, f32[112,128]{1,0:T(8,128)S(1)}, u32[]{:S(2)}, u32[]{:S(2)}) collective-permute-start(f32[112,128]{1,0:T(8,128)S(1)} %pair_sum.1.own.after), channel_id=1, source_target_pairs={{0,2},{1,3},{2,0},{3,1},{4,6},{5,7},{6,4},{7,5},{8,10},{9,11},{10,... | collective-permute-start | bytes 172040 | tf_op jit(solution)/shard_map/ppermute | solution.py:329
  38.4 4.2 %collective-permute-start.12 = (f32[112,128]{1,0:T(8,128)S(1)}, f32[112,128]{1,0:T(8,128)S(1)}, u32[]{:S(2)}, u32[]{:S(2)}) collective-permute-start(f32[112,128]{1,0:T(8,128)S(1)} %pair_sum.1.own.after), channel_id=1, source_target_pairs={{0,1},{1,0},{2,3},{3,2},{4,5},{5,4},{6,7},{7,6},{8,9},{9,8},{10,11... | collective-permute-start | bytes 172040 | tf_op jit(solution)/shard_map/ppermute | solution.py:329
  42.6 1.7 %copy-start.1 = (s32[8]{0:T(128)S(1)}, s32[8]{0:T(128)}, u32[]{:S(2)}) copy-start(s32[8]{0:T(128)} %active.1) | copy-start | bytes 100
  42.7 1.7 %collective-permute-start.16 = (f32[640,128]{1,0:T(8,128)S(1)}, f32[640,128]{1,0:T(8,128)S(1)}, u32[]{:S(2)}, u32[]{:S(2)}) collective-permute-start(f32[640,128]{1,0:T(8,128)S(1)} %join.1.joined_mine), channel_id=1, source_target_pairs={{0,8},{8,0},{16,24},{24,16},{1,9},{9,1},{17,25},{25,17},{2,10},{10... | collective-permute-start | bytes 983048 | tf_op jit(solution)/shard_map/ppermute | solution.py:321

commit v6 on v5

--- a/solution.py
+++ b/solution.py
@@ -120,8 +120,7 @@
     pieces[size:, :] = across[size:, :]
 
 
-def join_kernel(own, part1, part2, part3, chip_slab, mate1, joined):
-    del mate1
+def join_kernel(own, part1, part2, part3, chip_slab, joined):
     size = own.shape[1] // 2
     count = own.shape[0] - size
     for step, part in enumerate((own, part1, part2, part3)):
@@ -136,7 +135,9 @@
 
 
 def product(left, right):
-    return dot(left[0], right[0]) + (dot(left[0], right[1]) + dot(left[1], right[0]))
+    return dot(
+        jnp.concatenate([left[0], left[0], left[1]], axis=1), jnp.concatenate([right[0], right[1], right[0]], axis=0)
+    )
 
 
 def row_product(left, right):
@@ -172,30 +173,13 @@
 
 def finish_kernel(
     total_rows, active, joined_mine, joined_mate, own, mate, across1, mate1, across2, mate2,
-    out, gram, highs, lows, factor, left, result, state_flags, sems, out_sems,
+    out, gram, highs, lows, factor, result, state_flags, fetch_sem, out_sems,
 ):
     chip, core = chip_index(), core_index()
     half, width = across1.shape
     cols = gram.shape[0]
-    near, far = pl.multiple_of(chip * half, half), pl.multiple_of((1 - chip) * half, half)
-    fetch = pltpu.make_async_copy(active, state_flags, sems.at[6])
+    fetch = pltpu.make_async_copy(active, state_flags, fetch_sem)
     fetch.start()
-    every = pl.ds(0, 2 * half)
-    copies = [
-        pltpu.make_async_copy(source, left.at[where, index * width : (index + 1) * width], sems.at[number])
-        for number, (source, where, index) in enumerate(
-            [
-                (own, every, 0),
-                (mate, every, 1),
-                (across1, pl.ds(near, half), 2),
-                (mate1, pl.ds(near, half), 3),
-                (across2, pl.ds(far, half), 2),
-                (mate2, pl.ds(far, half), 3),
-            ]
-        )
-    ]
-    for copy in copies:
-        copy.start()
 
     def parts(start, stop):
         mine, theirs = joined_mine[start:stop, :], joined_mate[start:stop, :]
@@ -293,16 +277,20 @@
         ],
         axis=0,
     )
-    for copy in copies:
-        copy.wait()
-    pieces = out_sems.shape[0]
-    size = out.shape[0] // pieces
+    pieces = out_sems.shape[0] // 2
+    size = half // pieces
     stores = []
-    for piece in range(pieces):
-        rows = slice(piece * size, (piece + 1) * size)
-        result[rows, :] = dot(left[rows, :], weights).astype(BF16)
-        stores.append(pltpu.make_async_copy(result.at[rows, :], out.at[rows, :], out_sems.at[piece]))
-        stores[-1].start()
+    for part, (across, other) in enumerate(((across1, mate1), (across2, mate2))):
+        start = half * (chip if part == 0 else 1 - chip)
+        for index in range(pieces):
+            near = slice(index * size, (index + 1) * size)
+            rows = pl.ds(pl.multiple_of(start + index * size, size), size)
+            left = jnp.concatenate([own[rows, :], mate[rows, :], across[near, :], other[near, :]], axis=1)
+            result[rows, :] = dot(left, weights).astype(BF16)
+            stores.append(
+                pltpu.make_async_copy(result.at[rows, :], out.at[rows, :], out_sems.at[part * pieces + index])
+            )
+            stores[-1].start()
     for store in stores:
         store.wait()
 
@@ -360,14 +348,14 @@
     pair_sum, payload, chip_slab = call(
         group_sum_kernel, (pair, both, shape((4 * quarter, width), F32)), 5, 0, "group_sum"
     )(keep, chip_piece, *parts)
-    mate1 = swap(after(across1, pair_sum), 1)
     pair_parts = [move(payload, bits, chips) for bits in groups for chips in range(2) if bits or chips]
     pieces = call(pair_sum_kernel, both, 1 + len(pair_parts), 0, "pair_sum")(pair_sum, *pair_parts)
     parts = [move(pieces, step) for step in (1, 2, 3)]
     mate2 = swap(after(across2, pieces), 1)
-    joined_mine = call(
-        join_kernel, shape((4 * (size + 2 * quarter), width), F32), 0, 0, "join", in_specs=[VMEM] * 5 + [ANY]
-    )(pieces, *parts, chip_slab, mate1)
+    mate1 = swap(after(across1, pieces), 1)
+    joined_mine = call(join_kernel, shape((4 * (size + 2 * quarter), width), F32), 5, 0, "join")(
+        pieces, *parts, chip_slab
+    )
     joined_mate = swap(joined_mine, 1)
 
     return call(
@@ -381,13 +369,12 @@
             pltpu.VMEM((ITERS - 1, cols, cols), BF16),
             pltpu.VMEM((ITERS - 1, cols, cols), BF16),
             pltpu.VMEM((cols, width), BF16),
-            pltpu.VMEM((rows, cols), BF16),
             pltpu.VMEM((rows, width), BF16),
             pltpu.SMEM(active.shape, jnp.int32),
-            pltpu.SemaphoreType.DMA((7,)),
+            pltpu.SemaphoreType.DMA,
             pltpu.SemaphoreType.DMA((4,)),
         ],
-        in_specs=[ANY, VMEM, VMEM] + [ANY] * 6,
+        in_specs=[ANY] + [VMEM] * 8,
         out_specs=ANY,
         mib=24,
     )(

time: 54.8 us -> 54.1 us (0.987)
  waiting for transfers between devices: 18.8 us -> 18.1 us
    ppermute x13, waiting for transfers between devices: 17.1 us -> 16.5 us  [move(): return lax.ppermute(value, ('state', 'row'), pairs)]
  transfers between devices with their start and end apart: 19 -> 19, of which waited for: 12 -> 13; matrix products, arithmetic and copies ran while one was open for 2% -> 2% of each run, Pallas kernels for 3% -> 3%
where the time goes in v6:
time: 54.1 us; the launch traced here: 53.9 us
  starting transfers between devices  23.3 us (43%)
  waiting for transfers between devices  18.1 us (33%)
  Pallas kernels  11.3 us (21%)
  local copies, waits for them, and re-layouts  1.15 us (2%)
    ppermute x13, starting transfers between devices, move(): return lax.ppermute(value, ('state', 'row'), pairs)  17.8 us
    ppermute x13, waiting for transfers between devices, move(): return lax.ppermute(value, ('state', 'row'), pairs)  16.5 us
    pallas_call x1, Pallas kernels, shards(): call(functools.partial(finish_kernel, float(total_rows)), shape((rows, wi...  9.81 us
    ppermute x6, starting transfers between devices, swap(): lax.ppermute(value, 'state', [(index, index ^ bit) for index in range(4)])  5.49 us
    ppermute x6, waiting for transfers between devices, swap(): lax.ppermute(value, 'state', [(index, index ^ bit) for index in range(4)])  1.63 us
  transfers between devices with their start and end apart: 19, of which 13 were waited for; matrix products, arithmetic and copies ran while one was open for 2% of the time, Pallas kernels for 3%

profile of v6, /device:TPU:0, one launch (start us, length us, event | category | flops | bytes accessed | tf_op | source)
XLA Modules:
  0.0 53.9 jit_solution(9132241720164206391)
XLA Ops:
  0.0 0.0 copy-start
  0.0 0.5 collective-permute-start
  0.5 1.1 %constant_dynamic-slice_fusion = bf16[2048,128]{1,0:T(8,128)(2,1)S(1)} fusion(bf16[4096,128]{1,0:T(8,128)(2,1)} %own.7, s32[]{:T(128)S(6)} %select_n.9), kind=kLoop, calls=%fused_computation | loop fusion | bytes 1048580 | tf_op jit(solution)/shard_map/dynamic_slice | solution.py:325
  1.5 2.6 %collective-permute-start.1 = (bf16[2048,128]{1,0:T(8,128)(2,1)S(1)}, bf16[2048,128]{1,0:T(8,128)(2,1)S(1)}, u32[]{:S(2)}, u32[]{:S(2)}) collective-permute-start(bf16[2048,128]{1,0:T(8,128)(2,1)S(1)} %constant_dynamic-slice_fusion), channel_id=1, source_target_pairs={{0,16},{8,24},{16,0},{24,8},{1,17},{9,25},{17,1},{25,9},{2,18},{10... | collective-permute-start | bytes 1572872 | tf_op jit(solution)/shard_map/ppermute | solution.py:309
  4.2 0.0 collective-permute-done.mate
  4.2 0.0 copy-done
  4.2 0.8 %chip_gram.1 = (f32[48,128]{1,0:T(8,128)S(1)}, f32[48,128]{1,0:T(8,128)S(1)}, f32[48,128]{1,0:T(8,128)S(1)}, f32[48,128]{1,0:T(8,128)S(1)}) custom-call(bf16[4096,128]{1,0:T(8,128)(2,1)S(1)} %copy-done, bf16[4096,128]{1,0:T(8,128)(2,1)S(1)} %collective-permute-done.mate), custom_call_target="tpu_custom_call" | custom-call | tf_op jit(solution)/shard_map/chip_gram/pallas_call | solution.py:329
  4.9 0.1 later.1
  5.0 1.7 %collective-permute-start.17 = (bf16[2048,128]{1,0:T(8,128)(2,1)S(1)}, bf16[2048,128]{1,0:T(8,128)(2,1)S(1)}, u32[]{:S(2)}, u32[]{:S(2)}) collective-permute-start(bf16[2048,128]{1,0:T(8,128)(2,1)S(1)} %later.1), channel_id=1, source_target_pairs={{0,16},{8,24},{16,0},{24,8},{1,17},{9,25},{17,1},{25,9},{2,18},{10... | collective-permute-start | bytes 1572872 | tf_op jit(solution)/shard_map/ppermute | solution.py:309
  6.7 1.5 %collective-permute-start.2 = (f32[48,128]{1,0:T(8,128)S(1)}, f32[48,128]{1,0:T(8,128)S(1)}, u32[]{:S(2)}, u32[]{:S(2)}) collective-permute-start(f32[48,128]{1,0:T(8,128)S(1)} %get-tuple-element.18), channel_id=1, source_target_pairs={{0,1},{1,0},{2,3},{3,2},{4,5},{5,4},{6,7},{7,6},{8,9},{9,8},{10,11... | collective-permute-start | bytes 73736 | tf_op jit(solution)/shard_map/ppermute | solution.py:317
  8.2 1.6 %collective-permute-start.3 = (f32[48,128]{1,0:T(8,128)S(1)}, f32[48,128]{1,0:T(8,128)S(1)}, u32[]{:S(2)}, u32[]{:S(2)}) collective-permute-start(f32[48,128]{1,0:T(8,128)S(1)} %get-tuple-element.19), channel_id=1, source_target_pairs={{0,2},{1,3},{2,0},{3,1},{4,6},{5,7},{6,4},{7,5},{8,10},{9,11},{10,... | collective-permute-start | bytes 73736 | tf_op jit(solution)/shard_map/ppermute | solution.py:317
  9.8 0.4 collective-permute-start.4
  10.2 0.3 collective-permute-done.2.part1
  10.5 1.6 %collective-permute-done.3.part2 = f32[48,128]{1,0:T(8,128)S(1)} collective-permute-done((f32[48,128]{1,0:T(8,128)S(1)}, f32[48,128]{1,0:T(8,128)S(1)}, u32[]{:S(2)}, u32[]{:S(2)}) %collective-permute-start.3) | collective-permute-done | bytes 24608 | tf_op jit(solution)/shard_map/ppermute | solution.py:317
  12.2 2.4 %collective-permute-done.4.part3 = f32[48,128]{1,0:T(8,128)S(1)} collective-permute-done((f32[48,128]{1,0:T(8,128)S(1)}, f32[48,128]{1,0:T(8,128)S(1)}, u32[]{:S(2)}, u32[]{:S(2)}) %collective-permute-start.4) | collective-permute-done | bytes 24608 | tf_op jit(solution)/shard_map/ppermute | solution.py:317
  14.6 2.8 %collective-permute-start.5 = (f32[48,128]{1,0:T(8,128)S(1)}, f32[48,128]{1,0:T(8,128)S(1)}, u32[]{:S(2)}, u32[]{:S(2)}) collective-permute-start(f32[48,128]{1,0:T(8,128)S(1)} %chip_sum.1.rest_0_), channel_id=1, source_target_pairs={{0,4},{1,5},{2,6},{3,7},{4,0},{5,1},{6,2},{7,3},{8,12},{9,13},{10,... | collective-permute-start | bytes 73736 | tf_op jit(solution)/shard_map/ppermute | solution.py:317
  17.4 0.0 collective-permute-done.1.across.across1
  17.4 2.1 %collective-permute-done.5.rest_1_ = f32[48,128]{1,0:T(8,128)S(1)} collective-permute-done((f32[48,128]{1,0:T(8,128)S(1)}, f32[48,128]{1,0:T(8,128)S(1)}, u32[]{:S(2)}, u32[]{:S(2)}) %collective-permute-start.5) | collective-permute-done | bytes 24608 | tf_op jit(solution)/shard_map/ppermute | solution.py:317
  19.5 0.6 %pair_gram.1 = (f32[48,128]{1,0:T(8,128)S(1)}, f32[64,128]{1,0:T(8,128)S(1)}, f32[112,128]{1,0:T(8,128)S(1)}, f32[112,128]{1,0:T(8,128)S(1)}, f32[112,128]{1,0:T(8,128)S(1)}) custom-call(bf16[4096,128]{1,0:T(8,128)(2,1)S(1)} %copy-done, bf16[4096,128]{1,0:T(8,128)(2,1)S(1)} %collective-permute-done.mate, ...), custom_call_target="tpu_custom_call" | custom-call | tf_op jit(solution)/shard_map/pair_gram/pallas_call | solution.py:343
  20.1 0.6 %collective-permute-start.6 = (f32[112,128]{1,0:T(8,128)S(1)}, f32[112,128]{1,0:T(8,128)S(1)}, u32[]{:S(2)}, u32[]{:S(2)}) collective-permute-start(f32[112,128]{1,0:T(8,128)S(1)} %get-tuple-element.23), channel_id=1, source_target_pairs={{0,1},{1,0},{2,3},{3,2},{4,5},{5,4},{6,7},{7,6},{8,9},{9,8},{10,11... | collective-permute-start | bytes 172040 | tf_op jit(solution)/shard_map/ppermute | solution.py:317
  20.6 0.5 collective-permute-start.7
  21.1 2.5 %collective-permute-start.8 = (f32[112,128]{1,0:T(8,128)S(1)}, f32[112,128]{1,0:T(8,128)S(1)}, u32[]{:S(2)}, u32[]{:S(2)}) collective-permute-start(f32[112,128]{1,0:T(8,128)S(1)} %get-tuple-element.25), channel_id=1, source_target_pairs={{0,3},{1,2},{2,1},{3,0},{4,7},{5,6},{6,5},{7,4},{8,11},{9,10},{10,... | collective-permute-start | bytes 172040 | tf_op jit(solution)/shard_map/ppermute | solution.py:317
  23.6 0.9 %collective-permute-done.6.part1 = f32[112,128]{1,0:T(8,128)S(1)} collective-permute-done((f32[112,128]{1,0:T(8,128)S(1)}, f32[112,128]{1,0:T(8,128)S(1)}, u32[]{:S(2)}, u32[]{:S(2)}) %collective-permute-start.6) | collective-permute-done | bytes 57376 | tf_op jit(solution)/shard_map/ppermute | solution.py:317
  24.5 0.3 collective-permute-done.7.part2
  24.8 1.6 %collective-permute-done.8.part3 = f32[112,128]{1,0:T(8,128)S(1)} collective-permute-done((f32[112,128]{1,0:T(8,128)S(1)}, f32[112,128]{1,0:T(8,128)S(1)}, u32[]{:S(2)}, u32[]{:S(2)}) %collective-permute-start.8) | collective-permute-done | bytes 57376 | tf_op jit(solution)/shard_map/ppermute | solution.py:317
  26.4 3.4 %collective-permute-start.11 = (f32[112,128]{1,0:T(8,128)S(1)}, f32[112,128]{1,0:T(8,128)S(1)}, u32[]{:S(2)}, u32[]{:S(2)}) collective-permute-start(f32[112,128]{1,0:T(8,128)S(1)} %get-tuple-element.27), channel_id=1, source_target_pairs={{0,20},{1,21},{2,30},{3,31},{4,16},{5,17},{6,26},{7,27},{8,28},{9,... | collective-permute-start | bytes 172040 | tf_op jit(solution)/shard_map/ppermute | solution.py:317
  29.8 0.3 collective-permute-start.10
  30.2 0.7 %collective-permute-start.9 = (f32[112,128]{1,0:T(8,128)S(1)}, f32[112,128]{1,0:T(8,128)S(1)}, u32[]{:S(2)}, u32[]{:S(2)}) collective-permute-start(f32[112,128]{1,0:T(8,128)S(1)} %get-tuple-element.27), channel_id=1, source_target_pairs={{0,16},{1,17},{2,26},{3,27},{4,20},{5,21},{6,30},{7,31},{8,24},{9,... | collective-permute-start | bytes 172040 | tf_op jit(solution)/shard_map/ppermute | solution.py:317
  30.9 2.8 %collective-permute-done.11.rest_1_ = f32[112,128]{1,0:T(8,128)S(1)} collective-permute-done((f32[112,128]{1,0:T(8,128)S(1)}, f32[112,128]{1,0:T(8,128)S(1)}, u32[]{:S(2)}, u32[]{:S(2)}) %collective-permute-start.11) | collective-permute-done | bytes 57376 | tf_op jit(solution)/shard_map/ppermute | solution.py:317
  33.7 1.2 %collective-permute-done.10.rest_0_ = f32[112,128]{1,0:T(8,128)S(1)} collective-permute-done((f32[112,128]{1,0:T(8,128)S(1)}, f32[112,128]{1,0:T(8,128)S(1)}, u32[]{:S(2)}, u32[]{:S(2)}) %collective-permute-start.10) | collective-permute-done | bytes 57376 | tf_op jit(solution)/shard_map/ppermute | solution.py:317
  34.9 0.0 collective-permute-done.9.across
  34.9 0.1 collective-permute-start.16
  35.0 0.0 collective-permute-done.17.across2
  35.1 0.6 %collective-permute-start.18 = (bf16[2048,128]{1,0:T(8,128)(2,1)S(1)}, bf16[2048,128]{1,0:T(8,128)(2,1)S(1)}, u32[]{:S(2)}, u32[]{:S(2)}) collective-permute-start(bf16[2048,128]{1,0:T(8,128)(2,1)S(1)} %after.3), channel_id=1, source_target_pairs={{0,8},{8,0},{16,24},{24,16},{1,9},{9,1},{17,25},{25,17},{2,10},{10... | collective-permute-start | bytes 1572872 | tf_op jit(solution)/shard_map/ppermute | solution.py:309
  35.6 0.9 %collective-permute-start.14 = (f32[112,128]{1,0:T(8,128)S(1)}, f32[112,128]{1,0:T(8,128)S(1)}, u32[]{:S(2)}, u32[]{:S(2)}) collective-permute-start(f32[112,128]{1,0:T(8,128)S(1)} %pair_sum.1.own.after), channel_id=1, source_target_pairs={{0,3},{1,2},{2,1},{3,0},{4,7},{5,6},{6,5},{7,4},{8,11},{9,10},{10,... | collective-permute-start | bytes 172040 | tf_op jit(solution)/shard_map/ppermute | solution.py:317
  36.5 1.7 %collective-permute-start.13 = (f32[112,128]{1,0:T(8,128)S(1)}, f32[112,128]{1,0:T(8,128)S(1)}, u32[]{:S(2)}, u32[]{:S(2)}) collective-permute-start(f32[112,128]{1,0:T(8,128)S(1)} %pair_sum.1.own.after), channel_id=1, source_target_pairs={{0,2},{1,3},{2,0},{3,1},{4,6},{5,7},{6,4},{7,5},{8,10},{9,11},{10,... | collective-permute-start | bytes 172040 | tf_op jit(solution)/shard_map/ppermute | solution.py:317
  38.2 0.9 %collective-permute-start.12 = (f32[112,128]{1,0:T(8,128)S(1)}, f32[112,128]{1,0:T(8,128)S(1)}, u32[]{:S(2)}, u32[]{:S(2)}) collective-permute-start(f32[112,128]{1,0:T(8,128)S(1)} %pair_sum.1.own.after), channel_id=1, source_target_pairs={{0,1},{1,0},{2,3},{3,2},{4,5},{5,4},{6,7},{7,6},{8,9},{9,8},{10,11... | collective-permute-start | bytes 172040 | tf_op jit(solution)/shard_map/ppermute | solution.py:317
  39.1 2.0 %collective-permute-done.14.part3 = f32[112,128]{1,0:T(8,128)S(1)} collective-permute-done((f32[112,128]{1,0:T(8,128)S(1)}, f32[112,128]{1,0:T(8,128)S(1)}, u32[]{:S(2)}, u32[]{:S(2)}) %collective-permute-start.14) | collective-permute-done | bytes 57376 | tf_op jit(solution)/shard_map/ppermute | solution.py:317
  41.2 0.2 collective-permute-done.13.part2
  41.3 1.1 %collective-permute-done.12.part1 = f32[112,128]{1,0:T(8,128)S(1)} collective-permute-done((f32[112,128]{1,0:T(8,128)S(1)}, f32[112,128]{1,0:T(8,128)S(1)}, u32[]{:S(2)}, u32[]{:S(2)}) %collective-permute-start.12) | collective-permute-done | bytes 57376 | tf_op jit(solution)/shard_map/ppermute | solution.py:317
  42.4 0.0 copy-start.1
  42.4 0.1 collective-permute-start.15
  42.5 1.6 %collective-permute-done.15.joined_mate = f32[640,128]{1,0:T(8,128)S(1)} collective-permute-done((f32[640,128]{1,0:T(8,128)S(1)}, f32[640,128]{1,0:T(8,128)S(1)}, u32[]{:S(2)}, u32[]{:S(2)}) %collective-permute-start.15) | collective-permute-done | bytes 327712 | tf_op jit(solution)/shard_map/ppermute | solution.py:309
  44.1 0.0 collective-permute-done.16.mate1
  44.1 0.0 collective-permute-done.18.mate2
  44.1 0.0 copy-done.1
  44.1 9.8 %finish.1 = bf16[4096,128]{1,0:T(8,128)(2,1)} custom-call(s32[8]{0:T(128)S(1)} %copy-done.1, f32[640,128]{1,0:T(8,128)S(1)} %join.1.joined_mine, f32[640,128]{1,0:T(8,128)S(1)} %collective-permute-done.15.joined_mate, bf16[4096,128]{1,0:T(8,128)(2,1)S(1)} %copy-done, bf16[4096,128]{1,0:T(8,128)(2,1)S(1)} %collective-permute-done.mate, ...), custom_call_target="tpu_custom_call" | custom-call | tf_op jit(solution)/shard_map/finish/pallas_call | solution.py:361
  (8 shorter events, 0.1 us)
Async XLA Ops:
  0.0 4.2 %copy-start = (bf16[4096,128]{1,0:T(8,128)(2,1)S(1)}, bf16[4096,128]{1,0:T(8,128)(2,1)}, u32[]{:S(2)}) copy-start(bf16[4096,128]{1,0:T(8,128)(2,1)} %own.7) | copy-start | bytes 3145732
  0.0 4.2 %collective-permute-start = (bf16[4096,128]{1,0:T(8,128)(2,1)}, bf16[4096,128]{1,0:T(8,128)(2,1)S(1)}, u32[]{:S(2)}, u32[]{:S(2)}) collective-permute-start(bf16[4096,128]{1,0:T(8,128)(2,1)} %own.7), channel_id=1, source_target_pairs={{0,8},{8,0},{16,24},{24,16},{1,9},{9,1},{17,25},{25,17},{2,10},{10... | collective-permute-start | bytes 3145736 | tf_op jit(solution)/shard_map/ppermute | solution.py:309
  1.5 15.9 %collective-permute-start.1 = (bf16[2048,128]{1,0:T(8,128)(2,1)S(1)}, bf16[2048,128]{1,0:T(8,128)(2,1)S(1)}, u32[]{:S(2)}, u32[]{:S(2)}) collective-permute-start(bf16[2048,128]{1,0:T(8,128)(2,1)S(1)} %constant_dynamic-slice_fusion), channel_id=1, source_target_pairs={{0,16},{8,24},{16,0},{24,8},{1,17},{9,25},{17,1},{25,9},{2,18},{10... | collective-permute-start | bytes 1572872 | tf_op jit(solution)/shard_map/ppermute | solution.py:309
  5.0 30.0 %collective-permute-start.17 = (bf16[2048,128]{1,0:T(8,128)(2,1)S(1)}, bf16[2048,128]{1,0:T(8,128)(2,1)S(1)}, u32[]{:S(2)}, u32[]{:S(2)}) collective-permute-start(bf16[2048,128]{1,0:T(8,128)(2,1)S(1)} %later.1), channel_id=1, source_target_pairs={{0,16},{8,24},{16,0},{24,8},{1,17},{9,25},{17,1},{25,9},{2,18},{10... | collective-permute-start | bytes 1572872 | tf_op jit(solution)/shard_map/ppermute | solution.py:309
  6.7 3.8 %collective-permute-start.2 = (f32[48,128]{1,0:T(8,128)S(1)}, f32[48,128]{1,0:T(8,128)S(1)}, u32[]{:S(2)}, u32[]{:S(2)}) collective-permute-start(f32[48,128]{1,0:T(8,128)S(1)} %get-tuple-element.18), channel_id=1, source_target_pairs={{0,1},{1,0},{2,3},{3,2},{4,5},{5,4},{6,7},{7,6},{8,9},{9,8},{10,11... | collective-permute-start | bytes 73736 | tf_op jit(solution)/shard_map/ppermute | solution.py:317
  8.2 3.9 %collective-permute-start.3 = (f32[48,128]{1,0:T(8,128)S(1)}, f32[48,128]{1,0:T(8,128)S(1)}, u32[]{:S(2)}, u32[]{:S(2)}) collective-permute-start(f32[48,128]{1,0:T(8,128)S(1)} %get-tuple-element.19), channel_id=1, source_target_pairs={{0,2},{1,3},{2,0},{3,1},{4,6},{5,7},{6,4},{7,5},{8,10},{9,11},{10,... | collective-permute-start | bytes 73736 | tf_op jit(solution)/shard_map/ppermute | solution.py:317
  9.8 4.7 %collective-permute-start.4 = (f32[48,128]{1,0:T(8,128)S(1)}, f32[48,128]{1,0:T(8,128)S(1)}, u32[]{:S(2)}, u32[]{:S(2)}) collective-permute-start(f32[48,128]{1,0:T(8,128)S(1)} %get-tuple-element.20), channel_id=1, source_target_pairs={{0,3},{1,2},{2,1},{3,0},{4,7},{5,6},{6,5},{7,4},{8,11},{9,10},{10,... | collective-permute-start | bytes 73736 | tf_op jit(solution)/shard_map/ppermute | solution.py:317
  14.6 4.9 %collective-permute-start.5 = (f32[48,128]{1,0:T(8,128)S(1)}, f32[48,128]{1,0:T(8,128)S(1)}, u32[]{:S(2)}, u32[]{:S(2)}) collective-permute-start(f32[48,128]{1,0:T(8,128)S(1)} %chip_sum.1.rest_0_), channel_id=1, source_target_pairs={{0,4},{1,5},{2,6},{3,7},{4,0},{5,1},{6,2},{7,3},{8,12},{9,13},{10,... | collective-permute-start | bytes 73736 | tf_op jit(solution)/shard_map/ppermute | solution.py:317
  20.1 4.4 %collective-permute-start.6 = (f32[112,128]{1,0:T(8,128)S(1)}, f32[112,128]{1,0:T(8,128)S(1)}, u32[]{:S(2)}, u32[]{:S(2)}) collective-permute-start(f32[112,128]{1,0:T(8,128)S(1)} %get-tuple-element.23), channel_id=1, source_target_pairs={{0,1},{1,0},{2,3},{3,2},{4,5},{5,4},{6,7},{7,6},{8,9},{9,8},{10,11... | collective-permute-start | bytes 172040 | tf_op jit(solution)/shard_map/ppermute | solution.py:317
  20.6 4.2 %collective-permute-start.7 = (f32[112,128]{1,0:T(8,128)S(1)}, f32[112,128]{1,0:T(8,128)S(1)}, u32[]{:S(2)}, u32[]{:S(2)}) collective-permute-start(f32[112,128]{1,0:T(8,128)S(1)} %get-tuple-element.24), channel_id=1, source_target_pairs={{0,2},{1,3},{2,0},{3,1},{4,6},{5,7},{6,4},{7,5},{8,10},{9,11},{10,... | collective-permute-start | bytes 172040 | tf_op jit(solution)/shard_map/ppermute | solution.py:317
  21.1 5.2 %collective-permute-start.8 = (f32[112,128]{1,0:T(8,128)S(1)}, f32[112,128]{1,0:T(8,128)S(1)}, u32[]{:S(2)}, u32[]{:S(2)}) collective-permute-start(f32[112,128]{1,0:T(8,128)S(1)} %get-tuple-element.25), channel_id=1, source_target_pairs={{0,3},{1,2},{2,1},{3,0},{4,7},{5,6},{6,5},{7,4},{8,11},{9,10},{10,... | collective-permute-start | bytes 172040 | tf_op jit(solution)/shard_map/ppermute | solution.py:317
  26.4 7.3 %collective-permute-start.11 = (f32[112,128]{1,0:T(8,128)S(1)}, f32[112,128]{1,0:T(8,128)S(1)}, u32[]{:S(2)}, u32[]{:S(2)}) collective-permute-start(f32[112,128]{1,0:T(8,128)S(1)} %get-tuple-element.27), channel_id=1, source_target_pairs={{0,20},{1,21},{2,30},{3,31},{4,16},{5,17},{6,26},{7,27},{8,28},{9,... | collective-permute-start | bytes 172040 | tf_op jit(solution)/shard_map/ppermute | solution.py:317
  29.8 5.1 %collective-permute-start.10 = (f32[112,128]{1,0:T(8,128)S(1)}, f32[112,128]{1,0:T(8,128)S(1)}, u32[]{:S(2)}, u32[]{:S(2)}) collective-permute-start(f32[112,128]{1,0:T(8,128)S(1)} %get-tuple-element.27), channel_id=1, source_target_pairs={{0,4},{1,5},{2,6},{3,7},{4,0},{5,1},{6,2},{7,3},{8,12},{9,13},{10,... | collective-permute-start | bytes 172040 | tf_op jit(solution)/shard_map/ppermute | solution.py:317
  30.2 4.8 %collective-permute-start.9 = (f32[112,128]{1,0:T(8,128)S(1)}, f32[112,128]{1,0:T(8,128)S(1)}, u32[]{:S(2)}, u32[]{:S(2)}) collective-permute-start(f32[112,128]{1,0:T(8,128)S(1)} %get-tuple-element.27), channel_id=1, source_target_pairs={{0,16},{1,17},{2,26},{3,27},{4,20},{5,21},{6,30},{7,31},{8,24},{9,... | collective-permute-start | bytes 172040 | tf_op jit(solution)/shard_map/ppermute | solution.py:317
  34.9 9.2 %collective-permute-start.16 = (bf16[2048,128]{1,0:T(8,128)(2,1)S(1)}, bf16[2048,128]{1,0:T(8,128)(2,1)S(1)}, u32[]{:S(2)}, u32[]{:S(2)}) collective-permute-start(bf16[2048,128]{1,0:T(8,128)(2,1)S(1)} %after.2), channel_id=1, source_target_pairs={{0,8},{8,0},{16,24},{24,16},{1,9},{9,1},{17,25},{25,17},{2,10},{10... | collective-permute-start | bytes 1572872 | tf_op jit(solution)/shard_map/ppermute | solution.py:309
  35.1 9.0 %collective-permute-start.18 = (bf16[2048,128]{1,0:T(8,128)(2,1)S(1)}, bf16[2048,128]{1,0:T(8,128)(2,1)S(1)}, u32[]{:S(2)}, u32[]{:S(2)}) collective-permute-start(bf16[2048,128]{1,0:T(8,128)(2,1)S(1)} %after.3), channel_id=1, source_target_pairs={{0,8},{8,0},{16,24},{24,16},{1,9},{9,1},{17,25},{25,17},{2,10},{10... | collective-permute-start | bytes 1572872 | tf_op jit(solution)/shard_map/ppermute | solution.py:309
  35.6 5.5 %collective-permute-start.14 = (f32[112,128]{1,0:T(8,128)S(1)}, f32[112,128]{1,0:T(8,128)S(1)}, u32[]{:S(2)}, u32[]{:S(2)}) collective-permute-start(f32[112,128]{1,0:T(8,128)S(1)} %pair_sum.1.own.after), channel_id=1, source_target_pairs={{0,3},{1,2},{2,1},{3,0},{4,7},{5,6},{6,5},{7,4},{8,11},{9,10},{10,... | collective-permute-start | bytes 172040 | tf_op jit(solution)/shard_map/ppermute | solution.py:317
  36.5 4.8 %collective-permute-start.13 = (f32[112,128]{1,0:T(8,128)S(1)}, f32[112,128]{1,0:T(8,128)S(1)}, u32[]{:S(2)}, u32[]{:S(2)}) collective-permute-start(f32[112,128]{1,0:T(8,128)S(1)} %pair_sum.1.own.after), channel_id=1, source_target_pairs={{0,2},{1,3},{2,0},{3,1},{4,6},{5,7},{6,4},{7,5},{8,10},{9,11},{10,... | collective-permute-start | bytes 172040 | tf_op jit(solution)/shard_map/ppermute | solution.py:317
  38.2 4.2 %collective-permute-start.12 = (f32[112,128]{1,0:T(8,128)S(1)}, f32[112,128]{1,0:T(8,128)S(1)}, u32[]{:S(2)}, u32[]{:S(2)}) collective-permute-start(f32[112,128]{1,0:T(8,128)S(1)} %pair_sum.1.own.after), channel_id=1, source_target_pairs={{0,1},{1,0},{2,3},{3,2},{4,5},{5,4},{6,7},{7,6},{8,9},{9,8},{10,11... | collective-permute-start | bytes 172040 | tf_op jit(solution)/shard_map/ppermute | solution.py:317
  42.4 1.7 %copy-start.1 = (s32[8]{0:T(128)S(1)}, s32[8]{0:T(128)}, u32[]{:S(2)}) copy-start(s32[8]{0:T(128)} %active.1) | copy-start | bytes 100
  42.4 1.7 %collective-permute-start.15 = (f32[640,128]{1,0:T(8,128)S(1)}, f32[640,128]{1,0:T(8,128)S(1)}, u32[]{:S(2)}, u32[]{:S(2)}) collective-permute-start(f32[640,128]{1,0:T(8,128)S(1)} %join.1.joined_mine), channel_id=1, source_target_pairs={{0,8},{8,0},{16,24},{24,16},{1,9},{9,1},{17,25},{25,17},{2,10},{10... | collective-permute-start | bytes 983048 | tf_op jit(solution)/shard_map/ppermute | solution.py:309

commit v7 on v6

--- a/solution.py
+++ b/solution.py
@@ -149,18 +149,6 @@
 def symmetric(first, mixed, last):
     return jnp.concatenate(
         [jnp.concatenate([first, mixed], axis=1), jnp.concatenate([mixed.T, last], axis=1)], axis=0
-    )
-
-
-def symmetric_square(high, low):
-    half = high.shape[0] // 2
-    cross_part = dot(high, low)
-    upper = dot(high[:half], high)
-    last = dot(high[half:], high[:, half:])
-    return symmetric(
-        upper[:, :half] + (cross_part[:half, :half] + cross_part[:half, :half].T),
-        upper[:, half:] + (cross_part[:half, half:] + cross_part[half:, :half].T),
-        last + (cross_part[half:, half:] + cross_part[half:, half:].T),
     )
 
 
@@ -242,7 +230,7 @@
     for step in range(last):
         high, low = split(current)
         highs[step], lows[step] = high, low
-        square = symmetric_square(high, low)
+        square = symmetric_product((high, low), (high, low))
         cube = symmetric_product((high, low), split(square))
         current = 2.25 * current - 1.5 * square + 0.25 * cube
     highs[last], lows[last] = split(current)

time: 54.1 us -> 53.8 us (level)
  no operation moved by 1% of the time
where the time goes in v7:
time: 53.8 us; the launch traced here: 53.7 us
  starting transfers between devices  23.3 us (43%)
  waiting for transfers between devices  18.1 us (34%)
  Pallas kernels  11 us (20%)
  local copies, waits for them, and re-layouts  1.15 us (2%)
    ppermute x13, starting transfers between devices, move(): return lax.ppermute(value, ('state', 'row'), pairs)  17.8 us
    ppermute x13, waiting for transfers between devices, move(): return lax.ppermute(value, ('state', 'row'), pairs)  16.5 us
    pallas_call x1, Pallas kernels, shards(): call(functools.partial(finish_kernel, float(total_rows)), shape((rows, wi...  9.56 us
    ppermute x6, starting transfers between devices, swap(): lax.ppermute(value, 'state', [(index, index ^ bit) for index in range(4)])  5.49 us
    ppermute x6, waiting for transfers between devices, swap(): lax.ppermute(value, 'state', [(index, index ^ bit) for index in range(4)])  1.63 us
  transfers between devices with their start and end apart: 19, of which 13 were waited for; matrix products, arithmetic and copies ran while one was open for 2% of the time, Pallas kernels for 3%

profile of v7, /device:TPU:0, one launch (start us, length us, event | category | flops | bytes accessed | tf_op | source)
XLA Modules:
  0.0 53.7 jit_solution(16165844524456738141)
XLA Ops:
  0.0 0.0 copy-start
  0.0 0.5 collective-permute-start
  0.5 1.1 %constant_dynamic-slice_fusion = bf16[2048,128]{1,0:T(8,128)(2,1)S(1)} fusion(bf16[4096,128]{1,0:T(8,128)(2,1)} %own.7, s32[]{:T(128)S(6)} %select_n.9), kind=kLoop, calls=%fused_computation | loop fusion | bytes 1048580 | tf_op jit(solution)/shard_map/dynamic_slice | solution.py:313
  1.5 2.6 %collective-permute-start.1 = (bf16[2048,128]{1,0:T(8,128)(2,1)S(1)}, bf16[2048,128]{1,0:T(8,128)(2,1)S(1)}, u32[]{:S(2)}, u32[]{:S(2)}) collective-permute-start(bf16[2048,128]{1,0:T(8,128)(2,1)S(1)} %constant_dynamic-slice_fusion), channel_id=1, source_target_pairs={{0,16},{8,24},{16,0},{24,8},{1,17},{9,25},{17,1},{25,9},{2,18},{10... | collective-permute-start | bytes 1572872 | tf_op jit(solution)/shard_map/ppermute | solution.py:297
  4.2 0.0 collective-permute-done.mate
  4.2 0.0 copy-done
  4.2 0.8 %chip_gram.1 = (f32[48,128]{1,0:T(8,128)S(1)}, f32[48,128]{1,0:T(8,128)S(1)}, f32[48,128]{1,0:T(8,128)S(1)}, f32[48,128]{1,0:T(8,128)S(1)}) custom-call(bf16[4096,128]{1,0:T(8,128)(2,1)S(1)} %copy-done, bf16[4096,128]{1,0:T(8,128)(2,1)S(1)} %collective-permute-done.mate), custom_call_target="tpu_custom_call" | custom-call | tf_op jit(solution)/shard_map/chip_gram/pallas_call | solution.py:317
  4.9 0.1 later.1
  5.0 1.7 %collective-permute-start.17 = (bf16[2048,128]{1,0:T(8,128)(2,1)S(1)}, bf16[2048,128]{1,0:T(8,128)(2,1)S(1)}, u32[]{:S(2)}, u32[]{:S(2)}) collective-permute-start(bf16[2048,128]{1,0:T(8,128)(2,1)S(1)} %later.1), channel_id=1, source_target_pairs={{0,16},{8,24},{16,0},{24,8},{1,17},{9,25},{17,1},{25,9},{2,18},{10... | collective-permute-start | bytes 1572872 | tf_op jit(solution)/shard_map/ppermute | solution.py:297
  6.7 1.5 %collective-permute-start.2 = (f32[48,128]{1,0:T(8,128)S(1)}, f32[48,128]{1,0:T(8,128)S(1)}, u32[]{:S(2)}, u32[]{:S(2)}) collective-permute-start(f32[48,128]{1,0:T(8,128)S(1)} %get-tuple-element.18), channel_id=1, source_target_pairs={{0,1},{1,0},{2,3},{3,2},{4,5},{5,4},{6,7},{7,6},{8,9},{9,8},{10,11... | collective-permute-start | bytes 73736 | tf_op jit(solution)/shard_map/ppermute | solution.py:305
  8.2 1.6 %collective-permute-start.3 = (f32[48,128]{1,0:T(8,128)S(1)}, f32[48,128]{1,0:T(8,128)S(1)}, u32[]{:S(2)}, u32[]{:S(2)}) collective-permute-start(f32[48,128]{1,0:T(8,128)S(1)} %get-tuple-element.19), channel_id=1, source_target_pairs={{0,2},{1,3},{2,0},{3,1},{4,6},{5,7},{6,4},{7,5},{8,10},{9,11},{10,... | collective-permute-start | bytes 73736 | tf_op jit(solution)/shard_map/ppermute | solution.py:305
  9.8 0.4 collective-permute-start.4
  10.2 0.3 collective-permute-done.2.part1
  10.5 1.6 %collective-permute-done.3.part2 = f32[48,128]{1,0:T(8,128)S(1)} collective-permute-done((f32[48,128]{1,0:T(8,128)S(1)}, f32[48,128]{1,0:T(8,128)S(1)}, u32[]{:S(2)}, u32[]{:S(2)}) %collective-permute-start.3) | collective-permute-done | bytes 24608 | tf_op jit(solution)/shard_map/ppermute | solution.py:305
  12.2 2.4 %collective-permute-done.4.part3 = f32[48,128]{1,0:T(8,128)S(1)} collective-permute-done((f32[48,128]{1,0:T(8,128)S(1)}, f32[48,128]{1,0:T(8,128)S(1)}, u32[]{:S(2)}, u32[]{:S(2)}) %collective-permute-start.4) | collective-permute-done | bytes 24608 | tf_op jit(solution)/shard_map/ppermute | solution.py:305
  14.6 2.8 %collective-permute-start.5 = (f32[48,128]{1,0:T(8,128)S(1)}, f32[48,128]{1,0:T(8,128)S(1)}, u32[]{:S(2)}, u32[]{:S(2)}) collective-permute-start(f32[48,128]{1,0:T(8,128)S(1)} %chip_sum.1.rest_0_), channel_id=1, source_target_pairs={{0,4},{1,5},{2,6},{3,7},{4,0},{5,1},{6,2},{7,3},{8,12},{9,13},{10,... | collective-permute-start | bytes 73736 | tf_op jit(solution)/shard_map/ppermute | solution.py:305
  17.4 0.0 collective-permute-done.1.across.across1
  17.4 2.1 %collective-permute-done.5.rest_1_ = f32[48,128]{1,0:T(8,128)S(1)} collective-permute-done((f32[48,128]{1,0:T(8,128)S(1)}, f32[48,128]{1,0:T(8,128)S(1)}, u32[]{:S(2)}, u32[]{:S(2)}) %collective-permute-start.5) | collective-permute-done | bytes 24608 | tf_op jit(solution)/shard_map/ppermute | solution.py:305
  19.5 0.6 %pair_gram.1 = (f32[48,128]{1,0:T(8,128)S(1)}, f32[64,128]{1,0:T(8,128)S(1)}, f32[112,128]{1,0:T(8,128)S(1)}, f32[112,128]{1,0:T(8,128)S(1)}, f32[112,128]{1,0:T(8,128)S(1)}) custom-call(bf16[4096,128]{1,0:T(8,128)(2,1)S(1)} %copy-done, bf16[4096,128]{1,0:T(8,128)(2,1)S(1)} %collective-permute-done.mate, ...), custom_call_target="tpu_custom_call" | custom-call | tf_op jit(solution)/shard_map/pair_gram/pallas_call | solution.py:331
  20.1 0.6 %collective-permute-start.6 = (f32[112,128]{1,0:T(8,128)S(1)}, f32[112,128]{1,0:T(8,128)S(1)}, u32[]{:S(2)}, u32[]{:S(2)}) collective-permute-start(f32[112,128]{1,0:T(8,128)S(1)} %get-tuple-element.23), channel_id=1, source_target_pairs={{0,1},{1,0},{2,3},{3,2},{4,5},{5,4},{6,7},{7,6},{8,9},{9,8},{10,11... | collective-permute-start | bytes 172040 | tf_op jit(solution)/shard_map/ppermute | solution.py:305
  20.6 0.5 collective-permute-start.7
  21.1 2.5 %collective-permute-start.8 = (f32[112,128]{1,0:T(8,128)S(1)}, f32[112,128]{1,0:T(8,128)S(1)}, u32[]{:S(2)}, u32[]{:S(2)}) collective-permute-start(f32[112,128]{1,0:T(8,128)S(1)} %get-tuple-element.25), channel_id=1, source_target_pairs={{0,3},{1,2},{2,1},{3,0},{4,7},{5,6},{6,5},{7,4},{8,11},{9,10},{10,... | collective-permute-start | bytes 172040 | tf_op jit(solution)/shard_map/ppermute | solution.py:305
  23.6 0.9 %collective-permute-done.6.part1 = f32[112,128]{1,0:T(8,128)S(1)} collective-permute-done((f32[112,128]{1,0:T(8,128)S(1)}, f32[112,128]{1,0:T(8,128)S(1)}, u32[]{:S(2)}, u32[]{:S(2)}) %collective-permute-start.6) | collective-permute-done | bytes 57376 | tf_op jit(solution)/shard_map/ppermute | solution.py:305
  24.5 0.3 collective-permute-done.7.part2
  24.8 1.6 %collective-permute-done.8.part3 = f32[112,128]{1,0:T(8,128)S(1)} collective-permute-done((f32[112,128]{1,0:T(8,128)S(1)}, f32[112,128]{1,0:T(8,128)S(1)}, u32[]{:S(2)}, u32[]{:S(2)}) %collective-permute-start.8) | collective-permute-done | bytes 57376 | tf_op jit(solution)/shard_map/ppermute | solution.py:305
  26.4 3.4 %collective-permute-start.11 = (f32[112,128]{1,0:T(8,128)S(1)}, f32[112,128]{1,0:T(8,128)S(1)}, u32[]{:S(2)}, u32[]{:S(2)}) collective-permute-start(f32[112,128]{1,0:T(8,128)S(1)} %get-tuple-element.27), channel_id=1, source_target_pairs={{0,20},{1,21},{2,30},{3,31},{4,16},{5,17},{6,26},{7,27},{8,28},{9,... | collective-permute-start | bytes 172040 | tf_op jit(solution)/shard_map/ppermute | solution.py:305
  29.8 0.3 collective-permute-start.10
  30.2 0.7 %collective-permute-start.9 = (f32[112,128]{1,0:T(8,128)S(1)}, f32[112,128]{1,0:T(8,128)S(1)}, u32[]{:S(2)}, u32[]{:S(2)}) collective-permute-start(f32[112,128]{1,0:T(8,128)S(1)} %get-tuple-element.27), channel_id=1, source_target_pairs={{0,16},{1,17},{2,26},{3,27},{4,20},{5,21},{6,30},{7,31},{8,24},{9,... | collective-permute-start | bytes 172040 | tf_op jit(solution)/shard_map/ppermute | solution.py:305
  30.9 2.8 %collective-permute-done.11.rest_1_ = f32[112,128]{1,0:T(8,128)S(1)} collective-permute-done((f32[112,128]{1,0:T(8,128)S(1)}, f32[112,128]{1,0:T(8,128)S(1)}, u32[]{:S(2)}, u32[]{:S(2)}) %collective-permute-start.11) | collective-permute-done | bytes 57376 | tf_op jit(solution)/shard_map/ppermute | solution.py:305
  33.7 1.2 %collective-permute-done.10.rest_0_ = f32[112,128]{1,0:T(8,128)S(1)} collective-permute-done((f32[112,128]{1,0:T(8,128)S(1)}, f32[112,128]{1,0:T(8,128)S(1)}, u32[]{:S(2)}, u32[]{:S(2)}) %collective-permute-start.10) | collective-permute-done | bytes 57376 | tf_op jit(solution)/shard_map/ppermute | solution.py:305
  34.9 0.0 collective-permute-done.9.across
  34.9 0.1 collective-permute-start.16
  35.0 0.0 collective-permute-done.17.across2
  35.1 0.6 %collective-permute-start.18 = (bf16[2048,128]{1,0:T(8,128)(2,1)S(1)}, bf16[2048,128]{1,0:T(8,128)(2,1)S(1)}, u32[]{:S(2)}, u32[]{:S(2)}) collective-permute-start(bf16[2048,128]{1,0:T(8,128)(2,1)S(1)} %after.3), channel_id=1, source_target_pairs={{0,8},{8,0},{16,24},{24,16},{1,9},{9,1},{17,25},{25,17},{2,10},{10... | collective-permute-start | bytes 1572872 | tf_op jit(solution)/shard_map/ppermute | solution.py:297
  35.6 0.9 %collective-permute-start.14 = (f32[112,128]{1,0:T(8,128)S(1)}, f32[112,128]{1,0:T(8,128)S(1)}, u32[]{:S(2)}, u32[]{:S(2)}) collective-permute-start(f32[112,128]{1,0:T(8,128)S(1)} %pair_sum.1.own.after), channel_id=1, source_target_pairs={{0,3},{1,2},{2,1},{3,0},{4,7},{5,6},{6,5},{7,4},{8,11},{9,10},{10,... | collective-permute-start | bytes 172040 | tf_op jit(solution)/shard_map/ppermute | solution.py:305
  36.5 1.7 %collective-permute-start.13 = (f32[112,128]{1,0:T(8,128)S(1)}, f32[112,128]{1,0:T(8,128)S(1)}, u32[]{:S(2)}, u32[]{:S(2)}) collective-permute-start(f32[112,128]{1,0:T(8,128)S(1)} %pair_sum.1.own.after), channel_id=1, source_target_pairs={{0,2},{1,3},{2,0},{3,1},{4,6},{5,7},{6,4},{7,5},{8,10},{9,11},{10,... | collective-permute-start | bytes 172040 | tf_op jit(solution)/shard_map/ppermute | solution.py:305
  38.2 0.9 %collective-permute-start.12 = (f32[112,128]{1,0:T(8,128)S(1)}, f32[112,128]{1,0:T(8,128)S(1)}, u32[]{:S(2)}, u32[]{:S(2)}) collective-permute-start(f32[112,128]{1,0:T(8,128)S(1)} %pair_sum.1.own.after), channel_id=1, source_target_pairs={{0,1},{1,0},{2,3},{3,2},{4,5},{5,4},{6,7},{7,6},{8,9},{9,8},{10,11... | collective-permute-start | bytes 172040 | tf_op jit(solution)/shard_map/ppermute | solution.py:305
  39.1 2.0 %collective-permute-done.14.part3 = f32[112,128]{1,0:T(8,128)S(1)} collective-permute-done((f32[112,128]{1,0:T(8,128)S(1)}, f32[112,128]{1,0:T(8,128)S(1)}, u32[]{:S(2)}, u32[]{:S(2)}) %collective-permute-start.14) | collective-permute-done | bytes 57376 | tf_op jit(solution)/shard_map/ppermute | solution.py:305
  41.2 0.2 collective-permute-done.13.part2
  41.3 1.1 %collective-permute-done.12.part1 = f32[112,128]{1,0:T(8,128)S(1)} collective-permute-done((f32[112,128]{1,0:T(8,128)S(1)}, f32[112,128]{1,0:T(8,128)S(1)}, u32[]{:S(2)}, u32[]{:S(2)}) %collective-permute-start.12) | collective-permute-done | bytes 57376 | tf_op jit(solution)/shard_map/ppermute | solution.py:305
  42.4 0.0 copy-start.1
  42.4 0.1 collective-permute-start.15
  42.5 1.6 %collective-permute-done.15.joined_mate = f32[640,128]{1,0:T(8,128)S(1)} collective-permute-done((f32[640,128]{1,0:T(8,128)S(1)}, f32[640,128]{1,0:T(8,128)S(1)}, u32[]{:S(2)}, u32[]{:S(2)}) %collective-permute-start.15) | collective-permute-done | bytes 327712 | tf_op jit(solution)/shard_map/ppermute | solution.py:297
  44.1 0.0 collective-permute-done.16.mate1
  44.1 0.0 collective-permute-done.18.mate2
  44.1 0.0 copy-done.1
  44.1 9.6 %finish.1 = bf16[4096,128]{1,0:T(8,128)(2,1)} custom-call(s32[8]{0:T(128)S(1)} %copy-done.1, f32[640,128]{1,0:T(8,128)S(1)} %join.1.joined_mine, f32[640,128]{1,0:T(8,128)S(1)} %collective-permute-done.15.joined_mate, bf16[4096,128]{1,0:T(8,128)(2,1)S(1)} %copy-done, bf16[4096,128]{1,0:T(8,128)(2,1)S(1)} %collective-permute-done.mate, ...), custom_call_target="tpu_custom_call" | custom-call | tf_op jit(solution)/shard_map/finish/pallas_call | solution.py:349
  (8 shorter events, 0.1 us)
Async XLA Ops:
  0.0 4.2 %copy-start = (bf16[4096,128]{1,0:T(8,128)(2,1)S(1)}, bf16[4096,128]{1,0:T(8,128)(2,1)}, u32[]{:S(2)}) copy-start(bf16[4096,128]{1,0:T(8,128)(2,1)} %own.7) | copy-start | bytes 3145732
  0.0 4.2 %collective-permute-start = (bf16[4096,128]{1,0:T(8,128)(2,1)}, bf16[4096,128]{1,0:T(8,128)(2,1)S(1)}, u32[]{:S(2)}, u32[]{:S(2)}) collective-permute-start(bf16[4096,128]{1,0:T(8,128)(2,1)} %own.7), channel_id=1, source_target_pairs={{0,8},{8,0},{16,24},{24,16},{1,9},{9,1},{17,25},{25,17},{2,10},{10... | collective-permute-start | bytes 3145736 | tf_op jit(solution)/shard_map/ppermute | solution.py:297
  1.5 15.9 %collective-permute-start.1 = (bf16[2048,128]{1,0:T(8,128)(2,1)S(1)}, bf16[2048,128]{1,0:T(8,128)(2,1)S(1)}, u32[]{:S(2)}, u32[]{:S(2)}) collective-permute-start(bf16[2048,128]{1,0:T(8,128)(2,1)S(1)} %constant_dynamic-slice_fusion), channel_id=1, source_target_pairs={{0,16},{8,24},{16,0},{24,8},{1,17},{9,25},{17,1},{25,9},{2,18},{10... | collective-permute-start | bytes 1572872 | tf_op jit(solution)/shard_map/ppermute | solution.py:297
  5.0 30.0 %collective-permute-start.17 = (bf16[2048,128]{1,0:T(8,128)(2,1)S(1)}, bf16[2048,128]{1,0:T(8,128)(2,1)S(1)}, u32[]{:S(2)}, u32[]{:S(2)}) collective-permute-start(bf16[2048,128]{1,0:T(8,128)(2,1)S(1)} %later.1), channel_id=1, source_target_pairs={{0,16},{8,24},{16,0},{24,8},{1,17},{9,25},{17,1},{25,9},{2,18},{10... | collective-permute-start | bytes 1572872 | tf_op jit(solution)/shard_map/ppermute | solution.py:297
  6.7 3.8 %collective-permute-start.2 = (f32[48,128]{1,0:T(8,128)S(1)}, f32[48,128]{1,0:T(8,128)S(1)}, u32[]{:S(2)}, u32[]{:S(2)}) collective-permute-start(f32[48,128]{1,0:T(8,128)S(1)} %get-tuple-element.18), channel_id=1, source_target_pairs={{0,1},{1,0},{2,3},{3,2},{4,5},{5,4},{6,7},{7,6},{8,9},{9,8},{10,11... | collective-permute-start | bytes 73736 | tf_op jit(solution)/shard_map/ppermute | solution.py:305
  8.2 3.9 %collective-permute-start.3 = (f32[48,128]{1,0:T(8,128)S(1)}, f32[48,128]{1,0:T(8,128)S(1)}, u32[]{:S(2)}, u32[]{:S(2)}) collective-permute-start(f32[48,128]{1,0:T(8,128)S(1)} %get-tuple-element.19), channel_id=1, source_target_pairs={{0,2},{1,3},{2,0},{3,1},{4,6},{5,7},{6,4},{7,5},{8,10},{9,11},{10,... | collective-permute-start | bytes 73736 | tf_op jit(solution)/shard_map/ppermute | solution.py:305
  9.8 4.7 %collective-permute-start.4 = (f32[48,128]{1,0:T(8,128)S(1)}, f32[48,128]{1,0:T(8,128)S(1)}, u32[]{:S(2)}, u32[]{:S(2)}) collective-permute-start(f32[48,128]{1,0:T(8,128)S(1)} %get-tuple-element.20), channel_id=1, source_target_pairs={{0,3},{1,2},{2,1},{3,0},{4,7},{5,6},{6,5},{7,4},{8,11},{9,10},{10,... | collective-permute-start | bytes 73736 | tf_op jit(solution)/shard_map/ppermute | solution.py:305
  14.6 4.9 %collective-permute-start.5 = (f32[48,128]{1,0:T(8,128)S(1)}, f32[48,128]{1,0:T(8,128)S(1)}, u32[]{:S(2)}, u32[]{:S(2)}) collective-permute-start(f32[48,128]{1,0:T(8,128)S(1)} %chip_sum.1.rest_0_), channel_id=1, source_target_pairs={{0,4},{1,5},{2,6},{3,7},{4,0},{5,1},{6,2},{7,3},{8,12},{9,13},{10,... | collective-permute-start | bytes 73736 | tf_op jit(solution)/shard_map/ppermute | solution.py:305
  20.1 4.4 %collective-permute-start.6 = (f32[112,128]{1,0:T(8,128)S(1)}, f32[112,128]{1,0:T(8,128)S(1)}, u32[]{:S(2)}, u32[]{:S(2)}) collective-permute-start(f32[112,128]{1,0:T(8,128)S(1)} %get-tuple-element.23), channel_id=1, source_target_pairs={{0,1},{1,0},{2,3},{3,2},{4,5},{5,4},{6,7},{7,6},{8,9},{9,8},{10,11... | collective-permute-start | bytes 172040 | tf_op jit(solution)/shard_map/ppermute | solution.py:305
  20.6 4.2 %collective-permute-start.7 = (f32[112,128]{1,0:T(8,128)S(1)}, f32[112,128]{1,0:T(8,128)S(1)}, u32[]{:S(2)}, u32[]{:S(2)}) collective-permute-start(f32[112,128]{1,0:T(8,128)S(1)} %get-tuple-element.24), channel_id=1, source_target_pairs={{0,2},{1,3},{2,0},{3,1},{4,6},{5,7},{6,4},{7,5},{8,10},{9,11},{10,... | collective-permute-start | bytes 172040 | tf_op jit(solution)/shard_map/ppermute | solution.py:305
  21.1 5.2 %collective-permute-start.8 = (f32[112,128]{1,0:T(8,128)S(1)}, f32[112,128]{1,0:T(8,128)S(1)}, u32[]{:S(2)}, u32[]{:S(2)}) collective-permute-start(f32[112,128]{1,0:T(8,128)S(1)} %get-tuple-element.25), channel_id=1, source_target_pairs={{0,3},{1,2},{2,1},{3,0},{4,7},{5,6},{6,5},{7,4},{8,11},{9,10},{10,... | collective-permute-start | bytes 172040 | tf_op jit(solution)/shard_map/ppermute | solution.py:305
  26.4 7.3 %collective-permute-start.11 = (f32[112,128]{1,0:T(8,128)S(1)}, f32[112,128]{1,0:T(8,128)S(1)}, u32[]{:S(2)}, u32[]{:S(2)}) collective-permute-start(f32[112,128]{1,0:T(8,128)S(1)} %get-tuple-element.27), channel_id=1, source_target_pairs={{0,20},{1,21},{2,30},{3,31},{4,16},{5,17},{6,26},{7,27},{8,28},{9,... | collective-permute-start | bytes 172040 | tf_op jit(solution)/shard_map/ppermute | solution.py:305
  29.8 5.1 %collective-permute-start.10 = (f32[112,128]{1,0:T(8,128)S(1)}, f32[112,128]{1,0:T(8,128)S(1)}, u32[]{:S(2)}, u32[]{:S(2)}) collective-permute-start(f32[112,128]{1,0:T(8,128)S(1)} %get-tuple-element.27), channel_id=1, source_target_pairs={{0,4},{1,5},{2,6},{3,7},{4,0},{5,1},{6,2},{7,3},{8,12},{9,13},{10,... | collective-permute-start | bytes 172040 | tf_op jit(solution)/shard_map/ppermute | solution.py:305
  30.2 4.8 %collective-permute-start.9 = (f32[112,128]{1,0:T(8,128)S(1)}, f32[112,128]{1,0:T(8,128)S(1)}, u32[]{:S(2)}, u32[]{:S(2)}) collective-permute-start(f32[112,128]{1,0:T(8,128)S(1)} %get-tuple-element.27), channel_id=1, source_target_pairs={{0,16},{1,17},{2,26},{3,27},{4,20},{5,21},{6,30},{7,31},{8,24},{9,... | collective-permute-start | bytes 172040 | tf_op jit(solution)/shard_map/ppermute | solution.py:305
  34.9 9.2 %collective-permute-start.16 = (bf16[2048,128]{1,0:T(8,128)(2,1)S(1)}, bf16[2048,128]{1,0:T(8,128)(2,1)S(1)}, u32[]{:S(2)}, u32[]{:S(2)}) collective-permute-start(bf16[2048,128]{1,0:T(8,128)(2,1)S(1)} %after.2), channel_id=1, source_target_pairs={{0,8},{8,0},{16,24},{24,16},{1,9},{9,1},{17,25},{25,17},{2,10},{10... | collective-permute-start | bytes 1572872 | tf_op jit(solution)/shard_map/ppermute | solution.py:297
  35.1 9.0 %collective-permute-start.18 = (bf16[2048,128]{1,0:T(8,128)(2,1)S(1)}, bf16[2048,128]{1,0:T(8,128)(2,1)S(1)}, u32[]{:S(2)}, u32[]{:S(2)}) collective-permute-start(bf16[2048,128]{1,0:T(8,128)(2,1)S(1)} %after.3), channel_id=1, source_target_pairs={{0,8},{8,0},{16,24},{24,16},{1,9},{9,1},{17,25},{25,17},{2,10},{10... | collective-permute-start | bytes 1572872 | tf_op jit(solution)/shard_map/ppermute | solution.py:297
  35.6 5.5 %collective-permute-start.14 = (f32[112,128]{1,0:T(8,128)S(1)}, f32[112,128]{1,0:T(8,128)S(1)}, u32[]{:S(2)}, u32[]{:S(2)}) collective-permute-start(f32[112,128]{1,0:T(8,128)S(1)} %pair_sum.1.own.after), channel_id=1, source_target_pairs={{0,3},{1,2},{2,1},{3,0},{4,7},{5,6},{6,5},{7,4},{8,11},{9,10},{10,... | collective-permute-start | bytes 172040 | tf_op jit(solution)/shard_map/ppermute | solution.py:305
  36.5 4.8 %collective-permute-start.13 = (f32[112,128]{1,0:T(8,128)S(1)}, f32[112,128]{1,0:T(8,128)S(1)}, u32[]{:S(2)}, u32[]{:S(2)}) collective-permute-start(f32[112,128]{1,0:T(8,128)S(1)} %pair_sum.1.own.after), channel_id=1, source_target_pairs={{0,2},{1,3},{2,0},{3,1},{4,6},{5,7},{6,4},{7,5},{8,10},{9,11},{10,... | collective-permute-start | bytes 172040 | tf_op jit(solution)/shard_map/ppermute | solution.py:305
  38.2 4.2 %collective-permute-start.12 = (f32[112,128]{1,0:T(8,128)S(1)}, f32[112,128]{1,0:T(8,128)S(1)}, u32[]{:S(2)}, u32[]{:S(2)}) collective-permute-start(f32[112,128]{1,0:T(8,128)S(1)} %pair_sum.1.own.after), channel_id=1, source_target_pairs={{0,1},{1,0},{2,3},{3,2},{4,5},{5,4},{6,7},{7,6},{8,9},{9,8},{10,11... | collective-permute-start | bytes 172040 | tf_op jit(solution)/shard_map/ppermute | solution.py:305
  42.4 1.7 %copy-start.1 = (s32[8]{0:T(128)S(1)}, s32[8]{0:T(128)}, u32[]{:S(2)}) copy-start(s32[8]{0:T(128)} %active.1) | copy-start | bytes 100
  42.4 1.7 %collective-permute-start.15 = (f32[640,128]{1,0:T(8,128)S(1)}, f32[640,128]{1,0:T(8,128)S(1)}, u32[]{:S(2)}, u32[]{:S(2)}) collective-permute-start(f32[640,128]{1,0:T(8,128)S(1)} %join.1.joined_mine), channel_id=1, source_target_pairs={{0,8},{8,0},{16,24},{24,16},{1,9},{9,1},{17,25},{25,17},{2,10},{10... | collective-permute-start | bytes 983048 | tf_op jit(solution)/shard_map/ppermute | solution.py:297

commit v8 on v7

--- a/solution.py
+++ b/solution.py
@@ -8,6 +8,8 @@
 from jax.sharding import PartitionSpec as P
 
 ITERS = 5
+PAIR_COST = 14 * 10**9
+JOIN_COST = 15 * 10**8
 F32 = jnp.float32
 BF16 = jnp.bfloat16
 VMEM = pl.BlockSpec(memory_space=pltpu.VMEM)
@@ -31,7 +33,7 @@
         scratch_shapes=list(scratch),
         input_output_aliases=aliases or {},
         compiler_params=pltpu.CompilerParams(vmem_limit_bytes=mib * 2**20),
-        cost_estimate=pl.CostEstimate(flops=0, bytes_accessed=0, transcendentals=0),
+        cost_estimate=pl.CostEstimate(flops=flops, bytes_accessed=0, transcendentals=0),
         name=name,
     )
 
@@ -329,7 +331,7 @@
     chip_parts = [chip_sum] + [move(chip_sum, bits) for bits in groups[1:]]
     pair, both = shape((size, width), F32), shape((size + quarter, width), F32)
     chip_piece, keep, *sends = call(
-        pair_gram_kernel, (small, pair, both, both, both), 3 + len(chip_parts), 0, "pair_gram",
+        pair_gram_kernel, (small, pair, both, both, both), 3 + len(chip_parts), PAIR_COST, "pair_gram",
         scratch=[pltpu.VMEM((4 * size, width), F32)],
     )(vectors, mate, across1, *chip_parts)
     parts = [move(sends[step - 1], step) for step in (3, 2, 1)][::-1]
@@ -341,7 +343,7 @@
     parts = [move(pieces, step) for step in (1, 2, 3)]
     mate2 = swap(after(across2, pieces), 1)
     mate1 = swap(after(across1, pieces), 1)
-    joined_mine = call(join_kernel, shape((4 * (size + 2 * quarter), width), F32), 5, 0, "join")(
+    joined_mine = call(join_kernel, shape((4 * (size + 2 * quarter), width), F32), 5, JOIN_COST, "join")(
         pieces, *parts, chip_slab
     )
     joined_mate = swap(joined_mine, 1)
@@ -350,7 +352,7 @@
         functools.partial(finish_kernel, float(total_rows)),
         shape((rows, width), BF16),
         0,
-        12 * cols**3 * 3 + 2 * rows * cols * width,
+        0,
         "finish",
         scratch=[
             pltpu.VMEM((cols, cols), F32),

time: 53.8 us -> 52.6 us (0.978)
  waiting for transfers between devices: 18.1 us -> 17.1 us
    ppermute x13, waiting for transfers between devices: 16.5 us -> 15.5 us  [move(): return lax.ppermute(value, ('state', 'row'), pairs)]
  transfers between devices with their start and end apart: 19 -> 19, of which waited for: 13 -> 12; matrix products, arithmetic and copies ran while one was open for 2% -> 2% of each run, Pallas kernels for 3% -> 3%
where the time goes in v8:
time: 52.6 us; the launch traced here: 52.5 us
  starting transfers between devices  23.1 us (44%)
  waiting for transfers between devices  17.1 us (33%)
  Pallas kernels  11 us (21%)
  local copies, waits for them, and re-layouts  1.15 us (2%)
    ppermute x13, starting transfers between devices, move(): return lax.ppermute(value, ('state', 'row'), pairs)  17.8 us
    ppermute x13, waiting for transfers between devices, move(): return lax.ppermute(value, ('state', 'row'), pairs)  15.5 us
    pallas_call x1, Pallas kernels, shards(): call(functools.partial(finish_kernel, float(total_rows)), shape((rows, wi...  9.56 us
    ppermute x6, starting transfers between devices, swap(): lax.ppermute(value, 'state', [(index, index ^ bit) for index in range(4)])  5.28 us
    ppermute x6, waiting for transfers between devices, swap(): lax.ppermute(value, 'state', [(index, index ^ bit) for index in range(4)])  1.63 us
    dynamic_slice x1, local copies, waits for them, and re-layouts, shards(): lax.dynamic_slice_in_dim(vectors, (1 - chip) * half, half, 0)  1.08 us
  transfers between devices with their start and end apart: 19, of which 12 were waited for; matrix products, arithmetic and copies ran while one was open for 2% of the time, Pallas kernels for 3%

profile of v8, /device:TPU:0, one launch (start us, length us, event | category | flops | bytes accessed | tf_op | source)
XLA Modules:
  0.0 52.5 jit_solution(12647970398129399568)
XLA Ops:
  0.0 0.0 copy-start
  0.0 0.5 collective-permute-start
  0.5 1.1 %constant_dynamic-slice_fusion = bf16[2048,128]{1,0:T(8,128)(2,1)S(1)} fusion(bf16[4096,128]{1,0:T(8,128)(2,1)} %own.7, s32[]{:T(128)S(6)} %select_n.9), kind=kLoop, calls=%fused_computation | loop fusion | bytes 1048580 | tf_op jit(solution)/shard_map/dynamic_slice | solution.py:315
  1.5 2.6 %collective-permute-start.1 = (bf16[2048,128]{1,0:T(8,128)(2,1)S(1)}, bf16[2048,128]{1,0:T(8,128)(2,1)S(1)}, u32[]{:S(2)}, u32[]{:S(2)}) collective-permute-start(bf16[2048,128]{1,0:T(8,128)(2,1)S(1)} %constant_dynamic-slice_fusion), channel_id=1, source_target_pairs={{0,16},{8,24},{16,0},{24,8},{1,17},{9,25},{17,1},{25,9},{2,18},{10... | collective-permute-start | bytes 1572872 | tf_op jit(solution)/shard_map/ppermute | solution.py:299
  4.2 0.0 collective-permute-done.mate
  4.2 0.0 copy-done
  4.2 0.8 %chip_gram.1 = (f32[48,128]{1,0:T(8,128)S(1)}, f32[48,128]{1,0:T(8,128)S(1)}, f32[48,128]{1,0:T(8,128)S(1)}, f32[48,128]{1,0:T(8,128)S(1)}) custom-call(bf16[4096,128]{1,0:T(8,128)(2,1)S(1)} %copy-done, bf16[4096,128]{1,0:T(8,128)(2,1)S(1)} %collective-permute-done.mate), custom_call_target="tpu_custom_call" | custom-call | tf_op jit(solution)/shard_map/chip_gram/pallas_call | solution.py:319
  4.9 1.7 %collective-permute-start.2 = (f32[48,128]{1,0:T(8,128)S(1)}, f32[48,128]{1,0:T(8,128)S(1)}, u32[]{:S(2)}, u32[]{:S(2)}) collective-permute-start(f32[48,128]{1,0:T(8,128)S(1)} %get-tuple-element.18), channel_id=1, source_target_pairs={{0,1},{1,0},{2,3},{3,2},{4,5},{5,4},{6,7},{7,6},{8,9},{9,8},{10,11... | collective-permute-start | bytes 73736 | tf_op jit(solution)/shard_map/ppermute | solution.py:307
  6.7 1.6 %collective-permute-start.3 = (f32[48,128]{1,0:T(8,128)S(1)}, f32[48,128]{1,0:T(8,128)S(1)}, u32[]{:S(2)}, u32[]{:S(2)}) collective-permute-start(f32[48,128]{1,0:T(8,128)S(1)} %get-tuple-element.19), channel_id=1, source_target_pairs={{0,2},{1,3},{2,0},{3,1},{4,6},{5,7},{6,4},{7,5},{8,10},{9,11},{10,... | collective-permute-start | bytes 73736 | tf_op jit(solution)/shard_map/ppermute | solution.py:307
  8.2 0.3 collective-permute-start.4
  8.6 0.3 collective-permute-done.2.part1
  8.8 1.8 %collective-permute-done.3.part2 = f32[48,128]{1,0:T(8,128)S(1)} collective-permute-done((f32[48,128]{1,0:T(8,128)S(1)}, f32[48,128]{1,0:T(8,128)S(1)}, u32[]{:S(2)}, u32[]{:S(2)}) %collective-permute-start.3) | collective-permute-done | bytes 24608 | tf_op jit(solution)/shard_map/ppermute | solution.py:307
  10.6 2.3 %collective-permute-done.4.part3 = f32[48,128]{1,0:T(8,128)S(1)} collective-permute-done((f32[48,128]{1,0:T(8,128)S(1)}, f32[48,128]{1,0:T(8,128)S(1)}, u32[]{:S(2)}, u32[]{:S(2)}) %collective-permute-start.4) | collective-permute-done | bytes 24608 | tf_op jit(solution)/shard_map/ppermute | solution.py:307
  13.0 2.7 %collective-permute-start.5 = (f32[48,128]{1,0:T(8,128)S(1)}, f32[48,128]{1,0:T(8,128)S(1)}, u32[]{:S(2)}, u32[]{:S(2)}) collective-permute-start(f32[48,128]{1,0:T(8,128)S(1)} %chip_sum.1.rest_0_), channel_id=1, source_target_pairs={{0,4},{1,5},{2,6},{3,7},{4,0},{5,1},{6,2},{7,3},{8,12},{9,13},{10,... | collective-permute-start | bytes 73736 | tf_op jit(solution)/shard_map/ppermute | solution.py:307
  15.7 1.5 %collective-permute-start.17 = (bf16[2048,128]{1,0:T(8,128)(2,1)S(1)}, bf16[2048,128]{1,0:T(8,128)(2,1)S(1)}, u32[]{:S(2)}, u32[]{:S(2)}) collective-permute-start(bf16[2048,128]{1,0:T(8,128)(2,1)S(1)} %later.1), channel_id=1, source_target_pairs={{0,16},{8,24},{16,0},{24,8},{1,17},{9,25},{17,1},{25,9},{2,18},{10... | collective-permute-start | bytes 1572872 | tf_op jit(solution)/shard_map/ppermute | solution.py:299
  17.2 0.0 collective-permute-done.1.across.across1
  17.2 0.7 %collective-permute-done.5.rest_1_ = f32[48,128]{1,0:T(8,128)S(1)} collective-permute-done((f32[48,128]{1,0:T(8,128)S(1)}, f32[48,128]{1,0:T(8,128)S(1)}, u32[]{:S(2)}, u32[]{:S(2)}) %collective-permute-start.5) | collective-permute-done | bytes 24608 | tf_op jit(solution)/shard_map/ppermute | solution.py:307
  17.9 0.6 %pair_gram.1 = (f32[48,128]{1,0:T(8,128)S(1)}, f32[64,128]{1,0:T(8,128)S(1)}, f32[112,128]{1,0:T(8,128)S(1)}, f32[112,128]{1,0:T(8,128)S(1)}, f32[112,128]{1,0:T(8,128)S(1)}) custom-call(bf16[4096,128]{1,0:T(8,128)(2,1)S(1)} %copy-done, bf16[4096,128]{1,0:T(8,128)(2,1)S(1)} %collective-permute-done.mate, ...), custom_call_target="tpu_custom_call" | custom-call | flops 14000000000 | tf_op jit(solution)/shard_map/pair_gram/pallas_call | solution.py:333
  18.5 1.1 %collective-permute-start.6 = (f32[112,128]{1,0:T(8,128)S(1)}, f32[112,128]{1,0:T(8,128)S(1)}, u32[]{:S(2)}, u32[]{:S(2)}) collective-permute-start(f32[112,128]{1,0:T(8,128)S(1)} %get-tuple-element.23), channel_id=1, source_target_pairs={{0,1},{1,0},{2,3},{3,2},{4,5},{5,4},{6,7},{7,6},{8,9},{9,8},{10,11... | collective-permute-start | bytes 172040 | tf_op jit(solution)/shard_map/ppermute | solution.py:307
  19.6 1.6 %collective-permute-start.7 = (f32[112,128]{1,0:T(8,128)S(1)}, f32[112,128]{1,0:T(8,128)S(1)}, u32[]{:S(2)}, u32[]{:S(2)}) collective-permute-start(f32[112,128]{1,0:T(8,128)S(1)} %get-tuple-element.24), channel_id=1, source_target_pairs={{0,2},{1,3},{2,0},{3,1},{4,6},{5,7},{6,4},{7,5},{8,10},{9,11},{10,... | collective-permute-start | bytes 172040 | tf_op jit(solution)/shard_map/ppermute | solution.py:307
  21.1 0.9 %collective-permute-start.8 = (f32[112,128]{1,0:T(8,128)S(1)}, f32[112,128]{1,0:T(8,128)S(1)}, u32[]{:S(2)}, u32[]{:S(2)}) collective-permute-start(f32[112,128]{1,0:T(8,128)S(1)} %get-tuple-element.25), channel_id=1, source_target_pairs={{0,3},{1,2},{2,1},{3,0},{4,7},{5,6},{6,5},{7,4},{8,11},{9,10},{10,... | collective-permute-start | bytes 172040 | tf_op jit(solution)/shard_map/ppermute | solution.py:307
  22.0 0.7 %collective-permute-done.6.part1 = f32[112,128]{1,0:T(8,128)S(1)} collective-permute-done((f32[112,128]{1,0:T(8,128)S(1)}, f32[112,128]{1,0:T(8,128)S(1)}, u32[]{:S(2)}, u32[]{:S(2)}) %collective-permute-start.6) | collective-permute-done | bytes 57376 | tf_op jit(solution)/shard_map/ppermute | solution.py:307
  22.7 1.0 %collective-permute-done.7.part2 = f32[112,128]{1,0:T(8,128)S(1)} collective-permute-done((f32[112,128]{1,0:T(8,128)S(1)}, f32[112,128]{1,0:T(8,128)S(1)}, u32[]{:S(2)}, u32[]{:S(2)}) %collective-permute-start.7) | collective-permute-done | bytes 57376 | tf_op jit(solution)/shard_map/ppermute | solution.py:307
  23.7 2.5 %collective-permute-done.8.part3 = f32[112,128]{1,0:T(8,128)S(1)} collective-permute-done((f32[112,128]{1,0:T(8,128)S(1)}, f32[112,128]{1,0:T(8,128)S(1)}, u32[]{:S(2)}, u32[]{:S(2)}) %collective-permute-start.8) | collective-permute-done | bytes 57376 | tf_op jit(solution)/shard_map/ppermute | solution.py:307
  26.2 3.6 %collective-permute-start.11 = (f32[112,128]{1,0:T(8,128)S(1)}, f32[112,128]{1,0:T(8,128)S(1)}, u32[]{:S(2)}, u32[]{:S(2)}) collective-permute-start(f32[112,128]{1,0:T(8,128)S(1)} %get-tuple-element.27), channel_id=1, source_target_pairs={{0,20},{1,21},{2,30},{3,31},{4,16},{5,17},{6,26},{7,27},{8,28},{9,... | collective-permute-start | bytes 172040 | tf_op jit(solution)/shard_map/ppermute | solution.py:307
  29.8 0.3 collective-permute-start.10
  30.2 0.5 %collective-permute-start.9 = (f32[112,128]{1,0:T(8,128)S(1)}, f32[112,128]{1,0:T(8,128)S(1)}, u32[]{:S(2)}, u32[]{:S(2)}) collective-permute-start(f32[112,128]{1,0:T(8,128)S(1)} %get-tuple-element.27), channel_id=1, source_target_pairs={{0,16},{1,17},{2,26},{3,27},{4,20},{5,21},{6,30},{7,31},{8,24},{9,... | collective-permute-start | bytes 172040 | tf_op jit(solution)/shard_map/ppermute | solution.py:307
  30.7 4.0 %collective-permute-done.11.rest_1_ = f32[112,128]{1,0:T(8,128)S(1)} collective-permute-done((f32[112,128]{1,0:T(8,128)S(1)}, f32[112,128]{1,0:T(8,128)S(1)}, u32[]{:S(2)}, u32[]{:S(2)}) %collective-permute-start.11) | collective-permute-done | bytes 57376 | tf_op jit(solution)/shard_map/ppermute | solution.py:307
  34.7 0.3 collective-permute-done.10.rest_0_
  34.9 0.0 collective-permute-done.9.across
  34.9 0.1 collective-permute-start.14
  35.0 2.0 %collective-permute-start.13 = (f32[112,128]{1,0:T(8,128)S(1)}, f32[112,128]{1,0:T(8,128)S(1)}, u32[]{:S(2)}, u32[]{:S(2)}) collective-permute-start(f32[112,128]{1,0:T(8,128)S(1)} %pair_sum.1.own.after), channel_id=1, source_target_pairs={{0,2},{1,3},{2,0},{3,1},{4,6},{5,7},{6,4},{7,5},{8,10},{9,11},{10,... | collective-permute-start | bytes 172040 | tf_op jit(solution)/shard_map/ppermute | solution.py:307
  37.0 1.5 %collective-permute-start.12 = (f32[112,128]{1,0:T(8,128)S(1)}, f32[112,128]{1,0:T(8,128)S(1)}, u32[]{:S(2)}, u32[]{:S(2)}) collective-permute-start(f32[112,128]{1,0:T(8,128)S(1)} %pair_sum.1.own.after), channel_id=1, source_target_pairs={{0,1},{1,0},{2,3},{3,2},{4,5},{5,4},{6,7},{7,6},{8,9},{9,8},{10,11... | collective-permute-start | bytes 172040 | tf_op jit(solution)/shard_map/ppermute | solution.py:307
  38.5 0.1 collective-permute-start.16
  38.6 0.0 collective-permute-done.17.across2
  38.7 0.6 %collective-permute-start.18 = (bf16[2048,128]{1,0:T(8,128)(2,1)S(1)}, bf16[2048,128]{1,0:T(8,128)(2,1)S(1)}, u32[]{:S(2)}, u32[]{:S(2)}) collective-permute-start(bf16[2048,128]{1,0:T(8,128)(2,1)S(1)} %after.3), channel_id=1, source_target_pairs={{0,8},{8,0},{16,24},{24,16},{1,9},{9,1},{17,25},{25,17},{2,10},{10... | collective-permute-start | bytes 1572872 | tf_op jit(solution)/shard_map/ppermute | solution.py:299
  39.2 0.8 %collective-permute-done.14.part3 = f32[112,128]{1,0:T(8,128)S(1)} collective-permute-done((f32[112,128]{1,0:T(8,128)S(1)}, f32[112,128]{1,0:T(8,128)S(1)}, u32[]{:S(2)}, u32[]{:S(2)}) %collective-permute-start.14) | collective-permute-done | bytes 57376 | tf_op jit(solution)/shard_map/ppermute | solution.py:307
  40.1 0.0 collective-permute-done.13.part2
  40.1 1.1 %collective-permute-done.12.part1 = f32[112,128]{1,0:T(8,128)S(1)} collective-permute-done((f32[112,128]{1,0:T(8,128)S(1)}, f32[112,128]{1,0:T(8,128)S(1)}, u32[]{:S(2)}, u32[]{:S(2)}) %collective-permute-start.12) | collective-permute-done | bytes 57376 | tf_op jit(solution)/shard_map/ppermute | solution.py:307
  41.2 0.0 copy-start.1
  41.2 0.1 collective-permute-start.15
  41.3 1.6 %collective-permute-done.15.joined_mate = f32[640,128]{1,0:T(8,128)S(1)} collective-permute-done((f32[640,128]{1,0:T(8,128)S(1)}, f32[640,128]{1,0:T(8,128)S(1)}, u32[]{:S(2)}, u32[]{:S(2)}) %collective-permute-start.15) | collective-permute-done | bytes 327712 | tf_op jit(solution)/shard_map/ppermute | solution.py:299
  42.9 0.0 collective-permute-done.16.mate1
  42.9 0.0 collective-permute-done.18.mate2
  42.9 0.0 copy-done.1
  42.9 9.6 %finish.1 = bf16[4096,128]{1,0:T(8,128)(2,1)} custom-call(s32[8]{0:T(128)S(1)} %copy-done.1, f32[640,128]{1,0:T(8,128)S(1)} %join.1.joined_mine, f32[640,128]{1,0:T(8,128)S(1)} %collective-permute-done.15.joined_mate, bf16[4096,128]{1,0:T(8,128)(2,1)S(1)} %copy-done, bf16[4096,128]{1,0:T(8,128)(2,1)S(1)} %collective-permute-done.mate, ...), custom_call_target="tpu_custom_call" | custom-call | tf_op jit(solution)/shard_map/finish/pallas_call | solution.py:351
  (9 shorter events, 0.2 us)
Async XLA Ops:
  0.0 4.2 %copy-start = (bf16[4096,128]{1,0:T(8,128)(2,1)S(1)}, bf16[4096,128]{1,0:T(8,128)(2,1)}, u32[]{:S(2)}) copy-start(bf16[4096,128]{1,0:T(8,128)(2,1)} %own.7) | copy-start | bytes 3145732
  0.0 4.2 %collective-permute-start = (bf16[4096,128]{1,0:T(8,128)(2,1)}, bf16[4096,128]{1,0:T(8,128)(2,1)S(1)}, u32[]{:S(2)}, u32[]{:S(2)}) collective-permute-start(bf16[4096,128]{1,0:T(8,128)(2,1)} %own.7), channel_id=1, source_target_pairs={{0,8},{8,0},{16,24},{24,16},{1,9},{9,1},{17,25},{25,17},{2,10},{10... | collective-permute-start | bytes 3145736 | tf_op jit(solution)/shard_map/ppermute | solution.py:299
  1.5 15.7 %collective-permute-start.1 = (bf16[2048,128]{1,0:T(8,128)(2,1)S(1)}, bf16[2048,128]{1,0:T(8,128)(2,1)S(1)}, u32[]{:S(2)}, u32[]{:S(2)}) collective-permute-start(bf16[2048,128]{1,0:T(8,128)(2,1)S(1)} %constant_dynamic-slice_fusion), channel_id=1, source_target_pairs={{0,16},{8,24},{16,0},{24,8},{1,17},{9,25},{17,1},{25,9},{2,18},{10... | collective-permute-start | bytes 1572872 | tf_op jit(solution)/shard_map/ppermute | solution.py:299
  4.9 3.9 %collective-permute-start.2 = (f32[48,128]{1,0:T(8,128)S(1)}, f32[48,128]{1,0:T(8,128)S(1)}, u32[]{:S(2)}, u32[]{:S(2)}) collective-permute-start(f32[48,128]{1,0:T(8,128)S(1)} %get-tuple-element.18), channel_id=1, source_target_pairs={{0,1},{1,0},{2,3},{3,2},{4,5},{5,4},{6,7},{7,6},{8,9},{9,8},{10,11... | collective-permute-start | bytes 73736 | tf_op jit(solution)/shard_map/ppermute | solution.py:307
  6.7 4.0 %collective-permute-start.3 = (f32[48,128]{1,0:T(8,128)S(1)}, f32[48,128]{1,0:T(8,128)S(1)}, u32[]{:S(2)}, u32[]{:S(2)}) collective-permute-start(f32[48,128]{1,0:T(8,128)S(1)} %get-tuple-element.19), channel_id=1, source_target_pairs={{0,2},{1,3},{2,0},{3,1},{4,6},{5,7},{6,4},{7,5},{8,10},{9,11},{10,... | collective-permute-start | bytes 73736 | tf_op jit(solution)/shard_map/ppermute | solution.py:307
  8.2 4.7 %collective-permute-start.4 = (f32[48,128]{1,0:T(8,128)S(1)}, f32[48,128]{1,0:T(8,128)S(1)}, u32[]{:S(2)}, u32[]{:S(2)}) collective-permute-start(f32[48,128]{1,0:T(8,128)S(1)} %get-tuple-element.20), channel_id=1, source_target_pairs={{0,3},{1,2},{2,1},{3,0},{4,7},{5,6},{6,5},{7,4},{8,11},{9,10},{10,... | collective-permute-start | bytes 73736 | tf_op jit(solution)/shard_map/ppermute | solution.py:307
  13.0 4.9 %collective-permute-start.5 = (f32[48,128]{1,0:T(8,128)S(1)}, f32[48,128]{1,0:T(8,128)S(1)}, u32[]{:S(2)}, u32[]{:S(2)}) collective-permute-start(f32[48,128]{1,0:T(8,128)S(1)} %chip_sum.1.rest_0_), channel_id=1, source_target_pairs={{0,4},{1,5},{2,6},{3,7},{4,0},{5,1},{6,2},{7,3},{8,12},{9,13},{10,... | collective-permute-start | bytes 73736 | tf_op jit(solution)/shard_map/ppermute | solution.py:307
  15.7 22.9 %collective-permute-start.17 = (bf16[2048,128]{1,0:T(8,128)(2,1)S(1)}, bf16[2048,128]{1,0:T(8,128)(2,1)S(1)}, u32[]{:S(2)}, u32[]{:S(2)}) collective-permute-start(bf16[2048,128]{1,0:T(8,128)(2,1)S(1)} %later.1), channel_id=1, source_target_pairs={{0,16},{8,24},{16,0},{24,8},{1,17},{9,25},{17,1},{25,9},{2,18},{10... | collective-permute-start | bytes 1572872 | tf_op jit(solution)/shard_map/ppermute | solution.py:299
  18.5 4.2 %collective-permute-start.6 = (f32[112,128]{1,0:T(8,128)S(1)}, f32[112,128]{1,0:T(8,128)S(1)}, u32[]{:S(2)}, u32[]{:S(2)}) collective-permute-start(f32[112,128]{1,0:T(8,128)S(1)} %get-tuple-element.23), channel_id=1, source_target_pairs={{0,1},{1,0},{2,3},{3,2},{4,5},{5,4},{6,7},{7,6},{8,9},{9,8},{10,11... | collective-permute-start | bytes 172040 | tf_op jit(solution)/shard_map/ppermute | solution.py:307
  19.6 4.2 %collective-permute-start.7 = (f32[112,128]{1,0:T(8,128)S(1)}, f32[112,128]{1,0:T(8,128)S(1)}, u32[]{:S(2)}, u32[]{:S(2)}) collective-permute-start(f32[112,128]{1,0:T(8,128)S(1)} %get-tuple-element.24), channel_id=1, source_target_pairs={{0,2},{1,3},{2,0},{3,1},{4,6},{5,7},{6,4},{7,5},{8,10},{9,11},{10,... | collective-permute-start | bytes 172040 | tf_op jit(solution)/shard_map/ppermute | solution.py:307
  21.1 5.1 %collective-permute-start.8 = (f32[112,128]{1,0:T(8,128)S(1)}, f32[112,128]{1,0:T(8,128)S(1)}, u32[]{:S(2)}, u32[]{:S(2)}) collective-permute-start(f32[112,128]{1,0:T(8,128)S(1)} %get-tuple-element.25), channel_id=1, source_target_pairs={{0,3},{1,2},{2,1},{3,0},{4,7},{5,6},{6,5},{7,4},{8,11},{9,10},{10,... | collective-permute-start | bytes 172040 | tf_op jit(solution)/shard_map/ppermute | solution.py:307
  26.2 8.4 %collective-permute-start.11 = (f32[112,128]{1,0:T(8,128)S(1)}, f32[112,128]{1,0:T(8,128)S(1)}, u32[]{:S(2)}, u32[]{:S(2)}) collective-permute-start(f32[112,128]{1,0:T(8,128)S(1)} %get-tuple-element.27), channel_id=1, source_target_pairs={{0,20},{1,21},{2,30},{3,31},{4,16},{5,17},{6,26},{7,27},{8,28},{9,... | collective-permute-start | bytes 172040 | tf_op jit(solution)/shard_map/ppermute | solution.py:307
  29.8 5.1 %collective-permute-start.10 = (f32[112,128]{1,0:T(8,128)S(1)}, f32[112,128]{1,0:T(8,128)S(1)}, u32[]{:S(2)}, u32[]{:S(2)}) collective-permute-start(f32[112,128]{1,0:T(8,128)S(1)} %get-tuple-element.27), channel_id=1, source_target_pairs={{0,4},{1,5},{2,6},{3,7},{4,0},{5,1},{6,2},{7,3},{8,12},{9,13},{10,... | collective-permute-start | bytes 172040 | tf_op jit(solution)/shard_map/ppermute | solution.py:307
  30.2 4.7 %collective-permute-start.9 = (f32[112,128]{1,0:T(8,128)S(1)}, f32[112,128]{1,0:T(8,128)S(1)}, u32[]{:S(2)}, u32[]{:S(2)}) collective-permute-start(f32[112,128]{1,0:T(8,128)S(1)} %get-tuple-element.27), channel_id=1, source_target_pairs={{0,16},{1,17},{2,26},{3,27},{4,20},{5,21},{6,30},{7,31},{8,24},{9,... | collective-permute-start | bytes 172040 | tf_op jit(solution)/shard_map/ppermute | solution.py:307
  34.9 5.1 %collective-permute-start.14 = (f32[112,128]{1,0:T(8,128)S(1)}, f32[112,128]{1,0:T(8,128)S(1)}, u32[]{:S(2)}, u32[]{:S(2)}) collective-permute-start(f32[112,128]{1,0:T(8,128)S(1)} %pair_sum.1.own.after), channel_id=1, source_target_pairs={{0,3},{1,2},{2,1},{3,0},{4,7},{5,6},{6,5},{7,4},{8,11},{9,10},{10,... | collective-permute-start | bytes 172040 | tf_op jit(solution)/shard_map/ppermute | solution.py:307
  35.0 5.1 %collective-permute-start.13 = (f32[112,128]{1,0:T(8,128)S(1)}, f32[112,128]{1,0:T(8,128)S(1)}, u32[]{:S(2)}, u32[]{:S(2)}) collective-permute-start(f32[112,128]{1,0:T(8,128)S(1)} %pair_sum.1.own.after), channel_id=1, source_target_pairs={{0,2},{1,3},{2,0},{3,1},{4,6},{5,7},{6,4},{7,5},{8,10},{9,11},{10,... | collective-permute-start | bytes 172040 | tf_op jit(solution)/shard_map/ppermute | solution.py:307
  37.0 4.2 %collective-permute-start.12 = (f32[112,128]{1,0:T(8,128)S(1)}, f32[112,128]{1,0:T(8,128)S(1)}, u32[]{:S(2)}, u32[]{:S(2)}) collective-permute-start(f32[112,128]{1,0:T(8,128)S(1)} %pair_sum.1.own.after), channel_id=1, source_target_pairs={{0,1},{1,0},{2,3},{3,2},{4,5},{5,4},{6,7},{7,6},{8,9},{9,8},{10,11... | collective-permute-start | bytes 172040 | tf_op jit(solution)/shard_map/ppermute | solution.py:307
  38.5 4.4 %collective-permute-start.16 = (bf16[2048,128]{1,0:T(8,128)(2,1)S(1)}, bf16[2048,128]{1,0:T(8,128)(2,1)S(1)}, u32[]{:S(2)}, u32[]{:S(2)}) collective-permute-start(bf16[2048,128]{1,0:T(8,128)(2,1)S(1)} %after.2), channel_id=1, source_target_pairs={{0,8},{8,0},{16,24},{24,16},{1,9},{9,1},{17,25},{25,17},{2,10},{10... | collective-permute-start | bytes 1572872 | tf_op jit(solution)/shard_map/ppermute | solution.py:299
  38.7 4.3 %collective-permute-start.18 = (bf16[2048,128]{1,0:T(8,128)(2,1)S(1)}, bf16[2048,128]{1,0:T(8,128)(2,1)S(1)}, u32[]{:S(2)}, u32[]{:S(2)}) collective-permute-start(bf16[2048,128]{1,0:T(8,128)(2,1)S(1)} %after.3), channel_id=1, source_target_pairs={{0,8},{8,0},{16,24},{24,16},{1,9},{9,1},{17,25},{25,17},{2,10},{10... | collective-permute-start | bytes 1572872 | tf_op jit(solution)/shard_map/ppermute | solution.py:299
  41.2 1.7 %copy-start.1 = (s32[8]{0:T(128)S(1)}, s32[8]{0:T(128)}, u32[]{:S(2)}) copy-start(s32[8]{0:T(128)} %active.1) | copy-start | bytes 100
  41.2 1.7 %collective-permute-start.15 = (f32[640,128]{1,0:T(8,128)S(1)}, f32[640,128]{1,0:T(8,128)S(1)}, u32[]{:S(2)}, u32[]{:S(2)}) collective-permute-start(f32[640,128]{1,0:T(8,128)S(1)} %join.1.joined_mine), channel_id=1, source_target_pairs={{0,8},{8,0},{16,24},{24,16},{1,9},{9,1},{17,25},{25,17},{2,10},{10... | collective-permute-start | bytes 983048 | tf_op jit(solution)/shard_map/ppermute | solution.py:299

commit v9 on v8

--- a/solution.py
+++ b/solution.py
@@ -69,8 +69,9 @@
     core = core_index()
     width = own.shape[1]
     size = keep.shape[0]
-    between = cross(own[...], mate[...])
-    slab[0:width, :] = cross(own[...], own[...])
+    both = cross(own[...], jnp.concatenate([own[...], mate[...]], axis=1))
+    between = both[:, width:]
+    slab[0:width, :] = both[:, :width]
     slab[width:, :] = jnp.where(core == 0, between[: width // 2, :], between.T[width // 2 :, :])
     for step, out in enumerate((keep, send1, send2, send3)):
         out[...] = slab[piece(step, size), :]
@@ -87,8 +88,8 @@
     half, width = across.shape
     size = keep.shape[0]
     rows = pl.ds(pl.multiple_of(chip * half, half), half)
-    same = cross(across[...], own[rows, :])
-    other = cross(across[...], mate[rows, :])
+    both = cross(across[...], jnp.concatenate([own[rows, :], mate[rows, :]], axis=1))
+    same, other = both[:, :width], both[:, width:]
     slab[0:width, :] = jnp.where(chip == 0, same.T, same)
     slab[width : 2 * width, :] = jnp.where(chip == 0, other.T, other)
     chip_sum = tree_sum([part[...] for part in chip_parts])

time: 52.6 us -> 52.5 us (level)
  transfers between devices with their start and end apart: 19 -> 19, of which waited for: 12 -> 12; matrix products, arithmetic and copies ran while one was open for 2% -> 2% of each run, Pallas kernels for 3% -> 2%
where the time goes in v9:
time: 52.5 us; the launch traced here: 52.3 us
  starting transfers between devices  23.1 us (44%)
  waiting for transfers between devices  17.3 us (33%)
  Pallas kernels  10.7 us (20%)
  local copies, waits for them, and re-layouts  1.15 us (2%)
    ppermute x13, starting transfers between devices, move(): return lax.ppermute(value, ('state', 'row'), pairs)  17.8 us
    ppermute x13, waiting for transfers between devices, move(): return lax.ppermute(value, ('state', 'row'), pairs)  15.7 us
    pallas_call x1, Pallas kernels, shards(): call(functools.partial(finish_kernel, float(total_rows)), shape((rows, wi...  9.57 us
    ppermute x6, starting transfers between devices, swap(): lax.ppermute(value, 'state', [(index, index ^ bit) for index in range(4)])  5.28 us
    ppermute x6, waiting for transfers between devices, swap(): lax.ppermute(value, 'state', [(index, index ^ bit) for index in range(4)])  1.63 us
    dynamic_slice x1, local copies, waits for them, and re-layouts, shards(): lax.dynamic_slice_in_dim(vectors, (1 - chip) * half, half, 0)  1.08 us
  transfers between devices with their start and end apart: 19, of which 12 were waited for; matrix products, arithmetic and copies ran while one was open for 2% of the time, Pallas kernels for 2%

profile of v9, /device:TPU:0, one launch (start us, length us, event | category | flops | bytes accessed | tf_op | source)
XLA Modules:
  0.0 52.3 jit_solution(13588018481276462385)
XLA Ops:
  0.0 0.0 copy-start
  0.0 0.5 collective-permute-start
  0.5 1.1 %constant_dynamic-slice_fusion = bf16[2048,128]{1,0:T(8,128)(2,1)S(1)} fusion(bf16[4096,128]{1,0:T(8,128)(2,1)} %own.7, s32[]{:T(128)S(6)} %select_n.9), kind=kLoop, calls=%fused_computation | loop fusion | bytes 1048580 | tf_op jit(solution)/shard_map/dynamic_slice | solution.py:316
  1.5 2.6 %collective-permute-start.1 = (bf16[2048,128]{1,0:T(8,128)(2,1)S(1)}, bf16[2048,128]{1,0:T(8,128)(2,1)S(1)}, u32[]{:S(2)}, u32[]{:S(2)}) collective-permute-start(bf16[2048,128]{1,0:T(8,128)(2,1)S(1)} %constant_dynamic-slice_fusion), channel_id=1, source_target_pairs={{0,16},{8,24},{16,0},{24,8},{1,17},{9,25},{17,1},{25,9},{2,18},{10... | collective-permute-start | bytes 1572872 | tf_op jit(solution)/shard_map/ppermute | solution.py:300
  4.2 0.0 collective-permute-done.mate
  4.2 0.0 copy-done
  4.2 0.6 %chip_gram.1 = (f32[48,128]{1,0:T(8,128)S(1)}, f32[48,128]{1,0:T(8,128)S(1)}, f32[48,128]{1,0:T(8,128)S(1)}, f32[48,128]{1,0:T(8,128)S(1)}) custom-call(bf16[4096,128]{1,0:T(8,128)(2,1)S(1)} %copy-done, bf16[4096,128]{1,0:T(8,128)(2,1)S(1)} %collective-permute-done.mate), custom_call_target="tpu_custom_call" | custom-call | tf_op jit(solution)/shard_map/chip_gram/pallas_call | solution.py:320
  4.7 1.7 %collective-permute-start.2 = (f32[48,128]{1,0:T(8,128)S(1)}, f32[48,128]{1,0:T(8,128)S(1)}, u32[]{:S(2)}, u32[]{:S(2)}) collective-permute-start(f32[48,128]{1,0:T(8,128)S(1)} %get-tuple-element.18), channel_id=1, source_target_pairs={{0,1},{1,0},{2,3},{3,2},{4,5},{5,4},{6,7},{7,6},{8,9},{9,8},{10,11... | collective-permute-start | bytes 73736 | tf_op jit(solution)/shard_map/ppermute | solution.py:308
  6.5 1.6 %collective-permute-start.3 = (f32[48,128]{1,0:T(8,128)S(1)}, f32[48,128]{1,0:T(8,128)S(1)}, u32[]{:S(2)}, u32[]{:S(2)}) collective-permute-start(f32[48,128]{1,0:T(8,128)S(1)} %get-tuple-element.19), channel_id=1, source_target_pairs={{0,2},{1,3},{2,0},{3,1},{4,6},{5,7},{6,4},{7,5},{8,10},{9,11},{10,... | collective-permute-start | bytes 73736 | tf_op jit(solution)/shard_map/ppermute | solution.py:308
  8.1 0.3 collective-permute-start.4
  8.4 0.3 collective-permute-done.2.part1
  8.6 1.8 %collective-permute-done.3.part2 = f32[48,128]{1,0:T(8,128)S(1)} collective-permute-done((f32[48,128]{1,0:T(8,128)S(1)}, f32[48,128]{1,0:T(8,128)S(1)}, u32[]{:S(2)}, u32[]{:S(2)}) %collective-permute-start.3) | collective-permute-done | bytes 24608 | tf_op jit(solution)/shard_map/ppermute | solution.py:308
  10.4 2.3 %collective-permute-done.4.part3 = f32[48,128]{1,0:T(8,128)S(1)} collective-permute-done((f32[48,128]{1,0:T(8,128)S(1)}, f32[48,128]{1,0:T(8,128)S(1)}, u32[]{:S(2)}, u32[]{:S(2)}) %collective-permute-start.4) | collective-permute-done | bytes 24608 | tf_op jit(solution)/shard_map/ppermute | solution.py:308
  12.8 2.7 %collective-permute-start.5 = (f32[48,128]{1,0:T(8,128)S(1)}, f32[48,128]{1,0:T(8,128)S(1)}, u32[]{:S(2)}, u32[]{:S(2)}) collective-permute-start(f32[48,128]{1,0:T(8,128)S(1)} %chip_sum.1.rest_0_), channel_id=1, source_target_pairs={{0,4},{1,5},{2,6},{3,7},{4,0},{5,1},{6,2},{7,3},{8,12},{9,13},{10,... | collective-permute-start | bytes 73736 | tf_op jit(solution)/shard_map/ppermute | solution.py:308
  15.5 1.5 %collective-permute-start.17 = (bf16[2048,128]{1,0:T(8,128)(2,1)S(1)}, bf16[2048,128]{1,0:T(8,128)(2,1)S(1)}, u32[]{:S(2)}, u32[]{:S(2)}) collective-permute-start(bf16[2048,128]{1,0:T(8,128)(2,1)S(1)} %later.1), channel_id=1, source_target_pairs={{0,16},{8,24},{16,0},{24,8},{1,17},{9,25},{17,1},{25,9},{2,18},{10... | collective-permute-start | bytes 1572872 | tf_op jit(solution)/shard_map/ppermute | solution.py:300
  17.0 0.0 collective-permute-done.1.across.across1
  17.0 0.7 %collective-permute-done.5.rest_1_ = f32[48,128]{1,0:T(8,128)S(1)} collective-permute-done((f32[48,128]{1,0:T(8,128)S(1)}, f32[48,128]{1,0:T(8,128)S(1)}, u32[]{:S(2)}, u32[]{:S(2)}) %collective-permute-start.5) | collective-permute-done | bytes 24608 | tf_op jit(solution)/shard_map/ppermute | solution.py:308
  17.7 0.5 pair_gram.1
  18.2 1.3 %collective-permute-start.6 = (f32[112,128]{1,0:T(8,128)S(1)}, f32[112,128]{1,0:T(8,128)S(1)}, u32[]{:S(2)}, u32[]{:S(2)}) collective-permute-start(f32[112,128]{1,0:T(8,128)S(1)} %get-tuple-element.23), channel_id=1, source_target_pairs={{0,1},{1,0},{2,3},{3,2},{4,5},{5,4},{6,7},{7,6},{8,9},{9,8},{10,11... | collective-permute-start | bytes 172040 | tf_op jit(solution)/shard_map/ppermute | solution.py:308
  19.5 1.6 %collective-permute-start.7 = (f32[112,128]{1,0:T(8,128)S(1)}, f32[112,128]{1,0:T(8,128)S(1)}, u32[]{:S(2)}, u32[]{:S(2)}) collective-permute-start(f32[112,128]{1,0:T(8,128)S(1)} %get-tuple-element.24), channel_id=1, source_target_pairs={{0,2},{1,3},{2,0},{3,1},{4,6},{5,7},{6,4},{7,5},{8,10},{9,11},{10,... | collective-permute-start | bytes 172040 | tf_op jit(solution)/shard_map/ppermute | solution.py:308
  21.0 0.7 %collective-permute-start.8 = (f32[112,128]{1,0:T(8,128)S(1)}, f32[112,128]{1,0:T(8,128)S(1)}, u32[]{:S(2)}, u32[]{:S(2)}) collective-permute-start(f32[112,128]{1,0:T(8,128)S(1)} %get-tuple-element.25), channel_id=1, source_target_pairs={{0,3},{1,2},{2,1},{3,0},{4,7},{5,6},{6,5},{7,4},{8,11},{9,10},{10,... | collective-permute-start | bytes 172040 | tf_op jit(solution)/shard_map/ppermute | solution.py:308
  21.7 0.7 %collective-permute-done.6.part1 = f32[112,128]{1,0:T(8,128)S(1)} collective-permute-done((f32[112,128]{1,0:T(8,128)S(1)}, f32[112,128]{1,0:T(8,128)S(1)}, u32[]{:S(2)}, u32[]{:S(2)}) %collective-permute-start.6) | collective-permute-done | bytes 57376 | tf_op jit(solution)/shard_map/ppermute | solution.py:308
  22.4 1.2 %collective-permute-done.7.part2 = f32[112,128]{1,0:T(8,128)S(1)} collective-permute-done((f32[112,128]{1,0:T(8,128)S(1)}, f32[112,128]{1,0:T(8,128)S(1)}, u32[]{:S(2)}, u32[]{:S(2)}) %collective-permute-start.7) | collective-permute-done | bytes 57376 | tf_op jit(solution)/shard_map/ppermute | solution.py:308
  23.6 2.5 %collective-permute-done.8.part3 = f32[112,128]{1,0:T(8,128)S(1)} collective-permute-done((f32[112,128]{1,0:T(8,128)S(1)}, f32[112,128]{1,0:T(8,128)S(1)}, u32[]{:S(2)}, u32[]{:S(2)}) %collective-permute-start.8) | collective-permute-done | bytes 57376 | tf_op jit(solution)/shard_map/ppermute | solution.py:308
  26.1 3.6 %collective-permute-start.11 = (f32[112,128]{1,0:T(8,128)S(1)}, f32[112,128]{1,0:T(8,128)S(1)}, u32[]{:S(2)}, u32[]{:S(2)}) collective-permute-start(f32[112,128]{1,0:T(8,128)S(1)} %get-tuple-element.27), channel_id=1, source_target_pairs={{0,20},{1,21},{2,30},{3,31},{4,16},{5,17},{6,26},{7,27},{8,28},{9,... | collective-permute-start | bytes 172040 | tf_op jit(solution)/shard_map/ppermute | solution.py:308
  29.7 0.3 collective-permute-start.10
  30.1 0.5 %collective-permute-start.9 = (f32[112,128]{1,0:T(8,128)S(1)}, f32[112,128]{1,0:T(8,128)S(1)}, u32[]{:S(2)}, u32[]{:S(2)}) collective-permute-start(f32[112,128]{1,0:T(8,128)S(1)} %get-tuple-element.27), channel_id=1, source_target_pairs={{0,16},{1,17},{2,26},{3,27},{4,20},{5,21},{6,30},{7,31},{8,24},{9,... | collective-permute-start | bytes 172040 | tf_op jit(solution)/shard_map/ppermute | solution.py:308
  30.6 4.1 %collective-permute-done.11.rest_1_ = f32[112,128]{1,0:T(8,128)S(1)} collective-permute-done((f32[112,128]{1,0:T(8,128)S(1)}, f32[112,128]{1,0:T(8,128)S(1)}, u32[]{:S(2)}, u32[]{:S(2)}) %collective-permute-start.11) | collective-permute-done | bytes 57376 | tf_op jit(solution)/shard_map/ppermute | solution.py:308
  34.6 0.2 collective-permute-done.10.rest_0_
  34.8 0.0 collective-permute-done.9.across
  34.8 0.1 collective-permute-start.14
  34.9 2.0 %collective-permute-start.13 = (f32[112,128]{1,0:T(8,128)S(1)}, f32[112,128]{1,0:T(8,128)S(1)}, u32[]{:S(2)}, u32[]{:S(2)}) collective-permute-start(f32[112,128]{1,0:T(8,128)S(1)} %pair_sum.1.own.after), channel_id=1, source_target_pairs={{0,2},{1,3},{2,0},{3,1},{4,6},{5,7},{6,4},{7,5},{8,10},{9,11},{10,... | collective-permute-start | bytes 172040 | tf_op jit(solution)/shard_map/ppermute | solution.py:308
  36.9 1.5 %collective-permute-start.12 = (f32[112,128]{1,0:T(8,128)S(1)}, f32[112,128]{1,0:T(8,128)S(1)}, u32[]{:S(2)}, u32[]{:S(2)}) collective-permute-start(f32[112,128]{1,0:T(8,128)S(1)} %pair_sum.1.own.after), channel_id=1, source_target_pairs={{0,1},{1,0},{2,3},{3,2},{4,5},{5,4},{6,7},{7,6},{8,9},{9,8},{10,11... | collective-permute-start | bytes 172040 | tf_op jit(solution)/shard_map/ppermute | solution.py:308
  38.4 0.1 collective-permute-start.16
  38.5 0.0 collective-permute-done.17.across2
  38.6 0.6 %collective-permute-start.18 = (bf16[2048,128]{1,0:T(8,128)(2,1)S(1)}, bf16[2048,128]{1,0:T(8,128)(2,1)S(1)}, u32[]{:S(2)}, u32[]{:S(2)}) collective-permute-start(bf16[2048,128]{1,0:T(8,128)(2,1)S(1)} %after.3), channel_id=1, source_target_pairs={{0,8},{8,0},{16,24},{24,16},{1,9},{9,1},{17,25},{25,17},{2,10},{10... | collective-permute-start | bytes 1572872 | tf_op jit(solution)/shard_map/ppermute | solution.py:300
  39.1 0.8 %collective-permute-done.14.part3 = f32[112,128]{1,0:T(8,128)S(1)} collective-permute-done((f32[112,128]{1,0:T(8,128)S(1)}, f32[112,128]{1,0:T(8,128)S(1)}, u32[]{:S(2)}, u32[]{:S(2)}) %collective-permute-start.14) | collective-permute-done | bytes 57376 | tf_op jit(solution)/shard_map/ppermute | solution.py:308
  40.0 0.0 collective-permute-done.13.part2
  40.0 1.1 %collective-permute-done.12.part1 = f32[112,128]{1,0:T(8,128)S(1)} collective-permute-done((f32[112,128]{1,0:T(8,128)S(1)}, f32[112,128]{1,0:T(8,128)S(1)}, u32[]{:S(2)}, u32[]{:S(2)}) %collective-permute-start.12) | collective-permute-done | bytes 57376 | tf_op jit(solution)/shard_map/ppermute | solution.py:308
  41.0 0.0 copy-start.1
  41.1 0.1 collective-permute-start.15
  41.1 1.6 %collective-permute-done.15.joined_mate = f32[640,128]{1,0:T(8,128)S(1)} collective-permute-done((f32[640,128]{1,0:T(8,128)S(1)}, f32[640,128]{1,0:T(8,128)S(1)}, u32[]{:S(2)}, u32[]{:S(2)}) %collective-permute-start.15) | collective-permute-done | bytes 327712 | tf_op jit(solution)/shard_map/ppermute | solution.py:300
  42.8 0.0 collective-permute-done.16.mate1
  42.8 0.0 collective-permute-done.18.mate2
  42.8 0.0 copy-done.1
  42.8 9.6 %finish.1 = bf16[4096,128]{1,0:T(8,128)(2,1)} custom-call(s32[8]{0:T(128)S(1)} %copy-done.1, f32[640,128]{1,0:T(8,128)S(1)} %join.1.joined_mine, f32[640,128]{1,0:T(8,128)S(1)} %collective-permute-done.15.joined_mate, bf16[4096,128]{1,0:T(8,128)(2,1)S(1)} %copy-done, bf16[4096,128]{1,0:T(8,128)(2,1)S(1)} %collective-permute-done.mate, ...), custom_call_target="tpu_custom_call" | custom-call | tf_op jit(solution)/shard_map/finish/pallas_call | solution.py:352
  (9 shorter events, 0.2 us)
Async XLA Ops:
  0.0 4.2 %copy-start = (bf16[4096,128]{1,0:T(8,128)(2,1)S(1)}, bf16[4096,128]{1,0:T(8,128)(2,1)}, u32[]{:S(2)}) copy-start(bf16[4096,128]{1,0:T(8,128)(2,1)} %own.7) | copy-start | bytes 3145732
  0.0 4.2 %collective-permute-start = (bf16[4096,128]{1,0:T(8,128)(2,1)}, bf16[4096,128]{1,0:T(8,128)(2,1)S(1)}, u32[]{:S(2)}, u32[]{:S(2)}) collective-permute-start(bf16[4096,128]{1,0:T(8,128)(2,1)} %own.7), channel_id=1, source_target_pairs={{0,8},{8,0},{16,24},{24,16},{1,9},{9,1},{17,25},{25,17},{2,10},{10... | collective-permute-start | bytes 3145736 | tf_op jit(solution)/shard_map/ppermute | solution.py:300
  1.5 15.5 %collective-permute-start.1 = (bf16[2048,128]{1,0:T(8,128)(2,1)S(1)}, bf16[2048,128]{1,0:T(8,128)(2,1)S(1)}, u32[]{:S(2)}, u32[]{:S(2)}) collective-permute-start(bf16[2048,128]{1,0:T(8,128)(2,1)S(1)} %constant_dynamic-slice_fusion), channel_id=1, source_target_pairs={{0,16},{8,24},{16,0},{24,8},{1,17},{9,25},{17,1},{25,9},{2,18},{10... | collective-permute-start | bytes 1572872 | tf_op jit(solution)/shard_map/ppermute | solution.py:300
  4.7 3.9 %collective-permute-start.2 = (f32[48,128]{1,0:T(8,128)S(1)}, f32[48,128]{1,0:T(8,128)S(1)}, u32[]{:S(2)}, u32[]{:S(2)}) collective-permute-start(f32[48,128]{1,0:T(8,128)S(1)} %get-tuple-element.18), channel_id=1, source_target_pairs={{0,1},{1,0},{2,3},{3,2},{4,5},{5,4},{6,7},{7,6},{8,9},{9,8},{10,11... | collective-permute-start | bytes 73736 | tf_op jit(solution)/shard_map/ppermute | solution.py:308
  6.5 4.0 %collective-permute-start.3 = (f32[48,128]{1,0:T(8,128)S(1)}, f32[48,128]{1,0:T(8,128)S(1)}, u32[]{:S(2)}, u32[]{:S(2)}) collective-permute-start(f32[48,128]{1,0:T(8,128)S(1)} %get-tuple-element.19), channel_id=1, source_target_pairs={{0,2},{1,3},{2,0},{3,1},{4,6},{5,7},{6,4},{7,5},{8,10},{9,11},{10,... | collective-permute-start | bytes 73736 | tf_op jit(solution)/shard_map/ppermute | solution.py:308
  8.1 4.7 %collective-permute-start.4 = (f32[48,128]{1,0:T(8,128)S(1)}, f32[48,128]{1,0:T(8,128)S(1)}, u32[]{:S(2)}, u32[]{:S(2)}) collective-permute-start(f32[48,128]{1,0:T(8,128)S(1)} %get-tuple-element.20), channel_id=1, source_target_pairs={{0,3},{1,2},{2,1},{3,0},{4,7},{5,6},{6,5},{7,4},{8,11},{9,10},{10,... | collective-permute-start | bytes 73736 | tf_op jit(solution)/shard_map/ppermute | solution.py:308
  12.8 4.9 %collective-permute-start.5 = (f32[48,128]{1,0:T(8,128)S(1)}, f32[48,128]{1,0:T(8,128)S(1)}, u32[]{:S(2)}, u32[]{:S(2)}) collective-permute-start(f32[48,128]{1,0:T(8,128)S(1)} %chip_sum.1.rest_0_), channel_id=1, source_target_pairs={{0,4},{1,5},{2,6},{3,7},{4,0},{5,1},{6,2},{7,3},{8,12},{9,13},{10,... | collective-permute-start | bytes 73736 | tf_op jit(solution)/shard_map/ppermute | solution.py:308
  15.5 23.0 %collective-permute-start.17 = (bf16[2048,128]{1,0:T(8,128)(2,1)S(1)}, bf16[2048,128]{1,0:T(8,128)(2,1)S(1)}, u32[]{:S(2)}, u32[]{:S(2)}) collective-permute-start(bf16[2048,128]{1,0:T(8,128)(2,1)S(1)} %later.1), channel_id=1, source_target_pairs={{0,16},{8,24},{16,0},{24,8},{1,17},{9,25},{17,1},{25,9},{2,18},{10... | collective-permute-start | bytes 1572872 | tf_op jit(solution)/shard_map/ppermute | solution.py:300
  18.2 4.2 %collective-permute-start.6 = (f32[112,128]{1,0:T(8,128)S(1)}, f32[112,128]{1,0:T(8,128)S(1)}, u32[]{:S(2)}, u32[]{:S(2)}) collective-permute-start(f32[112,128]{1,0:T(8,128)S(1)} %get-tuple-element.23), channel_id=1, source_target_pairs={{0,1},{1,0},{2,3},{3,2},{4,5},{5,4},{6,7},{7,6},{8,9},{9,8},{10,11... | collective-permute-start | bytes 172040 | tf_op jit(solution)/shard_map/ppermute | solution.py:308
  19.5 4.2 %collective-permute-start.7 = (f32[112,128]{1,0:T(8,128)S(1)}, f32[112,128]{1,0:T(8,128)S(1)}, u32[]{:S(2)}, u32[]{:S(2)}) collective-permute-start(f32[112,128]{1,0:T(8,128)S(1)} %get-tuple-element.24), channel_id=1, source_target_pairs={{0,2},{1,3},{2,0},{3,1},{4,6},{5,7},{6,4},{7,5},{8,10},{9,11},{10,... | collective-permute-start | bytes 172040 | tf_op jit(solution)/shard_map/ppermute | solution.py:308
  21.0 5.1 %collective-permute-start.8 = (f32[112,128]{1,0:T(8,128)S(1)}, f32[112,128]{1,0:T(8,128)S(1)}, u32[]{:S(2)}, u32[]{:S(2)}) collective-permute-start(f32[112,128]{1,0:T(8,128)S(1)} %get-tuple-element.25), channel_id=1, source_target_pairs={{0,3},{1,2},{2,1},{3,0},{4,7},{5,6},{6,5},{7,4},{8,11},{9,10},{10,... | collective-permute-start | bytes 172040 | tf_op jit(solution)/shard_map/ppermute | solution.py:308
  26.1 8.5 %collective-permute-start.11 = (f32[112,128]{1,0:T(8,128)S(1)}, f32[112,128]{1,0:T(8,128)S(1)}, u32[]{:S(2)}, u32[]{:S(2)}) collective-permute-start(f32[112,128]{1,0:T(8,128)S(1)} %get-tuple-element.27), channel_id=1, source_target_pairs={{0,20},{1,21},{2,30},{3,31},{4,16},{5,17},{6,26},{7,27},{8,28},{9,... | collective-permute-start | bytes 172040 | tf_op jit(solution)/shard_map/ppermute | solution.py:308
  29.7 5.1 %collective-permute-start.10 = (f32[112,128]{1,0:T(8,128)S(1)}, f32[112,128]{1,0:T(8,128)S(1)}, u32[]{:S(2)}, u32[]{:S(2)}) collective-permute-start(f32[112,128]{1,0:T(8,128)S(1)} %get-tuple-element.27), channel_id=1, source_target_pairs={{0,4},{1,5},{2,6},{3,7},{4,0},{5,1},{6,2},{7,3},{8,12},{9,13},{10,... | collective-permute-start | bytes 172040 | tf_op jit(solution)/shard_map/ppermute | solution.py:308
  30.1 4.7 %collective-permute-start.9 = (f32[112,128]{1,0:T(8,128)S(1)}, f32[112,128]{1,0:T(8,128)S(1)}, u32[]{:S(2)}, u32[]{:S(2)}) collective-permute-start(f32[112,128]{1,0:T(8,128)S(1)} %get-tuple-element.27), channel_id=1, source_target_pairs={{0,16},{1,17},{2,26},{3,27},{4,20},{5,21},{6,30},{7,31},{8,24},{9,... | collective-permute-start | bytes 172040 | tf_op jit(solution)/shard_map/ppermute | solution.py:308
  34.8 5.1 %collective-permute-start.14 = (f32[112,128]{1,0:T(8,128)S(1)}, f32[112,128]{1,0:T(8,128)S(1)}, u32[]{:S(2)}, u32[]{:S(2)}) collective-permute-start(f32[112,128]{1,0:T(8,128)S(1)} %pair_sum.1.own.after), channel_id=1, source_target_pairs={{0,3},{1,2},{2,1},{3,0},{4,7},{5,6},{6,5},{7,4},{8,11},{9,10},{10,... | collective-permute-start | bytes 172040 | tf_op jit(solution)/shard_map/ppermute | solution.py:308
  34.9 5.1 %collective-permute-start.13 = (f32[112,128]{1,0:T(8,128)S(1)}, f32[112,128]{1,0:T(8,128)S(1)}, u32[]{:S(2)}, u32[]{:S(2)}) collective-permute-start(f32[112,128]{1,0:T(8,128)S(1)} %pair_sum.1.own.after), channel_id=1, source_target_pairs={{0,2},{1,3},{2,0},{3,1},{4,6},{5,7},{6,4},{7,5},{8,10},{9,11},{10,... | collective-permute-start | bytes 172040 | tf_op jit(solution)/shard_map/ppermute | solution.py:308
  36.9 4.2 %collective-permute-start.12 = (f32[112,128]{1,0:T(8,128)S(1)}, f32[112,128]{1,0:T(8,128)S(1)}, u32[]{:S(2)}, u32[]{:S(2)}) collective-permute-start(f32[112,128]{1,0:T(8,128)S(1)} %pair_sum.1.own.after), channel_id=1, source_target_pairs={{0,1},{1,0},{2,3},{3,2},{4,5},{5,4},{6,7},{7,6},{8,9},{9,8},{10,11... | collective-permute-start | bytes 172040 | tf_op jit(solution)/shard_map/ppermute | solution.py:308
  38.4 4.3 %collective-permute-start.16 = (bf16[2048,128]{1,0:T(8,128)(2,1)S(1)}, bf16[2048,128]{1,0:T(8,128)(2,1)S(1)}, u32[]{:S(2)}, u32[]{:S(2)}) collective-permute-start(bf16[2048,128]{1,0:T(8,128)(2,1)S(1)} %after.2), channel_id=1, source_target_pairs={{0,8},{8,0},{16,24},{24,16},{1,9},{9,1},{17,25},{25,17},{2,10},{10... | collective-permute-start | bytes 1572872 | tf_op jit(solution)/shard_map/ppermute | solution.py:300
  38.6 4.2 %collective-permute-start.18 = (bf16[2048,128]{1,0:T(8,128)(2,1)S(1)}, bf16[2048,128]{1,0:T(8,128)(2,1)S(1)}, u32[]{:S(2)}, u32[]{:S(2)}) collective-permute-start(bf16[2048,128]{1,0:T(8,128)(2,1)S(1)} %after.3), channel_id=1, source_target_pairs={{0,8},{8,0},{16,24},{24,16},{1,9},{9,1},{17,25},{25,17},{2,10},{10... | collective-permute-start | bytes 1572872 | tf_op jit(solution)/shard_map/ppermute | solution.py:300
  41.0 1.7 %copy-start.1 = (s32[8]{0:T(128)S(1)}, s32[8]{0:T(128)}, u32[]{:S(2)}) copy-start(s32[8]{0:T(128)} %active.1) | copy-start | bytes 100
  41.1 1.7 %collective-permute-start.15 = (f32[640,128]{1,0:T(8,128)S(1)}, f32[640,128]{1,0:T(8,128)S(1)}, u32[]{:S(2)}, u32[]{:S(2)}) collective-permute-start(f32[640,128]{1,0:T(8,128)S(1)} %join.1.joined_mine), channel_id=1, source_target_pairs={{0,8},{8,0},{16,24},{24,16},{1,9},{9,1},{17,25},{25,17},{2,10},{10... | collective-permute-start | bytes 983048 | tf_op jit(solution)/shard_map/ppermute | solution.py:300

commit v10 on v9

--- a/solution.py
+++ b/solution.py
@@ -149,17 +149,16 @@
     return both[:count] + (both[count:] + dot(left[0], right[1]))
 
 
-def symmetric(first, mixed, last):
-    return jnp.concatenate(
-        [jnp.concatenate([first, mixed], axis=1), jnp.concatenate([mixed.T, last], axis=1)], axis=0
-    )
+def symmetric(upper, last):
+    half = last.shape[0]
+    return jnp.concatenate([upper, jnp.concatenate([upper[:, half:].T, last], axis=1)], axis=0)
 
 
 def symmetric_product(left, right):
     half = left[0].shape[0] // 2
     upper = product((left[0][:half], left[1][:half]), right)
     last = product((left[0][half:], left[1][half:]), (right[0][:, half:], right[1][:, half:]))
-    return symmetric(upper[:, :half], upper[:, half:], last)
+    return upper, last
 
 
 def finish_kernel(
@@ -234,8 +233,10 @@
         high, low = split(current)
         highs[step], lows[step] = high, low
         square = symmetric_product((high, low), (high, low))
-        cube = symmetric_product((high, low), split(square))
-        current = 2.25 * current - 1.5 * square + 0.25 * cube
+        cube = symmetric_product((high, low), split(symmetric(*square)))
+        middle = cols // 2
+        before = current[:middle], current[middle:, middle:]
+        current = symmetric(*[2.25 * old - 1.5 * two + 0.25 * three for old, two, three in zip(before, square, cube)])
     highs[last], lows[last] = split(current)
     gram[...] = current
 

time: 52.5 us -> 52.4 us (level)
  no operation moved by 1% of the time
where the time goes in v10:
time: 52.4 us; the launch traced here: 52.3 us
  starting transfers between devices  23.1 us (44%)
  waiting for transfers between devices  17.3 us (33%)
  Pallas kernels  10.6 us (20%)
  local copies, waits for them, and re-layouts  1.15 us (2%)
    ppermute x13, starting transfers between devices, move(): return lax.ppermute(value, ('state', 'row'), pairs)  17.8 us
    ppermute x13, waiting for transfers between devices, move(): return lax.ppermute(value, ('state', 'row'), pairs)  15.7 us
    pallas_call x1, Pallas kernels, shards(): call(functools.partial(finish_kernel, float(total_rows)), shape((rows, wi...  9.49 us
    ppermute x6, starting transfers between devices, swap(): lax.ppermute(value, 'state', [(index, index ^ bit) for index in range(4)])  5.28 us
    ppermute x6, waiting for transfers between devices, swap(): lax.ppermute(value, 'state', [(index, index ^ bit) for index in range(4)])  1.63 us
    dynamic_slice x1, local copies, waits for them, and re-layouts, shards(): lax.dynamic_slice_in_dim(vectors, (1 - chip) * half, half, 0)  1.08 us
  transfers between devices with their start and end apart: 19, of which 12 were waited for; matrix products, arithmetic and copies ran while one was open for 2% of the time, Pallas kernels for 2%

profile of v10, /device:TPU:0, one launch (start us, length us, event | category | flops | bytes accessed | tf_op | source)
XLA Modules:
  0.0 52.3 jit_solution(15666496279339159235)
XLA Ops:
  0.0 0.0 copy-start
  0.0 0.5 collective-permute-start
  0.5 1.1 %constant_dynamic-slice_fusion = bf16[2048,128]{1,0:T(8,128)(2,1)S(1)} fusion(bf16[4096,128]{1,0:T(8,128)(2,1)} %own.7, s32[]{:T(128)S(6)} %select_n.9), kind=kLoop, calls=%fused_computation | loop fusion | bytes 1048580 | tf_op jit(solution)/shard_map/dynamic_slice | solution.py:317
  1.5 2.6 %collective-permute-start.1 = (bf16[2048,128]{1,0:T(8,128)(2,1)S(1)}, bf16[2048,128]{1,0:T(8,128)(2,1)S(1)}, u32[]{:S(2)}, u32[]{:S(2)}) collective-permute-start(bf16[2048,128]{1,0:T(8,128)(2,1)S(1)} %constant_dynamic-slice_fusion), channel_id=1, source_target_pairs={{0,16},{8,24},{16,0},{24,8},{1,17},{9,25},{17,1},{25,9},{2,18},{10... | collective-permute-start | bytes 1572872 | tf_op jit(solution)/shard_map/ppermute | solution.py:301
  4.2 0.0 collective-permute-done.mate
  4.2 0.0 copy-done
  4.2 0.6 %chip_gram.1 = (f32[48,128]{1,0:T(8,128)S(1)}, f32[48,128]{1,0:T(8,128)S(1)}, f32[48,128]{1,0:T(8,128)S(1)}, f32[48,128]{1,0:T(8,128)S(1)}) custom-call(bf16[4096,128]{1,0:T(8,128)(2,1)S(1)} %copy-done, bf16[4096,128]{1,0:T(8,128)(2,1)S(1)} %collective-permute-done.mate), custom_call_target="tpu_custom_call" | custom-call | tf_op jit(solution)/shard_map/chip_gram/pallas_call | solution.py:321
  4.7 1.7 %collective-permute-start.2 = (f32[48,128]{1,0:T(8,128)S(1)}, f32[48,128]{1,0:T(8,128)S(1)}, u32[]{:S(2)}, u32[]{:S(2)}) collective-permute-start(f32[48,128]{1,0:T(8,128)S(1)} %get-tuple-element.18), channel_id=1, source_target_pairs={{0,1},{1,0},{2,3},{3,2},{4,5},{5,4},{6,7},{7,6},{8,9},{9,8},{10,11... | collective-permute-start | bytes 73736 | tf_op jit(solution)/shard_map/ppermute | solution.py:309
  6.5 1.6 %collective-permute-start.3 = (f32[48,128]{1,0:T(8,128)S(1)}, f32[48,128]{1,0:T(8,128)S(1)}, u32[]{:S(2)}, u32[]{:S(2)}) collective-permute-start(f32[48,128]{1,0:T(8,128)S(1)} %get-tuple-element.19), channel_id=1, source_target_pairs={{0,2},{1,3},{2,0},{3,1},{4,6},{5,7},{6,4},{7,5},{8,10},{9,11},{10,... | collective-permute-start | bytes 73736 | tf_op jit(solution)/shard_map/ppermute | solution.py:309
  8.1 0.3 collective-permute-start.4
  8.4 0.3 collective-permute-done.2.part1
  8.6 1.8 %collective-permute-done.3.part2 = f32[48,128]{1,0:T(8,128)S(1)} collective-permute-done((f32[48,128]{1,0:T(8,128)S(1)}, f32[48,128]{1,0:T(8,128)S(1)}, u32[]{:S(2)}, u32[]{:S(2)}) %collective-permute-start.3) | collective-permute-done | bytes 24608 | tf_op jit(solution)/shard_map/ppermute | solution.py:309
  10.4 2.3 %collective-permute-done.4.part3 = f32[48,128]{1,0:T(8,128)S(1)} collective-permute-done((f32[48,128]{1,0:T(8,128)S(1)}, f32[48,128]{1,0:T(8,128)S(1)}, u32[]{:S(2)}, u32[]{:S(2)}) %collective-permute-start.4) | collective-permute-done | bytes 24608 | tf_op jit(solution)/shard_map/ppermute | solution.py:309
  12.8 2.7 %collective-permute-start.5 = (f32[48,128]{1,0:T(8,128)S(1)}, f32[48,128]{1,0:T(8,128)S(1)}, u32[]{:S(2)}, u32[]{:S(2)}) collective-permute-start(f32[48,128]{1,0:T(8,128)S(1)} %chip_sum.1.rest_0_), channel_id=1, source_target_pairs={{0,4},{1,5},{2,6},{3,7},{4,0},{5,1},{6,2},{7,3},{8,12},{9,13},{10,... | collective-permute-start | bytes 73736 | tf_op jit(solution)/shard_map/ppermute | solution.py:309
  15.5 1.5 %collective-permute-start.17 = (bf16[2048,128]{1,0:T(8,128)(2,1)S(1)}, bf16[2048,128]{1,0:T(8,128)(2,1)S(1)}, u32[]{:S(2)}, u32[]{:S(2)}) collective-permute-start(bf16[2048,128]{1,0:T(8,128)(2,1)S(1)} %later.1), channel_id=1, source_target_pairs={{0,16},{8,24},{16,0},{24,8},{1,17},{9,25},{17,1},{25,9},{2,18},{10... | collective-permute-start | bytes 1572872 | tf_op jit(solution)/shard_map/ppermute | solution.py:301
  17.0 0.0 collective-permute-done.1.across.across1
  17.0 0.7 %collective-permute-done.5.rest_1_ = f32[48,128]{1,0:T(8,128)S(1)} collective-permute-done((f32[48,128]{1,0:T(8,128)S(1)}, f32[48,128]{1,0:T(8,128)S(1)}, u32[]{:S(2)}, u32[]{:S(2)}) %collective-permute-start.5) | collective-permute-done | bytes 24608 | tf_op jit(solution)/shard_map/ppermute | solution.py:309
  17.7 0.5 pair_gram.1
  18.2 1.3 %collective-permute-start.6 = (f32[112,128]{1,0:T(8,128)S(1)}, f32[112,128]{1,0:T(8,128)S(1)}, u32[]{:S(2)}, u32[]{:S(2)}) collective-permute-start(f32[112,128]{1,0:T(8,128)S(1)} %get-tuple-element.23), channel_id=1, source_target_pairs={{0,1},{1,0},{2,3},{3,2},{4,5},{5,4},{6,7},{7,6},{8,9},{9,8},{10,11... | collective-permute-start | bytes 172040 | tf_op jit(solution)/shard_map/ppermute | solution.py:309
  19.5 1.6 %collective-permute-start.7 = (f32[112,128]{1,0:T(8,128)S(1)}, f32[112,128]{1,0:T(8,128)S(1)}, u32[]{:S(2)}, u32[]{:S(2)}) collective-permute-start(f32[112,128]{1,0:T(8,128)S(1)} %get-tuple-element.24), channel_id=1, source_target_pairs={{0,2},{1,3},{2,0},{3,1},{4,6},{5,7},{6,4},{7,5},{8,10},{9,11},{10,... | collective-permute-start | bytes 172040 | tf_op jit(solution)/shard_map/ppermute | solution.py:309
  21.0 0.7 %collective-permute-start.8 = (f32[112,128]{1,0:T(8,128)S(1)}, f32[112,128]{1,0:T(8,128)S(1)}, u32[]{:S(2)}, u32[]{:S(2)}) collective-permute-start(f32[112,128]{1,0:T(8,128)S(1)} %get-tuple-element.25), channel_id=1, source_target_pairs={{0,3},{1,2},{2,1},{3,0},{4,7},{5,6},{6,5},{7,4},{8,11},{9,10},{10,... | collective-permute-start | bytes 172040 | tf_op jit(solution)/shard_map/ppermute | solution.py:309
  21.7 0.7 %collective-permute-done.6.part1 = f32[112,128]{1,0:T(8,128)S(1)} collective-permute-done((f32[112,128]{1,0:T(8,128)S(1)}, f32[112,128]{1,0:T(8,128)S(1)}, u32[]{:S(2)}, u32[]{:S(2)}) %collective-permute-start.6) | collective-permute-done | bytes 57376 | tf_op jit(solution)/shard_map/ppermute | solution.py:309
  22.4 1.2 %collective-permute-done.7.part2 = f32[112,128]{1,0:T(8,128)S(1)} collective-permute-done((f32[112,128]{1,0:T(8,128)S(1)}, f32[112,128]{1,0:T(8,128)S(1)}, u32[]{:S(2)}, u32[]{:S(2)}) %collective-permute-start.7) | collective-permute-done | bytes 57376 | tf_op jit(solution)/shard_map/ppermute | solution.py:309
  23.6 2.5 %collective-permute-done.8.part3 = f32[112,128]{1,0:T(8,128)S(1)} collective-permute-done((f32[112,128]{1,0:T(8,128)S(1)}, f32[112,128]{1,0:T(8,128)S(1)}, u32[]{:S(2)}, u32[]{:S(2)}) %collective-permute-start.8) | collective-permute-done | bytes 57376 | tf_op jit(solution)/shard_map/ppermute | solution.py:309
  26.1 3.6 %collective-permute-start.11 = (f32[112,128]{1,0:T(8,128)S(1)}, f32[112,128]{1,0:T(8,128)S(1)}, u32[]{:S(2)}, u32[]{:S(2)}) collective-permute-start(f32[112,128]{1,0:T(8,128)S(1)} %get-tuple-element.27), channel_id=1, source_target_pairs={{0,20},{1,21},{2,30},{3,31},{4,16},{5,17},{6,26},{7,27},{8,28},{9,... | collective-permute-start | bytes 172040 | tf_op jit(solution)/shard_map/ppermute | solution.py:309
  29.7 0.3 collective-permute-start.10
  30.1 0.5 %collective-permute-start.9 = (f32[112,128]{1,0:T(8,128)S(1)}, f32[112,128]{1,0:T(8,128)S(1)}, u32[]{:S(2)}, u32[]{:S(2)}) collective-permute-start(f32[112,128]{1,0:T(8,128)S(1)} %get-tuple-element.27), channel_id=1, source_target_pairs={{0,16},{1,17},{2,26},{3,27},{4,20},{5,21},{6,30},{7,31},{8,24},{9,... | collective-permute-start | bytes 172040 | tf_op jit(solution)/shard_map/ppermute | solution.py:309
  30.6 4.1 %collective-permute-done.11.rest_1_ = f32[112,128]{1,0:T(8,128)S(1)} collective-permute-done((f32[112,128]{1,0:T(8,128)S(1)}, f32[112,128]{1,0:T(8,128)S(1)}, u32[]{:S(2)}, u32[]{:S(2)}) %collective-permute-start.11) | collective-permute-done | bytes 57376 | tf_op jit(solution)/shard_map/ppermute | solution.py:309
  34.6 0.2 collective-permute-done.10.rest_0_
  34.8 0.0 collective-permute-done.9.across
  34.8 0.1 collective-permute-start.14
  34.9 2.0 %collective-permute-start.13 = (f32[112,128]{1,0:T(8,128)S(1)}, f32[112,128]{1,0:T(8,128)S(1)}, u32[]{:S(2)}, u32[]{:S(2)}) collective-permute-start(f32[112,128]{1,0:T(8,128)S(1)} %pair_sum.1.own.after), channel_id=1, source_target_pairs={{0,2},{1,3},{2,0},{3,1},{4,6},{5,7},{6,4},{7,5},{8,10},{9,11},{10,... | collective-permute-start | bytes 172040 | tf_op jit(solution)/shard_map/ppermute | solution.py:309
  36.9 1.5 %collective-permute-start.12 = (f32[112,128]{1,0:T(8,128)S(1)}, f32[112,128]{1,0:T(8,128)S(1)}, u32[]{:S(2)}, u32[]{:S(2)}) collective-permute-start(f32[112,128]{1,0:T(8,128)S(1)} %pair_sum.1.own.after), channel_id=1, source_target_pairs={{0,1},{1,0},{2,3},{3,2},{4,5},{5,4},{6,7},{7,6},{8,9},{9,8},{10,11... | collective-permute-start | bytes 172040 | tf_op jit(solution)/shard_map/ppermute | solution.py:309
  38.4 0.1 collective-permute-start.16
  38.5 0.0 collective-permute-done.17.across2
  38.6 0.6 %collective-permute-start.18 = (bf16[2048,128]{1,0:T(8,128)(2,1)S(1)}, bf16[2048,128]{1,0:T(8,128)(2,1)S(1)}, u32[]{:S(2)}, u32[]{:S(2)}) collective-permute-start(bf16[2048,128]{1,0:T(8,128)(2,1)S(1)} %after.3), channel_id=1, source_target_pairs={{0,8},{8,0},{16,24},{24,16},{1,9},{9,1},{17,25},{25,17},{2,10},{10... | collective-permute-start | bytes 1572872 | tf_op jit(solution)/shard_map/ppermute | solution.py:301
  39.1 0.8 %collective-permute-done.14.part3 = f32[112,128]{1,0:T(8,128)S(1)} collective-permute-done((f32[112,128]{1,0:T(8,128)S(1)}, f32[112,128]{1,0:T(8,128)S(1)}, u32[]{:S(2)}, u32[]{:S(2)}) %collective-permute-start.14) | collective-permute-done | bytes 57376 | tf_op jit(solution)/shard_map/ppermute | solution.py:309
  40.0 0.0 collective-permute-done.13.part2
  40.0 1.1 %collective-permute-done.12.part1 = f32[112,128]{1,0:T(8,128)S(1)} collective-permute-done((f32[112,128]{1,0:T(8,128)S(1)}, f32[112,128]{1,0:T(8,128)S(1)}, u32[]{:S(2)}, u32[]{:S(2)}) %collective-permute-start.12) | collective-permute-done | bytes 57376 | tf_op jit(solution)/shard_map/ppermute | solution.py:309
  41.0 0.0 copy-start.1
  41.1 0.1 collective-permute-start.15
  41.1 1.6 %collective-permute-done.15.joined_mate = f32[640,128]{1,0:T(8,128)S(1)} collective-permute-done((f32[640,128]{1,0:T(8,128)S(1)}, f32[640,128]{1,0:T(8,128)S(1)}, u32[]{:S(2)}, u32[]{:S(2)}) %collective-permute-start.15) | collective-permute-done | bytes 327712 | tf_op jit(solution)/shard_map/ppermute | solution.py:301
  42.8 0.0 collective-permute-done.16.mate1
  42.8 0.0 collective-permute-done.18.mate2
  42.8 0.0 copy-done.1
  42.8 9.5 %finish.1 = bf16[4096,128]{1,0:T(8,128)(2,1)} custom-call(s32[8]{0:T(128)S(1)} %copy-done.1, f32[640,128]{1,0:T(8,128)S(1)} %join.1.joined_mine, f32[640,128]{1,0:T(8,128)S(1)} %collective-permute-done.15.joined_mate, bf16[4096,128]{1,0:T(8,128)(2,1)S(1)} %copy-done, bf16[4096,128]{1,0:T(8,128)(2,1)S(1)} %collective-permute-done.mate, ...), custom_call_target="tpu_custom_call" | custom-call | tf_op jit(solution)/shard_map/finish/pallas_call | solution.py:353
  (9 shorter events, 0.2 us)
Async XLA Ops:
  0.0 4.2 %copy-start = (bf16[4096,128]{1,0:T(8,128)(2,1)S(1)}, bf16[4096,128]{1,0:T(8,128)(2,1)}, u32[]{:S(2)}) copy-start(bf16[4096,128]{1,0:T(8,128)(2,1)} %own.7) | copy-start | bytes 3145732
  0.0 4.2 %collective-permute-start = (bf16[4096,128]{1,0:T(8,128)(2,1)}, bf16[4096,128]{1,0:T(8,128)(2,1)S(1)}, u32[]{:S(2)}, u32[]{:S(2)}) collective-permute-start(bf16[4096,128]{1,0:T(8,128)(2,1)} %own.7), channel_id=1, source_target_pairs={{0,8},{8,0},{16,24},{24,16},{1,9},{9,1},{17,25},{25,17},{2,10},{10... | collective-permute-start | bytes 3145736 | tf_op jit(solution)/shard_map/ppermute | solution.py:301
  1.5 15.5 %collective-permute-start.1 = (bf16[2048,128]{1,0:T(8,128)(2,1)S(1)}, bf16[2048,128]{1,0:T(8,128)(2,1)S(1)}, u32[]{:S(2)}, u32[]{:S(2)}) collective-permute-start(bf16[2048,128]{1,0:T(8,128)(2,1)S(1)} %constant_dynamic-slice_fusion), channel_id=1, source_target_pairs={{0,16},{8,24},{16,0},{24,8},{1,17},{9,25},{17,1},{25,9},{2,18},{10... | collective-permute-start | bytes 1572872 | tf_op jit(solution)/shard_map/ppermute | solution.py:301
  4.7 3.9 %collective-permute-start.2 = (f32[48,128]{1,0:T(8,128)S(1)}, f32[48,128]{1,0:T(8,128)S(1)}, u32[]{:S(2)}, u32[]{:S(2)}) collective-permute-start(f32[48,128]{1,0:T(8,128)S(1)} %get-tuple-element.18), channel_id=1, source_target_pairs={{0,1},{1,0},{2,3},{3,2},{4,5},{5,4},{6,7},{7,6},{8,9},{9,8},{10,11... | collective-permute-start | bytes 73736 | tf_op jit(solution)/shard_map/ppermute | solution.py:309
  6.5 4.0 %collective-permute-start.3 = (f32[48,128]{1,0:T(8,128)S(1)}, f32[48,128]{1,0:T(8,128)S(1)}, u32[]{:S(2)}, u32[]{:S(2)}) collective-permute-start(f32[48,128]{1,0:T(8,128)S(1)} %get-tuple-element.19), channel_id=1, source_target_pairs={{0,2},{1,3},{2,0},{3,1},{4,6},{5,7},{6,4},{7,5},{8,10},{9,11},{10,... | collective-permute-start | bytes 73736 | tf_op jit(solution)/shard_map/ppermute | solution.py:309
  8.1 4.7 %collective-permute-start.4 = (f32[48,128]{1,0:T(8,128)S(1)}, f32[48,128]{1,0:T(8,128)S(1)}, u32[]{:S(2)}, u32[]{:S(2)}) collective-permute-start(f32[48,128]{1,0:T(8,128)S(1)} %get-tuple-element.20), channel_id=1, source_target_pairs={{0,3},{1,2},{2,1},{3,0},{4,7},{5,6},{6,5},{7,4},{8,11},{9,10},{10,... | collective-permute-start | bytes 73736 | tf_op jit(solution)/shard_map/ppermute | solution.py:309
  12.8 4.9 %collective-permute-start.5 = (f32[48,128]{1,0:T(8,128)S(1)}, f32[48,128]{1,0:T(8,128)S(1)}, u32[]{:S(2)}, u32[]{:S(2)}) collective-permute-start(f32[48,128]{1,0:T(8,128)S(1)} %chip_sum.1.rest_0_), channel_id=1, source_target_pairs={{0,4},{1,5},{2,6},{3,7},{4,0},{5,1},{6,2},{7,3},{8,12},{9,13},{10,... | collective-permute-start | bytes 73736 | tf_op jit(solution)/shard_map/ppermute | solution.py:309
  15.5 23.0 %collective-permute-start.17 = (bf16[2048,128]{1,0:T(8,128)(2,1)S(1)}, bf16[2048,128]{1,0:T(8,128)(2,1)S(1)}, u32[]{:S(2)}, u32[]{:S(2)}) collective-permute-start(bf16[2048,128]{1,0:T(8,128)(2,1)S(1)} %later.1), channel_id=1, source_target_pairs={{0,16},{8,24},{16,0},{24,8},{1,17},{9,25},{17,1},{25,9},{2,18},{10... | collective-permute-start | bytes 1572872 | tf_op jit(solution)/shard_map/ppermute | solution.py:301
  18.2 4.2 %collective-permute-start.6 = (f32[112,128]{1,0:T(8,128)S(1)}, f32[112,128]{1,0:T(8,128)S(1)}, u32[]{:S(2)}, u32[]{:S(2)}) collective-permute-start(f32[112,128]{1,0:T(8,128)S(1)} %get-tuple-element.23), channel_id=1, source_target_pairs={{0,1},{1,0},{2,3},{3,2},{4,5},{5,4},{6,7},{7,6},{8,9},{9,8},{10,11... | collective-permute-start | bytes 172040 | tf_op jit(solution)/shard_map/ppermute | solution.py:309
  19.5 4.2 %collective-permute-start.7 = (f32[112,128]{1,0:T(8,128)S(1)}, f32[112,128]{1,0:T(8,128)S(1)}, u32[]{:S(2)}, u32[]{:S(2)}) collective-permute-start(f32[112,128]{1,0:T(8,128)S(1)} %get-tuple-element.24), channel_id=1, source_target_pairs={{0,2},{1,3},{2,0},{3,1},{4,6},{5,7},{6,4},{7,5},{8,10},{9,11},{10,... | collective-permute-start | bytes 172040 | tf_op jit(solution)/shard_map/ppermute | solution.py:309
  21.0 5.1 %collective-permute-start.8 = (f32[112,128]{1,0:T(8,128)S(1)}, f32[112,128]{1,0:T(8,128)S(1)}, u32[]{:S(2)}, u32[]{:S(2)}) collective-permute-start(f32[112,128]{1,0:T(8,128)S(1)} %get-tuple-element.25), channel_id=1, source_target_pairs={{0,3},{1,2},{2,1},{3,0},{4,7},{5,6},{6,5},{7,4},{8,11},{9,10},{10,... | collective-permute-start | bytes 172040 | tf_op jit(solution)/shard_map/ppermute | solution.py:309
  26.1 8.5 %collective-permute-start.11 = (f32[112,128]{1,0:T(8,128)S(1)}, f32[112,128]{1,0:T(8,128)S(1)}, u32[]{:S(2)}, u32[]{:S(2)}) collective-permute-start(f32[112,128]{1,0:T(8,128)S(1)} %get-tuple-element.27), channel_id=1, source_target_pairs={{0,20},{1,21},{2,30},{3,31},{4,16},{5,17},{6,26},{7,27},{8,28},{9,... | collective-permute-start | bytes 172040 | tf_op jit(solution)/shard_map/ppermute | solution.py:309
  29.7 5.1 %collective-permute-start.10 = (f32[112,128]{1,0:T(8,128)S(1)}, f32[112,128]{1,0:T(8,128)S(1)}, u32[]{:S(2)}, u32[]{:S(2)}) collective-permute-start(f32[112,128]{1,0:T(8,128)S(1)} %get-tuple-element.27), channel_id=1, source_target_pairs={{0,4},{1,5},{2,6},{3,7},{4,0},{5,1},{6,2},{7,3},{8,12},{9,13},{10,... | collective-permute-start | bytes 172040 | tf_op jit(solution)/shard_map/ppermute | solution.py:309
  30.1 4.7 %collective-permute-start.9 = (f32[112,128]{1,0:T(8,128)S(1)}, f32[112,128]{1,0:T(8,128)S(1)}, u32[]{:S(2)}, u32[]{:S(2)}) collective-permute-start(f32[112,128]{1,0:T(8,128)S(1)} %get-tuple-element.27), channel_id=1, source_target_pairs={{0,16},{1,17},{2,26},{3,27},{4,20},{5,21},{6,30},{7,31},{8,24},{9,... | collective-permute-start | bytes 172040 | tf_op jit(solution)/shard_map/ppermute | solution.py:309
  34.8 5.1 %collective-permute-start.14 = (f32[112,128]{1,0:T(8,128)S(1)}, f32[112,128]{1,0:T(8,128)S(1)}, u32[]{:S(2)}, u32[]{:S(2)}) collective-permute-start(f32[112,128]{1,0:T(8,128)S(1)} %pair_sum.1.own.after), channel_id=1, source_target_pairs={{0,3},{1,2},{2,1},{3,0},{4,7},{5,6},{6,5},{7,4},{8,11},{9,10},{10,... | collective-permute-start | bytes 172040 | tf_op jit(solution)/shard_map/ppermute | solution.py:309
  34.9 5.1 %collective-permute-start.13 = (f32[112,128]{1,0:T(8,128)S(1)}, f32[112,128]{1,0:T(8,128)S(1)}, u32[]{:S(2)}, u32[]{:S(2)}) collective-permute-start(f32[112,128]{1,0:T(8,128)S(1)} %pair_sum.1.own.after), channel_id=1, source_target_pairs={{0,2},{1,3},{2,0},{3,1},{4,6},{5,7},{6,4},{7,5},{8,10},{9,11},{10,... | collective-permute-start | bytes 172040 | tf_op jit(solution)/shard_map/ppermute | solution.py:309
  36.9 4.2 %collective-permute-start.12 = (f32[112,128]{1,0:T(8,128)S(1)}, f32[112,128]{1,0:T(8,128)S(1)}, u32[]{:S(2)}, u32[]{:S(2)}) collective-permute-start(f32[112,128]{1,0:T(8,128)S(1)} %pair_sum.1.own.after), channel_id=1, source_target_pairs={{0,1},{1,0},{2,3},{3,2},{4,5},{5,4},{6,7},{7,6},{8,9},{9,8},{10,11... | collective-permute-start | bytes 172040 | tf_op jit(solution)/shard_map/ppermute | solution.py:309
  38.4 4.3 %collective-permute-start.16 = (bf16[2048,128]{1,0:T(8,128)(2,1)S(1)}, bf16[2048,128]{1,0:T(8,128)(2,1)S(1)}, u32[]{:S(2)}, u32[]{:S(2)}) collective-permute-start(bf16[2048,128]{1,0:T(8,128)(2,1)S(1)} %after.2), channel_id=1, source_target_pairs={{0,8},{8,0},{16,24},{24,16},{1,9},{9,1},{17,25},{25,17},{2,10},{10... | collective-permute-start | bytes 1572872 | tf_op jit(solution)/shard_map/ppermute | solution.py:301
  38.6 4.2 %collective-permute-start.18 = (bf16[2048,128]{1,0:T(8,128)(2,1)S(1)}, bf16[2048,128]{1,0:T(8,128)(2,1)S(1)}, u32[]{:S(2)}, u32[]{:S(2)}) collective-permute-start(bf16[2048,128]{1,0:T(8,128)(2,1)S(1)} %after.3), channel_id=1, source_target_pairs={{0,8},{8,0},{16,24},{24,16},{1,9},{9,1},{17,25},{25,17},{2,10},{10... | collective-permute-start | bytes 1572872 | tf_op jit(solution)/shard_map/ppermute | solution.py:301
  41.0 1.7 %copy-start.1 = (s32[8]{0:T(128)S(1)}, s32[8]{0:T(128)}, u32[]{:S(2)}) copy-start(s32[8]{0:T(128)} %active.1) | copy-start | bytes 100
  41.1 1.7 %collective-permute-start.15 = (f32[640,128]{1,0:T(8,128)S(1)}, f32[640,128]{1,0:T(8,128)S(1)}, u32[]{:S(2)}, u32[]{:S(2)}) collective-permute-start(f32[640,128]{1,0:T(8,128)S(1)} %join.1.joined_mine), channel_id=1, source_target_pairs={{0,8},{8,0},{16,24},{24,16},{1,9},{9,1},{17,25},{25,17},{2,10},{10... | collective-permute-start | bytes 983048 | tf_op jit(solution)/shard_map/ppermute | solution.py:301

commit v11 on v10

--- a/solution.py
+++ b/solution.py
@@ -9,7 +9,7 @@
 
 ITERS = 5
 PAIR_COST = 14 * 10**9
-JOIN_COST = 15 * 10**8
+JOIN_COST = 6 * 10**9
 F32 = jnp.float32
 BF16 = jnp.bfloat16
 VMEM = pl.BlockSpec(memory_space=pltpu.VMEM)

time: 52.4 us -> 52.4 us (level)
  no operation moved by 1% of the time
where the time goes in v11:
time: 52.4 us; the launch traced here: 52.3 us
  starting transfers between devices  23.1 us (44%)
  waiting for transfers between devices  17.3 us (33%)
  Pallas kernels  10.6 us (20%)
  local copies, waits for them, and re-layouts  1.15 us (2%)
    ppermute x13, starting transfers between devices, move(): return lax.ppermute(value, ('state', 'row'), pairs)  17.8 us
    ppermute x13, waiting for transfers between devices, move(): return lax.ppermute(value, ('state', 'row'), pairs)  15.7 us
    pallas_call x1, Pallas kernels, shards(): call(functools.partial(finish_kernel, float(total_rows)), shape((rows, wi...  9.49 us
    ppermute x6, starting transfers between devices, swap(): lax.ppermute(value, 'state', [(index, index ^ bit) for index in range(4)])  5.28 us
    ppermute x6, waiting for transfers between devices, swap(): lax.ppermute(value, 'state', [(index, index ^ bit) for index in range(4)])  1.63 us
    dynamic_slice x1, local copies, waits for them, and re-layouts, shards(): lax.dynamic_slice_in_dim(vectors, (1 - chip) * half, half, 0)  1.08 us
  transfers between devices with their start and end apart: 19, of which 12 were waited for; matrix products, arithmetic and copies ran while one was open for 2% of the time, Pallas kernels for 2%

profile of v11, /device:TPU:0, one launch (start us, length us, event | category | flops | bytes accessed | tf_op | source)
XLA Modules:
  0.0 52.3 jit_solution(15666496279339159235)
XLA Ops:
  0.0 0.0 copy-start
  0.0 0.5 collective-permute-start
  0.5 1.1 %constant_dynamic-slice_fusion = bf16[2048,128]{1,0:T(8,128)(2,1)S(1)} fusion(bf16[4096,128]{1,0:T(8,128)(2,1)} %own.7, s32[]{:T(128)S(6)} %select_n.9), kind=kLoop, calls=%fused_computation | loop fusion | bytes 1048580 | tf_op jit(solution)/shard_map/dynamic_slice | solution.py:317
  1.5 2.6 %collective-permute-start.1 = (bf16[2048,128]{1,0:T(8,128)(2,1)S(1)}, bf16[2048,128]{1,0:T(8,128)(2,1)S(1)}, u32[]{:S(2)}, u32[]{:S(2)}) collective-permute-start(bf16[2048,128]{1,0:T(8,128)(2,1)S(1)} %constant_dynamic-slice_fusion), channel_id=1, source_target_pairs={{0,16},{8,24},{16,0},{24,8},{1,17},{9,25},{17,1},{25,9},{2,18},{10... | collective-permute-start | bytes 1572872 | tf_op jit(solution)/shard_map/ppermute | solution.py:301
  4.2 0.0 collective-permute-done.mate
  4.2 0.0 copy-done
  4.2 0.6 %chip_gram.1 = (f32[48,128]{1,0:T(8,128)S(1)}, f32[48,128]{1,0:T(8,128)S(1)}, f32[48,128]{1,0:T(8,128)S(1)}, f32[48,128]{1,0:T(8,128)S(1)}) custom-call(bf16[4096,128]{1,0:T(8,128)(2,1)S(1)} %copy-done, bf16[4096,128]{1,0:T(8,128)(2,1)S(1)} %collective-permute-done.mate), custom_call_target="tpu_custom_call" | custom-call | tf_op jit(solution)/shard_map/chip_gram/pallas_call | solution.py:321
  4.7 1.7 %collective-permute-start.2 = (f32[48,128]{1,0:T(8,128)S(1)}, f32[48,128]{1,0:T(8,128)S(1)}, u32[]{:S(2)}, u32[]{:S(2)}) collective-permute-start(f32[48,128]{1,0:T(8,128)S(1)} %get-tuple-element.18), channel_id=1, source_target_pairs={{0,1},{1,0},{2,3},{3,2},{4,5},{5,4},{6,7},{7,6},{8,9},{9,8},{10,11... | collective-permute-start | bytes 73736 | tf_op jit(solution)/shard_map/ppermute | solution.py:309
  6.5 1.6 %collective-permute-start.3 = (f32[48,128]{1,0:T(8,128)S(1)}, f32[48,128]{1,0:T(8,128)S(1)}, u32[]{:S(2)}, u32[]{:S(2)}) collective-permute-start(f32[48,128]{1,0:T(8,128)S(1)} %get-tuple-element.19), channel_id=1, source_target_pairs={{0,2},{1,3},{2,0},{3,1},{4,6},{5,7},{6,4},{7,5},{8,10},{9,11},{10,... | collective-permute-start | bytes 73736 | tf_op jit(solution)/shard_map/ppermute | solution.py:309
  8.1 0.3 collective-permute-start.4
  8.4 0.3 collective-permute-done.2.part1
  8.6 1.8 %collective-permute-done.3.part2 = f32[48,128]{1,0:T(8,128)S(1)} collective-permute-done((f32[48,128]{1,0:T(8,128)S(1)}, f32[48,128]{1,0:T(8,128)S(1)}, u32[]{:S(2)}, u32[]{:S(2)}) %collective-permute-start.3) | collective-permute-done | bytes 24608 | tf_op jit(solution)/shard_map/ppermute | solution.py:309
  10.4 2.3 %collective-permute-done.4.part3 = f32[48,128]{1,0:T(8,128)S(1)} collective-permute-done((f32[48,128]{1,0:T(8,128)S(1)}, f32[48,128]{1,0:T(8,128)S(1)}, u32[]{:S(2)}, u32[]{:S(2)}) %collective-permute-start.4) | collective-permute-done | bytes 24608 | tf_op jit(solution)/shard_map/ppermute | solution.py:309
  12.8 2.7 %collective-permute-start.5 = (f32[48,128]{1,0:T(8,128)S(1)}, f32[48,128]{1,0:T(8,128)S(1)}, u32[]{:S(2)}, u32[]{:S(2)}) collective-permute-start(f32[48,128]{1,0:T(8,128)S(1)} %chip_sum.1.rest_0_), channel_id=1, source_target_pairs={{0,4},{1,5},{2,6},{3,7},{4,0},{5,1},{6,2},{7,3},{8,12},{9,13},{10,... | collective-permute-start | bytes 73736 | tf_op jit(solution)/shard_map/ppermute | solution.py:309
  15.5 1.5 %collective-permute-start.17 = (bf16[2048,128]{1,0:T(8,128)(2,1)S(1)}, bf16[2048,128]{1,0:T(8,128)(2,1)S(1)}, u32[]{:S(2)}, u32[]{:S(2)}) collective-permute-start(bf16[2048,128]{1,0:T(8,128)(2,1)S(1)} %later.1), channel_id=1, source_target_pairs={{0,16},{8,24},{16,0},{24,8},{1,17},{9,25},{17,1},{25,9},{2,18},{10... | collective-permute-start | bytes 1572872 | tf_op jit(solution)/shard_map/ppermute | solution.py:301
  17.0 0.0 collective-permute-done.1.across.across1
  17.0 0.7 %collective-permute-done.5.rest_1_ = f32[48,128]{1,0:T(8,128)S(1)} collective-permute-done((f32[48,128]{1,0:T(8,128)S(1)}, f32[48,128]{1,0:T(8,128)S(1)}, u32[]{:S(2)}, u32[]{:S(2)}) %collective-permute-start.5) | collective-permute-done | bytes 24608 | tf_op jit(solution)/shard_map/ppermute | solution.py:309
  17.7 0.5 pair_gram.1
  18.2 1.3 %collective-permute-start.6 = (f32[112,128]{1,0:T(8,128)S(1)}, f32[112,128]{1,0:T(8,128)S(1)}, u32[]{:S(2)}, u32[]{:S(2)}) collective-permute-start(f32[112,128]{1,0:T(8,128)S(1)} %get-tuple-element.23), channel_id=1, source_target_pairs={{0,1},{1,0},{2,3},{3,2},{4,5},{5,4},{6,7},{7,6},{8,9},{9,8},{10,11... | collective-permute-start | bytes 172040 | tf_op jit(solution)/shard_map/ppermute | solution.py:309
  19.5 1.6 %collective-permute-start.7 = (f32[112,128]{1,0:T(8,128)S(1)}, f32[112,128]{1,0:T(8,128)S(1)}, u32[]{:S(2)}, u32[]{:S(2)}) collective-permute-start(f32[112,128]{1,0:T(8,128)S(1)} %get-tuple-element.24), channel_id=1, source_target_pairs={{0,2},{1,3},{2,0},{3,1},{4,6},{5,7},{6,4},{7,5},{8,10},{9,11},{10,... | collective-permute-start | bytes 172040 | tf_op jit(solution)/shard_map/ppermute | solution.py:309
  21.0 0.7 %collective-permute-start.8 = (f32[112,128]{1,0:T(8,128)S(1)}, f32[112,128]{1,0:T(8,128)S(1)}, u32[]{:S(2)}, u32[]{:S(2)}) collective-permute-start(f32[112,128]{1,0:T(8,128)S(1)} %get-tuple-element.25), channel_id=1, source_target_pairs={{0,3},{1,2},{2,1},{3,0},{4,7},{5,6},{6,5},{7,4},{8,11},{9,10},{10,... | collective-permute-start | bytes 172040 | tf_op jit(solution)/shard_map/ppermute | solution.py:309
  21.7 0.7 %collective-permute-done.6.part1 = f32[112,128]{1,0:T(8,128)S(1)} collective-permute-done((f32[112,128]{1,0:T(8,128)S(1)}, f32[112,128]{1,0:T(8,128)S(1)}, u32[]{:S(2)}, u32[]{:S(2)}) %collective-permute-start.6) | collective-permute-done | bytes 57376 | tf_op jit(solution)/shard_map/ppermute | solution.py:309
  22.4 1.2 %collective-permute-done.7.part2 = f32[112,128]{1,0:T(8,128)S(1)} collective-permute-done((f32[112,128]{1,0:T(8,128)S(1)}, f32[112,128]{1,0:T(8,128)S(1)}, u32[]{:S(2)}, u32[]{:S(2)}) %collective-permute-start.7) | collective-permute-done | bytes 57376 | tf_op jit(solution)/shard_map/ppermute | solution.py:309
  23.6 2.5 %collective-permute-done.8.part3 = f32[112,128]{1,0:T(8,128)S(1)} collective-permute-done((f32[112,128]{1,0:T(8,128)S(1)}, f32[112,128]{1,0:T(8,128)S(1)}, u32[]{:S(2)}, u32[]{:S(2)}) %collective-permute-start.8) | collective-permute-done | bytes 57376 | tf_op jit(solution)/shard_map/ppermute | solution.py:309
  26.1 3.6 %collective-permute-start.11 = (f32[112,128]{1,0:T(8,128)S(1)}, f32[112,128]{1,0:T(8,128)S(1)}, u32[]{:S(2)}, u32[]{:S(2)}) collective-permute-start(f32[112,128]{1,0:T(8,128)S(1)} %get-tuple-element.27), channel_id=1, source_target_pairs={{0,20},{1,21},{2,30},{3,31},{4,16},{5,17},{6,26},{7,27},{8,28},{9,... | collective-permute-start | bytes 172040 | tf_op jit(solution)/shard_map/ppermute | solution.py:309
  29.7 0.3 collective-permute-start.10
  30.1 0.5 %collective-permute-start.9 = (f32[112,128]{1,0:T(8,128)S(1)}, f32[112,128]{1,0:T(8,128)S(1)}, u32[]{:S(2)}, u32[]{:S(2)}) collective-permute-start(f32[112,128]{1,0:T(8,128)S(1)} %get-tuple-element.27), channel_id=1, source_target_pairs={{0,16},{1,17},{2,26},{3,27},{4,20},{5,21},{6,30},{7,31},{8,24},{9,... | collective-permute-start | bytes 172040 | tf_op jit(solution)/shard_map/ppermute | solution.py:309
  30.6 4.1 %collective-permute-done.11.rest_1_ = f32[112,128]{1,0:T(8,128)S(1)} collective-permute-done((f32[112,128]{1,0:T(8,128)S(1)}, f32[112,128]{1,0:T(8,128)S(1)}, u32[]{:S(2)}, u32[]{:S(2)}) %collective-permute-start.11) | collective-permute-done | bytes 57376 | tf_op jit(solution)/shard_map/ppermute | solution.py:309
  34.6 0.2 collective-permute-done.10.rest_0_
  34.8 0.0 collective-permute-done.9.across
  34.8 0.1 collective-permute-start.14
  34.9 2.0 %collective-permute-start.13 = (f32[112,128]{1,0:T(8,128)S(1)}, f32[112,128]{1,0:T(8,128)S(1)}, u32[]{:S(2)}, u32[]{:S(2)}) collective-permute-start(f32[112,128]{1,0:T(8,128)S(1)} %pair_sum.1.own.after), channel_id=1, source_target_pairs={{0,2},{1,3},{2,0},{3,1},{4,6},{5,7},{6,4},{7,5},{8,10},{9,11},{10,... | collective-permute-start | bytes 172040 | tf_op jit(solution)/shard_map/ppermute | solution.py:309
  36.9 1.5 %collective-permute-start.12 = (f32[112,128]{1,0:T(8,128)S(1)}, f32[112,128]{1,0:T(8,128)S(1)}, u32[]{:S(2)}, u32[]{:S(2)}) collective-permute-start(f32[112,128]{1,0:T(8,128)S(1)} %pair_sum.1.own.after), channel_id=1, source_target_pairs={{0,1},{1,0},{2,3},{3,2},{4,5},{5,4},{6,7},{7,6},{8,9},{9,8},{10,11... | collective-permute-start | bytes 172040 | tf_op jit(solution)/shard_map/ppermute | solution.py:309
  38.4 0.1 collective-permute-start.16
  38.5 0.0 collective-permute-done.17.across2
  38.6 0.6 %collective-permute-start.18 = (bf16[2048,128]{1,0:T(8,128)(2,1)S(1)}, bf16[2048,128]{1,0:T(8,128)(2,1)S(1)}, u32[]{:S(2)}, u32[]{:S(2)}) collective-permute-start(bf16[2048,128]{1,0:T(8,128)(2,1)S(1)} %after.3), channel_id=1, source_target_pairs={{0,8},{8,0},{16,24},{24,16},{1,9},{9,1},{17,25},{25,17},{2,10},{10... | collective-permute-start | bytes 1572872 | tf_op jit(solution)/shard_map/ppermute | solution.py:301
  39.1 0.8 %collective-permute-done.14.part3 = f32[112,128]{1,0:T(8,128)S(1)} collective-permute-done((f32[112,128]{1,0:T(8,128)S(1)}, f32[112,128]{1,0:T(8,128)S(1)}, u32[]{:S(2)}, u32[]{:S(2)}) %collective-permute-start.14) | collective-permute-done | bytes 57376 | tf_op jit(solution)/shard_map/ppermute | solution.py:309
  40.0 0.0 collective-permute-done.13.part2
  40.0 1.1 %collective-permute-done.12.part1 = f32[112,128]{1,0:T(8,128)S(1)} collective-permute-done((f32[112,128]{1,0:T(8,128)S(1)}, f32[112,128]{1,0:T(8,128)S(1)}, u32[]{:S(2)}, u32[]{:S(2)}) %collective-permute-start.12) | collective-permute-done | bytes 57376 | tf_op jit(solution)/shard_map/ppermute | solution.py:309
  41.0 0.0 copy-start.1
  41.1 0.1 collective-permute-start.15
  41.1 1.6 %collective-permute-done.15.joined_mate = f32[640,128]{1,0:T(8,128)S(1)} collective-permute-done((f32[640,128]{1,0:T(8,128)S(1)}, f32[640,128]{1,0:T(8,128)S(1)}, u32[]{:S(2)}, u32[]{:S(2)}) %collective-permute-start.15) | collective-permute-done | bytes 327712 | tf_op jit(solution)/shard_map/ppermute | solution.py:301
  42.8 0.0 collective-permute-done.16.mate1
  42.8 0.0 collective-permute-done.18.mate2
  42.8 0.0 copy-done.1
  42.8 9.5 %finish.1 = bf16[4096,128]{1,0:T(8,128)(2,1)} custom-call(s32[8]{0:T(128)S(1)} %copy-done.1, f32[640,128]{1,0:T(8,128)S(1)} %join.1.joined_mine, f32[640,128]{1,0:T(8,128)S(1)} %collective-permute-done.15.joined_mate, bf16[4096,128]{1,0:T(8,128)(2,1)S(1)} %copy-done, bf16[4096,128]{1,0:T(8,128)(2,1)S(1)} %collective-permute-done.mate, ...), custom_call_target="tpu_custom_call" | custom-call | tf_op jit(solution)/shard_map/finish/pallas_call | solution.py:353
  (9 shorter events, 0.2 us)
Async XLA Ops:
  0.0 4.2 %copy-start = (bf16[4096,128]{1,0:T(8,128)(2,1)S(1)}, bf16[4096,128]{1,0:T(8,128)(2,1)}, u32[]{:S(2)}) copy-start(bf16[4096,128]{1,0:T(8,128)(2,1)} %own.7) | copy-start | bytes 3145732
  0.0 4.2 %collective-permute-start = (bf16[4096,128]{1,0:T(8,128)(2,1)}, bf16[4096,128]{1,0:T(8,128)(2,1)S(1)}, u32[]{:S(2)}, u32[]{:S(2)}) collective-permute-start(bf16[4096,128]{1,0:T(8,128)(2,1)} %own.7), channel_id=1, source_target_pairs={{0,8},{8,0},{16,24},{24,16},{1,9},{9,1},{17,25},{25,17},{2,10},{10... | collective-permute-start | bytes 3145736 | tf_op jit(solution)/shard_map/ppermute | solution.py:301
  1.5 15.5 %collective-permute-start.1 = (bf16[2048,128]{1,0:T(8,128)(2,1)S(1)}, bf16[2048,128]{1,0:T(8,128)(2,1)S(1)}, u32[]{:S(2)}, u32[]{:S(2)}) collective-permute-start(bf16[2048,128]{1,0:T(8,128)(2,1)S(1)} %constant_dynamic-slice_fusion), channel_id=1, source_target_pairs={{0,16},{8,24},{16,0},{24,8},{1,17},{9,25},{17,1},{25,9},{2,18},{10... | collective-permute-start | bytes 1572872 | tf_op jit(solution)/shard_map/ppermute | solution.py:301
  4.7 3.9 %collective-permute-start.2 = (f32[48,128]{1,0:T(8,128)S(1)}, f32[48,128]{1,0:T(8,128)S(1)}, u32[]{:S(2)}, u32[]{:S(2)}) collective-permute-start(f32[48,128]{1,0:T(8,128)S(1)} %get-tuple-element.18), channel_id=1, source_target_pairs={{0,1},{1,0},{2,3},{3,2},{4,5},{5,4},{6,7},{7,6},{8,9},{9,8},{10,11... | collective-permute-start | bytes 73736 | tf_op jit(solution)/shard_map/ppermute | solution.py:309
  6.5 4.0 %collective-permute-start.3 = (f32[48,128]{1,0:T(8,128)S(1)}, f32[48,128]{1,0:T(8,128)S(1)}, u32[]{:S(2)}, u32[]{:S(2)}) collective-permute-start(f32[48,128]{1,0:T(8,128)S(1)} %get-tuple-element.19), channel_id=1, source_target_pairs={{0,2},{1,3},{2,0},{3,1},{4,6},{5,7},{6,4},{7,5},{8,10},{9,11},{10,... | collective-permute-start | bytes 73736 | tf_op jit(solution)/shard_map/ppermute | solution.py:309
  8.1 4.7 %collective-permute-start.4 = (f32[48,128]{1,0:T(8,128)S(1)}, f32[48,128]{1,0:T(8,128)S(1)}, u32[]{:S(2)}, u32[]{:S(2)}) collective-permute-start(f32[48,128]{1,0:T(8,128)S(1)} %get-tuple-element.20), channel_id=1, source_target_pairs={{0,3},{1,2},{2,1},{3,0},{4,7},{5,6},{6,5},{7,4},{8,11},{9,10},{10,... | collective-permute-start | bytes 73736 | tf_op jit(solution)/shard_map/ppermute | solution.py:309
  12.8 4.9 %collective-permute-start.5 = (f32[48,128]{1,0:T(8,128)S(1)}, f32[48,128]{1,0:T(8,128)S(1)}, u32[]{:S(2)}, u32[]{:S(2)}) collective-permute-start(f32[48,128]{1,0:T(8,128)S(1)} %chip_sum.1.rest_0_), channel_id=1, source_target_pairs={{0,4},{1,5},{2,6},{3,7},{4,0},{5,1},{6,2},{7,3},{8,12},{9,13},{10,... | collective-permute-start | bytes 73736 | tf_op jit(solution)/shard_map/ppermute | solution.py:309
  15.5 23.0 %collective-permute-start.17 = (bf16[2048,128]{1,0:T(8,128)(2,1)S(1)}, bf16[2048,128]{1,0:T(8,128)(2,1)S(1)}, u32[]{:S(2)}, u32[]{:S(2)}) collective-permute-start(bf16[2048,128]{1,0:T(8,128)(2,1)S(1)} %later.1), channel_id=1, source_target_pairs={{0,16},{8,24},{16,0},{24,8},{1,17},{9,25},{17,1},{25,9},{2,18},{10... | collective-permute-start | bytes 1572872 | tf_op jit(solution)/shard_map/ppermute | solution.py:301
  18.2 4.2 %collective-permute-start.6 = (f32[112,128]{1,0:T(8,128)S(1)}, f32[112,128]{1,0:T(8,128)S(1)}, u32[]{:S(2)}, u32[]{:S(2)}) collective-permute-start(f32[112,128]{1,0:T(8,128)S(1)} %get-tuple-element.23), channel_id=1, source_target_pairs={{0,1},{1,0},{2,3},{3,2},{4,5},{5,4},{6,7},{7,6},{8,9},{9,8},{10,11... | collective-permute-start | bytes 172040 | tf_op jit(solution)/shard_map/ppermute | solution.py:309
  19.5 4.2 %collective-permute-start.7 = (f32[112,128]{1,0:T(8,128)S(1)}, f32[112,128]{1,0:T(8,128)S(1)}, u32[]{:S(2)}, u32[]{:S(2)}) collective-permute-start(f32[112,128]{1,0:T(8,128)S(1)} %get-tuple-element.24), channel_id=1, source_target_pairs={{0,2},{1,3},{2,0},{3,1},{4,6},{5,7},{6,4},{7,5},{8,10},{9,11},{10,... | collective-permute-start | bytes 172040 | tf_op jit(solution)/shard_map/ppermute | solution.py:309
  21.0 5.1 %collective-permute-start.8 = (f32[112,128]{1,0:T(8,128)S(1)}, f32[112,128]{1,0:T(8,128)S(1)}, u32[]{:S(2)}, u32[]{:S(2)}) collective-permute-start(f32[112,128]{1,0:T(8,128)S(1)} %get-tuple-element.25), channel_id=1, source_target_pairs={{0,3},{1,2},{2,1},{3,0},{4,7},{5,6},{6,5},{7,4},{8,11},{9,10},{10,... | collective-permute-start | bytes 172040 | tf_op jit(solution)/shard_map/ppermute | solution.py:309
  26.1 8.5 %collective-permute-start.11 = (f32[112,128]{1,0:T(8,128)S(1)}, f32[112,128]{1,0:T(8,128)S(1)}, u32[]{:S(2)}, u32[]{:S(2)}) collective-permute-start(f32[112,128]{1,0:T(8,128)S(1)} %get-tuple-element.27), channel_id=1, source_target_pairs={{0,20},{1,21},{2,30},{3,31},{4,16},{5,17},{6,26},{7,27},{8,28},{9,... | collective-permute-start | bytes 172040 | tf_op jit(solution)/shard_map/ppermute | solution.py:309
  29.7 5.1 %collective-permute-start.10 = (f32[112,128]{1,0:T(8,128)S(1)}, f32[112,128]{1,0:T(8,128)S(1)}, u32[]{:S(2)}, u32[]{:S(2)}) collective-permute-start(f32[112,128]{1,0:T(8,128)S(1)} %get-tuple-element.27), channel_id=1, source_target_pairs={{0,4},{1,5},{2,6},{3,7},{4,0},{5,1},{6,2},{7,3},{8,12},{9,13},{10,... | collective-permute-start | bytes 172040 | tf_op jit(solution)/shard_map/ppermute | solution.py:309
  30.1 4.7 %collective-permute-start.9 = (f32[112,128]{1,0:T(8,128)S(1)}, f32[112,128]{1,0:T(8,128)S(1)}, u32[]{:S(2)}, u32[]{:S(2)}) collective-permute-start(f32[112,128]{1,0:T(8,128)S(1)} %get-tuple-element.27), channel_id=1, source_target_pairs={{0,16},{1,17},{2,26},{3,27},{4,20},{5,21},{6,30},{7,31},{8,24},{9,... | collective-permute-start | bytes 172040 | tf_op jit(solution)/shard_map/ppermute | solution.py:309
  34.8 5.1 %collective-permute-start.14 = (f32[112,128]{1,0:T(8,128)S(1)}, f32[112,128]{1,0:T(8,128)S(1)}, u32[]{:S(2)}, u32[]{:S(2)}) collective-permute-start(f32[112,128]{1,0:T(8,128)S(1)} %pair_sum.1.own.after), channel_id=1, source_target_pairs={{0,3},{1,2},{2,1},{3,0},{4,7},{5,6},{6,5},{7,4},{8,11},{9,10},{10,... | collective-permute-start | bytes 172040 | tf_op jit(solution)/shard_map/ppermute | solution.py:309
  34.9 5.1 %collective-permute-start.13 = (f32[112,128]{1,0:T(8,128)S(1)}, f32[112,128]{1,0:T(8,128)S(1)}, u32[]{:S(2)}, u32[]{:S(2)}) collective-permute-start(f32[112,128]{1,0:T(8,128)S(1)} %pair_sum.1.own.after), channel_id=1, source_target_pairs={{0,2},{1,3},{2,0},{3,1},{4,6},{5,7},{6,4},{7,5},{8,10},{9,11},{10,... | collective-permute-start | bytes 172040 | tf_op jit(solution)/shard_map/ppermute | solution.py:309
  36.9 4.2 %collective-permute-start.12 = (f32[112,128]{1,0:T(8,128)S(1)}, f32[112,128]{1,0:T(8,128)S(1)}, u32[]{:S(2)}, u32[]{:S(2)}) collective-permute-start(f32[112,128]{1,0:T(8,128)S(1)} %pair_sum.1.own.after), channel_id=1, source_target_pairs={{0,1},{1,0},{2,3},{3,2},{4,5},{5,4},{6,7},{7,6},{8,9},{9,8},{10,11... | collective-permute-start | bytes 172040 | tf_op jit(solution)/shard_map/ppermute | solution.py:309
  38.4 4.3 %collective-permute-start.16 = (bf16[2048,128]{1,0:T(8,128)(2,1)S(1)}, bf16[2048,128]{1,0:T(8,128)(2,1)S(1)}, u32[]{:S(2)}, u32[]{:S(2)}) collective-permute-start(bf16[2048,128]{1,0:T(8,128)(2,1)S(1)} %after.2), channel_id=1, source_target_pairs={{0,8},{8,0},{16,24},{24,16},{1,9},{9,1},{17,25},{25,17},{2,10},{10... | collective-permute-start | bytes 1572872 | tf_op jit(solution)/shard_map/ppermute | solution.py:301
  38.6 4.2 %collective-permute-start.18 = (bf16[2048,128]{1,0:T(8,128)(2,1)S(1)}, bf16[2048,128]{1,0:T(8,128)(2,1)S(1)}, u32[]{:S(2)}, u32[]{:S(2)}) collective-permute-start(bf16[2048,128]{1,0:T(8,128)(2,1)S(1)} %after.3), channel_id=1, source_target_pairs={{0,8},{8,0},{16,24},{24,16},{1,9},{9,1},{17,25},{25,17},{2,10},{10... | collective-permute-start | bytes 1572872 | tf_op jit(solution)/shard_map/ppermute | solution.py:301
  41.0 1.7 %copy-start.1 = (s32[8]{0:T(128)S(1)}, s32[8]{0:T(128)}, u32[]{:S(2)}) copy-start(s32[8]{0:T(128)} %active.1) | copy-start | bytes 100
  41.1 1.7 %collective-permute-start.15 = (f32[640,128]{1,0:T(8,128)S(1)}, f32[640,128]{1,0:T(8,128)S(1)}, u32[]{:S(2)}, u32[]{:S(2)}) collective-permute-start(f32[640,128]{1,0:T(8,128)S(1)} %join.1.joined_mine), channel_id=1, source_target_pairs={{0,8},{8,0},{16,24},{24,16},{1,9},{9,1},{17,25},{25,17},{2,10},{10... | collective-permute-start | bytes 983048 | tf_op jit(solution)/shard_map/ppermute | solution.py:301
